TPU v7x, 32 devices: a whole 2x2x4 slice. The times are simulated.
32 devices in a mesh: dp: 8 (over y, x, core), ctx: 4 (over z).
Axes of the slice: x: 2, y: 2, z: 4, core: 2. Of those that a mesh axis runs over, the one named last changes fastest.
Arguments:
- query_frames: bfloat16 [8192, 2560], P(('dp', 'ctx')), parts along dimension 0, may hold values from -8 to 8
- key_frames: bfloat16 [8192, 2560], P(('dp', 'ctx')), parts along dimension 0, may hold values from -8 to 8
- value_frames: bfloat16 [8192, 2560], P(('dp', 'ctx')), parts along dimension 0, may hold values from -6 to 6
- stream: bfloat16 [8192, 5120], P(('dp', 'ctx')), parts along dimension 0, may hold values from -1.25 to 1.25
- out_weight: bfloat16 [2560, 5120], P('ctx'), may hold values from -0.125 to 0.125
Outputs:
- layer_out: bfloat16 [8192, 5120], P(('dp', 'ctx')), parts along dimension 0
There are 8 independent parts, one for each index of `dp`. A program takes and returns all parts, laid end to end along the dimension named above; an argument that names none is the same for every part. Nothing has to cross between parts.
All inputs are finite; a program needn't handle non-finite values.
Results may differ from a plain program's by a relative error of at most 0.01.
Values may be sent and summed in bfloat16 or wider, within the bound.
No kernel may reach another device: no remote copies, remote signals or barrier semaphores. Data moves between devices by JAX's collectives and lax.ppermute only.
A program may use at most 128 MiB of HBM per device.

v0:
```python
import jax
import jax.numpy as jnp
from jax import lax
from jax.sharding import PartitionSpec as P

HEADS = 20
HEAD_SIZE = 128


def passed_along(value, axis, steps):
    count = lax.axis_size(axis)
    leading, last = (max(0, -steps), min(count, count - steps))
    return lax.ppermute(value, axis, [(source, source + steps) for source in range(leading, last)])


def attend_window(query_block, key_window, value_window, valid):
    block_rows = query_block.shape[0]
    window_rows = key_window.shape[0]
    query_heads = query_block.reshape(block_rows, HEADS, HEAD_SIZE)
    key_heads = key_window.reshape(window_rows, HEADS, HEAD_SIZE)
    value_heads = value_window.reshape(window_rows, HEADS, HEAD_SIZE)
    scores = jnp.einsum(
        "qhd,khd->hqk", query_heads, key_heads, preferred_element_type=jnp.float32
    ) * HEAD_SIZE ** (-0.5)
    scores = jnp.where(valid[None, None, :], scores, -1e30)
    largest = jnp.max(scores, axis=2, keepdims=True)
    expon = jnp.exp(scores - largest)
    probs = (expon / jnp.sum(expon, axis=2, keepdims=True)).astype(jnp.bfloat16)
    context = jnp.einsum("hqk,khd->qhd", probs, value_heads, preferred_element_type=jnp.float32)
    return context.astype(jnp.bfloat16).reshape(block_rows, HEADS * HEAD_SIZE)


def local(query_frames, key_frames, value_frames, stream, out_weight):
    block_rows = query_frames.shape[0]
    position = lax.axis_index("ctx")
    members = lax.axis_size("ctx")
    key_value = jnp.stack([key_frames, value_frames], 0)
    earlier = passed_along(key_value, "ctx", 1)
    later = passed_along(key_value, "ctx", -1)
    window = jnp.concatenate([earlier, key_value, later], 1)
    earlier_ok = jnp.broadcast_to(position > 0, (block_rows,))
    middle_ok = jnp.ones((block_rows,), dtype=bool)
    later_ok = jnp.broadcast_to(position < members - 1, (block_rows,))
    valid = jnp.concatenate([earlier_ok, middle_ok, later_ok])
    context = attend_window(query_frames, window[0], window[1], valid)
    product = jnp.dot(
        context,
        lax.all_gather(out_weight, "ctx", axis=0, tiled=True),
        preferred_element_type=jnp.float32,
    )
    return (stream.astype(jnp.float32) + product).astype(jnp.bfloat16)


def solution(mesh):
    in_specs = (
        P(("dp", "ctx"), None),
        P(("dp", "ctx"), None),
        P(("dp", "ctx"), None),
        P(("dp", "ctx"), None),
        P("ctx", None),
    )
    out_specs = P(("dp", "ctx"), None)
    return jax.shard_map(local, mesh=mesh, in_specs=in_specs, out_specs=out_specs, check_vma=False)
```

profile of v0, /device:TPU:0, one launch (start us, length us, event | category | flops | bytes accessed | tf_op | source)
XLA Modules:
  0.0 520.7 jit_solution(15168149777031708235)
XLA Ops:
  6.5 0.0 copy-start.1
  6.5 0.0 all-gather.2.cloned.1.call-start
  6.5 0.7 all-gather.2.cloned.1.call-update
  7.3 0.6 copy-done.1
  7.9 0.6 copy.9
  8.5 1.6 copy.10
  10.1 1.7 pad_maximum_fusion.1
  11.8 6.5 %collective-permute-start = (bf16[2,256,2560]{1,2,0:T(8,128)(2,1)}, bf16[2,256,2560]{1,2,0:T(8,128)(2,1)}, u32[]{:S(2)}, u32[]{:S(2)}) collective-permute-start(bf16[2,256,2560]{1,2,0:T(8,128)(2,1)} %pad_maximum_fusion.1), channel_id=1, source_target_pairs={{0,1},{1,2},{2,3},{4,5},{5,6},{6,7},{8,9},{9,10},{10,11},{12,13},{... | collective-permute-start | bytes 7864328 | tf_op jit(solution)/shard_map/ppermute | solution.py:13
  18.3 1.3 collective-permute-start.1
  19.6 2.6 copy.11
  22.2 97.3 %collective-permute-done = bf16[2,256,2560]{1,2,0:T(8,128)(2,1)} collective-permute-done((bf16[2,256,2560]{1,2,0:T(8,128)(2,1)}, bf16[2,256,2560]{1,2,0:T(8,128)(2,1)}, u32[]{:S(2)}, u32[]{:S(2)}) %collective-permute-start) | collective-permute-done | bytes 2621472 | tf_op jit(solution)/shard_map/ppermute | solution.py:13
  119.5 53.5 %collective-permute-done.1 = bf16[2,256,2560]{1,2,0:T(8,128)(2,1)} collective-permute-done((bf16[2,256,2560]{1,2,0:T(8,128)(2,1)}, bf16[2,256,2560]{1,2,0:T(8,128)(2,1)}, u32[]{:S(2)}, u32[]{:S(2)}) %collective-permute-start.1) | collective-permute-done | bytes 2621472 | tf_op jit(solution)/shard_map/ppermute | solution.py:13
  173.1 3.3 pad_maximum_fusion
  176.4 0.0 copy-start.2
  176.4 3.3 fusion.15
  179.7 0.0 copy-done.2
  179.7 10.6 %fusion.16 = (f32[20,256]{1,0:T(8,128)S(1)}, f32[20,256,768]{1,2,0:T(8,128)}) fusion(pred[768]{0:T(1024)(128)(4,1)S(1)} %pad_add_fusion, bf16[768,20,128]{0,2,1:T(8,128)(2,1)} %bitcast.31, bf16[256,20,128]{0,2,1:T(8,128)(2,1)S(1)} %bitcast.33), kind=kOutput, calls=%fused_computation.21 | convolution fusion | flops 1022362368 | bytes 20992768 | tf_op jit(solution)/shard_map/sub | solution.py:27
  190.3 0.0 copy-start
  190.3 9.4 %fusion.10 = bf16[20,128,256]{2,1,0:T(8,128)(2,1)} fusion(bf16[768,20,128]{0,2,1:T(8,128)(2,1)} %bitcast.30, f32[20,256,768]{1,2,0:T(8,128)} %get-tuple-element.8, f32[20,256]{1,0:T(8,128)S(1)} %get-tuple-element.7), kind=kOutput, calls=%fused_computation.15 | convolution fusion | flops 1015152640 | bytes 20992000 | tf_op jit(solution)/shard_map/hqk,khd->qhd/dot_general | solution.py:29
  199.7 300.6 %all-gather.2.cloned.1.call-done = bf16[2560,5120]{1,0:T(8,128)(2,1)} async-done(((bf16[640,5120]{1,0:T(8,128)(2,1)}), bf16[2560,5120]{1,0:T(8,128)(2,1)}) %all-gather.2.cloned.1.call-update) | async-done | bytes 26214416 | tf_op jit(solution)/shard_map/all_gather | solution.py:48
  500.4 0.0 copy-done
  500.4 13.5 %fusion.9 = bf16[256,5120]{1,0:T(8,128)(2,1)} fusion(bf16[256,2560]{0,1:T(8,128)(2,1)} %bitcast.32, bf16[2560,5120]{1,0:T(8,128)(2,1)} %all-gather.2.cloned.1.call-done, bf16[256,5120]{1,0:T(8,128)(2,1)S(1)} %copy-done), kind=kOutput, calls=%fused_computation.13 | convolution fusion | flops 6714818560 | bytes 32768000 | tf_op jit(solution)/shard_map/dot_general | solution.py:46
  (4 shorter events, 0.0 us)
Async XLA Ops:
  6.5 1.3 copy-start.1
  6.5 493.8 %all-gather.2.cloned.1.call-start = ((), (), s32[]{:S(2)}) async-start(), calls=%async_computation | async-start | bytes 32768000 | tf_op jit(solution)/shard_map/all_gather | solution.py:48
  11.8 107.7 %collective-permute-start = (bf16[2,256,2560]{1,2,0:T(8,128)(2,1)}, bf16[2,256,2560]{1,2,0:T(8,128)(2,1)}, u32[]{:S(2)}, u32[]{:S(2)}) collective-permute-start(bf16[2,256,2560]{1,2,0:T(8,128)(2,1)} %pad_maximum_fusion.1), channel_id=1, source_target_pairs={{0,1},{1,2},{2,3},{4,5},{5,6},{6,7},{8,9},{9,10},{10,11},{12,13},{... | collective-permute-start | bytes 7864328 | tf_op jit(solution)/shard_map/ppermute | solution.py:13
  18.3 154.8 %collective-permute-start.1 = (bf16[2,256,2560]{1,2,0:T(8,128)(2,1)}, bf16[2,256,2560]{1,2,0:T(8,128)(2,1)}, u32[]{:S(2)}, u32[]{:S(2)}) collective-permute-start(bf16[2,256,2560]{1,2,0:T(8,128)(2,1)} %pad_maximum_fusion.1), channel_id=1, source_target_pairs={{1,0},{2,1},{3,2},{5,4},{6,5},{7,6},{9,8},{10,9},{11,10},{13,12},{... | collective-permute-start | bytes 7864328 | tf_op jit(solution)/shard_map/ppermute | solution.py:13
  176.4 3.3 copy-start.2
  190.3 310.1 %copy-start = (bf16[256,5120]{1,0:T(8,128)(2,1)S(1)}, bf16[256,5120]{1,0:T(8,128)(2,1)}, u32[]{:S(2)}) copy-start(bf16[256,5120]{1,0:T(8,128)(2,1)} %param.8) | copy-start | bytes 7864324
Sparse Core Ops, SparseCore 0:
  8.9 491.3 all-gather.1
where the time goes:
time: 521 us
  waiting for transfers between devices  452 us (87%)
  matrix products  33.5 us (6%)
  between operations  13.5 us (3%)
  local copies, waits for them, and re-layouts  8.77 us (2%)
  starting transfers between devices  7.75 us (1%)
    all_gather x1, waiting for transfers between devices, local(): lax.all_gather(out_weight, 'ctx', axis=0, tiled=True)  301 us
    ppermute x2, waiting for transfers between devices, passed_along(): lax.ppermute(value, axis, [(source, source + steps) for source in range(l...  151 us
    dot_general x1, matrix products, local(): jnp.dot(context, lax.all_gather(out_weight, 'ctx', axis=0, tiled=True), p...  13.5 us
    sub x1, matrix products, attend_window(): expon = jnp.exp(scores - largest)  10.6 us
  transfers between devices with their start and end apart: 3, of which 3 were waited for; matrix products, arithmetic and copies ran while one was open for 6% of the time, Pallas kernels for 0%

commit v1 on v0

v1 whole, which is shorter than its diff:
```python
import functools

import jax
import jax.numpy as jnp
from jax import lax
from jax.experimental import pallas as pl
from jax.experimental.pallas import tpu as pltpu
from jax.sharding import PartitionSpec as P

HEAD_SIZE = 128
LOG2_E = 1.4426950408889634
LOW = -1e30
MIB = 1024 * 1024


def passed_along(value, steps):
    count = lax.axis_size("ctx")
    leading, last = (max(0, -steps), min(count, count - steps))
    return lax.ppermute(value, "ctx", [(source, source + steps) for source in range(leading, last)])


def passed_round(value):
    count = lax.axis_size("ctx")
    return lax.ppermute(value, "ctx", [(source, (source + 1) % count) for source in range(count)])


def swapped(value, mask):
    count = lax.axis_size("dp")
    return lax.ppermute(value, "dp", [(source, source ^ mask) for source in range(count)])


def after(value, *tokens):
    def kernel(*refs):
        del refs

    place = pl.BlockSpec(memory_space=pl.ANY)
    return pl.pallas_call(
        kernel,
        out_shape=jax.ShapeDtypeStruct(value.shape, value.dtype),
        in_specs=[place] * (1 + len(tokens)),
        out_specs=place,
        input_output_aliases={0: 0},
        cost_estimate=pl.CostEstimate(flops=0, bytes_accessed=0, transcendentals=0),
        name="after",
    )(value, *tokens)


def near(piece):
    count = lax.axis_size("dp")
    return {1 << at: [swapped(piece, 1 << at)] for at in range(1, count.bit_length() - 1)}


def far(pieces):
    count = lax.axis_size("dp")
    pieces = dict(pieces)
    for mask in range(2, count, 2):
        if mask in pieces:
            continue
        low = mask & -mask
        high = mask ^ low
        if high & (high - 1) == 0:
            half = pieces[low][0].shape[0] // 2
            pieces[mask] = [swapped(pieces[low][0][:half], high), swapped(pieces[high][0][half:], low)]
        else:
            pieces[mask] = [swapped(part, low) for part in pieces[high]]
    return pieces


def both_cores(pieces):
    count = lax.axis_size("dp")
    pieces = dict(pieces)
    for mask in range(0, count, 2):
        pieces[mask ^ 1] = [swapped(part, 1) for part in pieces[mask]]
    return [pieces[mask] for mask in range(count)]


def pack_kernel(groups, key_up, value_up, key_down, value_down, token_ref, up_ref, down_ref):
    rows = key_up.shape[0]
    up_ref[:rows] = key_up[...]
    up_ref[rows:] = value_up[...]
    down_ref[:rows] = key_down[...]
    down_ref[rows:] = value_down[...]


def packed(groups, key_frames, value_frames, token, width):
    rows = key_frames.shape[0]
    shape = jax.ShapeDtypeStruct((2 * rows, width), key_frames.dtype)
    up = pl.BlockSpec((rows, width), lambda step, groups: (0, groups[0]))
    down = pl.BlockSpec((rows, width), lambda step, groups: (0, groups[1]))
    both = pl.BlockSpec((2 * rows, width), lambda step, groups: (0, 0))
    return pl.pallas_call(
        pack_kernel,
        out_shape=(shape, shape),
        grid_spec=pltpu.PrefetchScalarGridSpec(
            num_scalar_prefetch=1,
            grid=(1,),
            in_specs=[up, up, down, down, pl.BlockSpec(memory_space=pl.ANY)],
            out_specs=[both, both],
        ),
        compiler_params=pltpu.CompilerParams(vmem_limit_bytes=16 * MIB),
        cost_estimate=pl.CostEstimate(flops=0, bytes_accessed=8 * rows * width * 2, transcendentals=0),
        name="pack_window",
    )(groups, key_frames, value_frames, key_frames, value_frames, token)


def attend_kernel(place, query_ref, key_ref, value_ref, earlier_ref, later_ref, context_ref):
    rows, width = query_ref.shape
    ones = jnp.ones((rows, HEAD_SIZE), jnp.bfloat16)
    sides = ((earlier_ref, place[1] > 0), (later_ref, place[2] > 0))
    for at in range(0, width, HEAD_SIZE):
        head = pl.ds(at, HEAD_SIZE)
        query = query_ref[:, head]

        def scores(keys):
            return lax.dot_general(query, keys, (((1,), (1,)), ((), ())), preferred_element_type=jnp.float32)

        parts = [scores(key_ref[:, head])]
        values = [value_ref[:, head]]
        for side, there in sides:
            parts.append(jnp.where(there, scores(side[:rows, head]), LOW))
            values.append(side[rows:, head])
        largest = jnp.max(functools.reduce(jnp.maximum, parts), axis=1, keepdims=True)
        sums = 0.0
        for part, value in zip(parts, values):
            expon = jnp.exp2((part - largest) * (HEAD_SIZE ** (-0.5) * LOG2_E)).astype(jnp.bfloat16)
            sums += jnp.dot(expon, jnp.concatenate([value, ones], 1), preferred_element_type=jnp.float32)
        context_ref[:, head] = (sums[:, :HEAD_SIZE] / sums[:, HEAD_SIZE:]).astype(context_ref.dtype)


def attended(place, query_frames, key_frames, value_frames, earlier, later):
    rows, width = earlier.shape[0] // 2, earlier.shape[1]
    heads = width // HEAD_SIZE
    own = pl.BlockSpec((rows, width), lambda step, place: (0, place[0]))
    other = pl.BlockSpec((2 * rows, width), lambda step, place: (0, 0))
    return pl.pallas_call(
        attend_kernel,
        out_shape=jax.ShapeDtypeStruct((rows, width), query_frames.dtype),
        grid_spec=pltpu.PrefetchScalarGridSpec(
            num_scalar_prefetch=1,
            grid=(1,),
            in_specs=[own, own, own, other, other],
            out_specs=pl.BlockSpec((rows, width), lambda step, place: (0, 0)),
        ),
        compiler_params=pltpu.CompilerParams(vmem_limit_bytes=24 * MIB),
        cost_estimate=pl.CostEstimate(
            flops=12 * rows * rows * width,
            bytes_accessed=16 * rows * width,
            transcendentals=3 * rows * rows * heads,
        ),
        name="attend_heads",
    )(place, query_frames, key_frames, value_frames, earlier, later)


def project_kernel(counts, blocks, own, *refs):
    step = pl.program_id(0)
    context_refs, refs = refs[: len(counts) + own], refs[len(counts) + own :]
    if own:
        weight_ref, refs = refs[0], refs[1:]
    base_ref, refs = refs[0], refs[1:]
    pieces = []
    for count in counts:
        slot = []
        for parts in count:
            slot.append(refs[:parts])
            refs = refs[parts:]
        pieces.append(slot)
    out_ref, held, sems = refs

    @pl.when(step == 0)
    def _():
        for block in range(blocks):
            for slot, parts_of in enumerate(pieces):
                at = 0
                for part in parts_of[block]:
                    pltpu.make_async_copy(
                        part, held.at[slot, block, pl.ds(at, part.shape[0])], sems.at[slot, block]
                    ).start()
                    at += part.shape[0]

    result = base_ref[...].astype(jnp.float32)
    if own:
        result += jnp.dot(context_refs[0][...], weight_ref[...], preferred_element_type=jnp.float32)
    for slot in range(len(counts)):
        whole = held.at[slot, step]
        pltpu.make_async_copy(whole, whole, sems.at[slot, step]).wait()
        result += jnp.dot(context_refs[slot + own][...], whole[...], preferred_element_type=jnp.float32)
    out_ref[...] = result.astype(out_ref.dtype)


def projected(place, contexts, weight, slots, base, out_dtype):
    rows, depth = contexts[0].shape
    blocks = len(slots[0])
    columns = base.shape[1] // blocks
    own = int(weight is not None)
    counts = tuple(tuple(len(parts) for parts in slot) for slot in slots)
    flat = [part for slot in slots for parts in slot for part in parts]
    column = lambda step, place: (0, lax.bitwise_xor(place[0], step))

    def kernel(place, *refs):
        project_kernel(counts, blocks, own, *refs)

    size = len(contexts) * depth * base.shape[1]
    return pl.pallas_call(
        kernel,
        out_shape=jax.ShapeDtypeStruct(base.shape, out_dtype),
        grid_spec=pltpu.PrefetchScalarGridSpec(
            num_scalar_prefetch=1,
            grid=(blocks,),
            in_specs=[pl.BlockSpec((rows, depth), lambda step, place: (0, 0)) for _ in contexts]
            + [pl.BlockSpec((depth, columns), column)] * own
            + [pl.BlockSpec((rows, columns), column)]
            + [pl.BlockSpec(memory_space=pl.ANY)] * len(flat),
            out_specs=pl.BlockSpec((rows, columns), column),
            scratch_shapes=[
                pltpu.VMEM((len(slots), blocks, depth, columns), jnp.bfloat16),
                pltpu.SemaphoreType.DMA((len(slots), blocks)),
            ],
        ),
        compiler_params=pltpu.CompilerParams(vmem_limit_bytes=32 * MIB),
        cost_estimate=pl.CostEstimate(
            flops=2 * rows * size,
            bytes_accessed=2 * size + 8 * rows * base.shape[1],
            transcendentals=0,
        ),
        name="project_slots",
    )(place, *contexts, *([weight] * own), base, *flat)


def by_slots(query_frames, key_frames, value_frames, stream, out_weight):
    width, columns = out_weight.shape
    position, members = lax.axis_index("ctx"), lax.axis_size("ctx")
    lane, lanes = lax.axis_index("dp"), lax.axis_size("dp")
    lane_place = jnp.stack([lane]).astype(jnp.int32)

    def group(slot):
        return lax.rem(position - slot + 2 * members, members)

    share = columns // lanes
    moving = lax.dynamic_slice_in_dim(out_weight, lane * share, share, 1)
    arrived, beside = [], []
    for slot in range(1, members):
        moving = passed_round(moving)
        if beside:
            moving = after(moving, *[part for parts in beside[-1].values() for part in parts])
        arrived.append(moving)
        beside.append(near(moving))
    slots = [both_cores(far({0: [piece], **pieces})) for piece, pieces in zip(arrived, beside)]

    contexts = []
    for slot in range(members):
        groups = jnp.stack([group(slot - 1), group(slot + 1)]).astype(jnp.int32)
        up, down = packed(groups, key_frames, value_frames, arrived[min(slot + 1, members - 2)], width)
        earlier, later = passed_along(up, 1), passed_along(down, -1)
        place = jnp.stack([group(slot), position, members - 1 - position]).astype(jnp.int32)
        contexts.append(attended(place, query_frames, key_frames, value_frames, earlier, later))

    sums = projected(lane_place, contexts[:-1], out_weight, slots[:-1], stream, jnp.float32)
    return projected(lane_place, contexts[-1:], None, slots[-1:], sums, stream.dtype)


def whole_window(query_frames, key_frames, value_frames, stream, out_weight):
    rows, width = query_frames.shape
    heads = width // HEAD_SIZE
    position, members = lax.axis_index("ctx"), lax.axis_size("ctx")
    both = jnp.stack([key_frames, value_frames], 0)
    window = jnp.concatenate([passed_along(both, 1), both, passed_along(both, -1)], 1)
    valid = jnp.repeat(jnp.stack([position > 0, True, position < members - 1]), rows)
    query, key, value = (a.reshape(-1, heads, HEAD_SIZE) for a in (query_frames, window[0], window[1]))
    scores = jnp.einsum("qhd,khd->hqk", query, key, preferred_element_type=jnp.float32) * HEAD_SIZE ** (-0.5)
    probs = jax.nn.softmax(jnp.where(valid[None, None, :], scores, LOW), axis=2).astype(jnp.bfloat16)
    context = jnp.einsum("hqk,khd->qhd", probs, value, preferred_element_type=jnp.float32)
    context = context.astype(jnp.bfloat16).reshape(rows, width)
    weight = lax.all_gather(out_weight, "ctx", axis=0, tiled=True)
    product = jnp.dot(context, weight, preferred_element_type=jnp.float32)
    return (stream.astype(jnp.float32) + product).astype(stream.dtype)


def local(query_frames, key_frames, value_frames, stream, out_weight):
    lanes, members = lax.axis_size("dp"), lax.axis_size("ctx")
    width, columns = out_weight.shape
    arguments = (query_frames, key_frames, value_frames, stream, out_weight)
    fits = width % HEAD_SIZE == 0 and columns % (lanes * HEAD_SIZE) == 0 and lanes & (lanes - 1) == 0
    if fits and members > 2 and lanes > 1:
        return by_slots(*arguments)
    return whole_window(*arguments)


def solution(mesh):
    in_specs = (
        P(("dp", "ctx"), None),
        P(("dp", "ctx"), None),
        P(("dp", "ctx"), None),
        P(("dp", "ctx"), None),
        P("ctx", None),
    )
    out_specs = P(("dp", "ctx"), None)
    return jax.shard_map(local, mesh=mesh, in_specs=in_specs, out_specs=out_specs, check_vma=False)
```

time: 521 us -> 197 us (0.38)
  waiting for transfers between devices: 452 us -> 93.5 us
  Pallas kernels: 0 us -> 38.7 us
  matrix products: 33.5 us -> 0 us
  starting transfers between devices: 7.75 us -> 41.2 us
  local copies, waits for them, and re-layouts: 8.77 us -> 21.9 us
  between operations: 13.5 us -> 0.54 us
    all_gather x1 -> x0, waiting for transfers between devices: 301 us -> none  [local(): lax.all_gather(out_weight, 'ctx', axis=0, tiled=True)]
    ppermute x2 -> x38, waiting for transfers between devices: 151 us -> 93.5 us  [the longest x8 40.6 us: passed_along(): lax.ppermute(value, 'ctx', [(source, source + steps) for source in range(...]
    pallas_call x0 -> x12, Pallas kernels: none -> 38.7 us  [the longest x2 22.5 us: projected(): pl.pallas_call(kernel, out_shape=jax.ShapeDtypeStruct(base.shape, out_dty...]
    ppermute x2 -> x38, starting transfers between devices: 7.75 us -> 41.2 us  [the longest x8 24.6 us: passed_along(): lax.ppermute(value, 'ctx', [(source, source + steps) for source in range(...]
    dot_general x2 -> x0, matrix products: 22.9 us -> none  [the longest x1 13.5 us: local(): jnp.dot(context, lax.all_gather(out_weight, 'ctx', axis=0, tiled=True), p...]
    sub x1 -> x0, matrix products: 10.6 us -> none  [attend_window(): expon = jnp.exp(scores - largest)]
    unnamed x9 -> x46, local copies, waits for them, and re-layouts: 5.45 us -> 11.4 us
    slice x1 -> x6, local copies, waits for them, and re-layouts: 3.31 us -> 9.25 us  [the longest x3 4.64 us: far(): pieces[low][0][:half]]
  transfers between devices with their start and end apart: 3 -> 38, of which waited for: 3 -> 12; matrix products, arithmetic and copies ran while one was open for 6% -> 5% of each run, Pallas kernels for 0% -> 16%
where the time goes in v1:
time: 197 us; the launch traced here: 196 us
  waiting for transfers between devices  93.5 us (47%)
  starting transfers between devices  41.2 us (21%)
  Pallas kernels  38.7 us (20%)
  local copies, waits for them, and re-layouts  21.9 us (11%)
    ppermute x8, waiting for transfers between devices, passed_along(): lax.ppermute(value, 'ctx', [(source, source + steps) for source in range(...  40.6 us
    ppermute x3, waiting for transfers between devices, passed_round(): lax.ppermute(value, 'ctx', [(source, (source + 1) % count) for source in...  30 us
    ppermute x8, starting transfers between devices, passed_along(): lax.ppermute(value, 'ctx', [(source, source + steps) for source in range(...  24.6 us
    ppermute x27, waiting for transfers between devices, swapped(): lax.ppermute(value, 'dp', [(source, source ^ mask) for source in range(co...  22.9 us
    pallas_call x2, Pallas kernels, projected(): pl.pallas_call(kernel, out_shape=jax.ShapeDtypeStruct(base.shape, out_dty...  22.5 us
    ppermute x27, starting transfers between devices, swapped(): lax.ppermute(value, 'dp', [(source, source ^ mask) for source in range(co...  13.5 us
    unnamed x46, local copies, waits for them, and re-layouts  11.4 us
    pallas_call x4, Pallas kernels, attended(): pl.pallas_call(attend_kernel, out_shape=jax.ShapeDtypeStruct((rows, width...  11.2 us
  transfers between devices with their start and end apart: 38, of which 12 were waited for; matrix products, arithmetic and copies ran while one was open for 5% of the time, Pallas kernels for 16%

profile of v1, /device:TPU:0, one launch (start us, length us, event | category | flops | bytes accessed | tf_op | source)
XLA Modules:
  0.0 196.2 jit_solution(14918644499920143064)
XLA Ops:
  1.2 3.1 %collective-permute-start = (bf16[640,640]{1,0:T(8,128)(2,1)S(1)}, bf16[640,640]{1,0:T(8,128)(2,1)S(1)}, u32[]{:S(2)}, u32[]{:S(2)}) collective-permute-start(bf16[640,640]{1,0:T(8,128)(2,1)S(1)} %constant_dynamic-slice_fusion), channel_id=1, source_target_pairs={{0,1},{1,2},{2,3},{3,0},{4,5},{5,6},{6,7},{7,4},{8,9},{9,10},{10,1... | collective-permute-start | bytes 2457608 | tf_op jit(solution)/shard_map/ppermute | solution.py:24
  4.3 20.3 %collective-permute-done.refs_5_ = bf16[640,640]{1,0:T(8,128)(2,1)S(1)} collective-permute-done((bf16[640,640]{1,0:T(8,128)(2,1)S(1)}, bf16[640,640]{1,0:T(8,128)(2,1)S(1)}, u32[]{:S(2)}, u32[]{:S(2)}) %collective-permute-start) | collective-permute-done | bytes 819232 | tf_op jit(solution)/shard_map/ppermute | solution.py:24
  24.6 1.5 collective-permute-start.2
  26.1 1.5 collective-permute-start.3
  27.6 16.5 %collective-permute-done.2.refs_1_.refs_7_ = bf16[640,640]{1,0:T(8,128)(2,1)} collective-permute-done((bf16[640,640]{1,0:T(8,128)(2,1)S(1)}, bf16[640,640]{1,0:T(8,128)(2,1)}, u32[]{:S(2)}, u32[]{:S(2)}) %collective-permute-start.2) | collective-permute-done | bytes 819232 | tf_op jit(solution)/shard_map/ppermute | solution.py:29
  44.1 1.8 slice.24
  47.2 1.8 slice.25
  49.0 1.5 collective-permute-start.19
  52.6 4.6 %collective-permute-start.9 = (bf16[512,640]{1,0:T(8,128)(2,1)S(1)}, bf16[512,640]{1,0:T(8,128)(2,1)S(1)}, u32[]{:S(2)}, u32[]{:S(2)}) collective-permute-start(bf16[512,640]{1,0:T(8,128)(2,1)S(1)} %get-tuple-element.15), channel_id=1, source_target_pairs={{0,1},{1,2},{2,3},{4,5},{5,6},{6,7},{8,9},{9,10},{10,11},{12,13},{... | collective-permute-start | bytes 1966088 | tf_op jit(solution)/shard_map/ppermute | solution.py:19
  59.7 11.2 %collective-permute-done.10.later_ref = bf16[512,640]{1,0:T(8,128)(2,1)S(1)} collective-permute-done((bf16[512,640]{1,0:T(8,128)(2,1)S(1)}, bf16[512,640]{1,0:T(8,128)(2,1)S(1)}, u32[]{:S(2)}, u32[]{:S(2)}) %collective-permute-start.10) | collective-permute-done | bytes 655392 | tf_op jit(solution)/shard_map/ppermute | solution.py:19
  73.2 2.8 %collective-permute-done.5.refs_1_.refs_17_ = bf16[640,640]{1,0:T(8,128)(2,1)} collective-permute-done((bf16[640,640]{1,0:T(8,128)(2,1)}, bf16[640,640]{1,0:T(8,128)(2,1)}, u32[]{:S(2)}, u32[]{:S(2)}) %collective-permute-start.5) | collective-permute-done | bytes 819232 | tf_op jit(solution)/shard_map/ppermute | solution.py:29
  76.6 9.7 %collective-permute-done.4.refs_0_ = bf16[640,640]{1,0:T(8,128)(2,1)S(1)} collective-permute-done((bf16[640,640]{1,0:T(8,128)(2,1)}, bf16[640,640]{1,0:T(8,128)(2,1)S(1)}, u32[]{:S(2)}, u32[]{:S(2)}) %collective-permute-start.4) | collective-permute-done | bytes 819232 | tf_op jit(solution)/shard_map/ppermute | solution.py:24
  88.3 1.9 pack_window.7
  90.2 5.2 %collective-permute-start.13 = (bf16[512,640]{1,0:T(8,128)(2,1)}, bf16[512,640]{1,0:T(8,128)(2,1)}, u32[]{:S(2)}, u32[]{:S(2)}) collective-permute-start(bf16[512,640]{1,0:T(8,128)(2,1)} %get-tuple-element.19), channel_id=1, source_target_pairs={{0,1},{1,2},{2,3},{4,5},{5,6},{6,7},{8,9},{9,10},{10,11},{12,13},{... | collective-permute-start | bytes 1966088 | tf_op jit(solution)/shard_map/ppermute | solution.py:19
  96.6 1.8 slice.26
  98.9 1.8 slice.27
  102.6 4.6 %collective-permute-start.11 = (bf16[512,640]{1,0:T(8,128)(2,1)S(1)}, bf16[512,640]{1,0:T(8,128)(2,1)S(1)}, u32[]{:S(2)}, u32[]{:S(2)}) collective-permute-start(bf16[512,640]{1,0:T(8,128)(2,1)S(1)} %get-tuple-element.17), channel_id=1, source_target_pairs={{0,1},{1,2},{2,3},{4,5},{5,6},{6,7},{8,9},{9,10},{10,11},{12,13},{... | collective-permute-start | bytes 1966088 | tf_op jit(solution)/shard_map/ppermute | solution.py:19
  107.2 2.3 %collective-permute-done.25.refs_21_ = bf16[320,640]{1,0:T(8,128)(2,1)} collective-permute-done((bf16[320,640]{1,0:T(8,128)(2,1)}, bf16[320,640]{1,0:T(8,128)(2,1)}, u32[]{:S(2)}, u32[]{:S(2)}) %collective-permute-start.25) | collective-permute-done | bytes 409632 | tf_op jit(solution)/shard_map/ppermute | solution.py:29
  110.8 1.6 pack_window.4
  112.4 4.9 %collective-permute-start.7 = (bf16[512,640]{1,0:T(8,128)(2,1)S(1)}, bf16[512,640]{1,0:T(8,128)(2,1)S(1)}, u32[]{:S(2)}, u32[]{:S(2)}) collective-permute-start(bf16[512,640]{1,0:T(8,128)(2,1)S(1)} %get-tuple-element.13), channel_id=1, source_target_pairs={{0,1},{1,2},{2,3},{4,5},{5,6},{6,7},{8,9},{9,10},{10,11},{12,13},{... | collective-permute-start | bytes 1966088 | tf_op jit(solution)/shard_map/ppermute | solution.py:19
  119.0 4.8 %collective-permute-done.11.earlier_ref = bf16[512,640]{1,0:T(8,128)(2,1)S(1)} collective-permute-done((bf16[512,640]{1,0:T(8,128)(2,1)S(1)}, bf16[512,640]{1,0:T(8,128)(2,1)S(1)}, u32[]{:S(2)}, u32[]{:S(2)}) %collective-permute-start.11) | collective-permute-done | bytes 655392 | tf_op jit(solution)/shard_map/ppermute | solution.py:19
  124.7 2.8 %collective-permute-done.12.later_ref = bf16[512,640]{1,0:T(8,128)(2,1)S(1)} collective-permute-done((bf16[512,640]{1,0:T(8,128)(2,1)S(1)}, bf16[512,640]{1,0:T(8,128)(2,1)S(1)}, u32[]{:S(2)}, u32[]{:S(2)}) %collective-permute-start.12) | collective-permute-done | bytes 655392 | tf_op jit(solution)/shard_map/ppermute | solution.py:19
  128.4 8.2 %collective-permute-done.7.earlier_ref = bf16[512,640]{1,0:T(8,128)(2,1)S(1)} collective-permute-done((bf16[512,640]{1,0:T(8,128)(2,1)S(1)}, bf16[512,640]{1,0:T(8,128)(2,1)S(1)}, u32[]{:S(2)}, u32[]{:S(2)}) %collective-permute-start.7) | collective-permute-done | bytes 655392 | tf_op jit(solution)/shard_map/ppermute | solution.py:19
  137.4 1.5 collective-permute-start.8
  142.9 12.9 %collective-permute-done.8.later_ref = bf16[512,640]{1,0:T(8,128)(2,1)} collective-permute-done((bf16[512,640]{1,0:T(8,128)(2,1)}, bf16[512,640]{1,0:T(8,128)(2,1)}, u32[]{:S(2)}, u32[]{:S(2)}) %collective-permute-start.8) | collective-permute-done | bytes 655392 | tf_op jit(solution)/shard_map/ppermute | solution.py:19
  158.0 1.3 copy-done.2
  161.5 2.2 %attend_heads.5.refs_0_ = bf16[256,640]{1,0:T(8,128)(2,1)S(1)} custom-call(s32[3]{0:T(128)S(1)} %get-tuple-element.21.place, bf16[256,2560]{1,0:T(8,128)(2,1)S(1)} %copy-done.2, bf16[256,2560]{1,0:T(8,128)(2,1)S(1)} %copy-done, bf16[256,2560]{1,0:T(8,128)(2,1)S(1)} %copy-done.1, bf16[512,640]{1,0:T(8,128)(2,1)S(1)} %copy-done.16, bf16[512,640]{1,0:T(8,128)(2,1)S(1)} %copy-done.14), custom_call_target="tpu_custom_call" | custom-call | flops 503316480 | bytes 2621440 | tf_op jit(solution)/shard_map/attend_heads/pallas_call | solution.py:135
  163.7 3.4 %attend_heads.7.refs_2_ = bf16[256,640]{1,0:T(8,128)(2,1)S(1)} custom-call(s32[3]{0:T(128)S(1)} %add_add_fusion.3.place, bf16[256,2560]{1,0:T(8,128)(2,1)S(1)} %copy-done.2, bf16[256,2560]{1,0:T(8,128)(2,1)S(1)} %copy-done, bf16[256,2560]{1,0:T(8,128)(2,1)S(1)} %copy-done.1, bf16[512,640]{1,0:T(8,128)(2,1)} %collective-permute-done.13.earlier_ref, ...), custom_call_target="tpu_custom_call" | custom-call | flops 503316480 | bytes 2621440 | tf_op jit(solution)/shard_map/attend_heads/pallas_call | solution.py:135
  167.1 2.2 %attend_heads.6.refs_1_ = bf16[256,640]{1,0:T(8,128)(2,1)S(1)} custom-call(s32[3]{0:T(128)S(1)} %get-tuple-element.22.place, bf16[256,2560]{1,0:T(8,128)(2,1)S(1)} %copy-done.2, bf16[256,2560]{1,0:T(8,128)(2,1)S(1)} %copy-done, bf16[256,2560]{1,0:T(8,128)(2,1)S(1)} %copy-done.1, bf16[512,640]{1,0:T(8,128)(2,1)S(1)} %copy-done.18, bf16[512,640]{1,0:T(8,128)(2,1)S(1)} %copy-done.20), custom_call_target="tpu_custom_call" | custom-call | flops 503316480 | bytes 2621440 | tf_op jit(solution)/shard_map/attend_heads/pallas_call | solution.py:135
  169.4 3.5 %attend_heads.4.refs_0_ = bf16[256,640]{1,0:T(8,128)(2,1)S(1)} custom-call(s32[3]{0:T(128)S(1)} %add_add_fusion.place, bf16[256,2560]{1,0:T(8,128)(2,1)S(1)} %copy-done.2, bf16[256,2560]{1,0:T(8,128)(2,1)S(1)} %copy-done, bf16[256,2560]{1,0:T(8,128)(2,1)S(1)} %copy-done.1, bf16[512,640]{1,0:T(8,128)(2,1)S(1)} %copy-done.22, ...), custom_call_target="tpu_custom_call" | custom-call | flops 503316480 | bytes 2621440 | tf_op jit(solution)/shard_map/attend_heads/pallas_call | solution.py:135
  173.4 15.3 %project_slots.2.refs_1_ = f32[256,5120]{1,0:T(8,128)S(1)} custom-call(s32[1]{0:T(128)} %bitcast.place, bf16[256,640]{1,0:T(8,128)(2,1)S(1)} %attend_heads.5.refs_0_, bf16[256,640]{1,0:T(8,128)(2,1)S(1)} %attend_heads.6.refs_1_, bf16[256,640]{1,0:T(8,128)(2,1)S(1)} %attend_heads.7.refs_2_, bf16[640,5120]{1,0:T(8,128)(2,1)} %refs_3_.1, ...), custom_call_target="tpu_custom_call" | custom-call | flops 5033164800 | bytes 30146560 | tf_op jit(solution)/shard_map/project_slots/pallas_call | solution.py:203
  188.9 7.2 %project_slots.3 = bf16[256,5120]{1,0:T(8,128)(2,1)} custom-call(s32[1]{0:T(128)} %bitcast.place, bf16[256,640]{1,0:T(8,128)(2,1)S(1)} %attend_heads.4.refs_0_, f32[256,5120]{1,0:T(8,128)S(1)} %project_slots.2.refs_1_, bf16[640,640]{1,0:T(8,128)(2,1)S(1)} %copy-done.5, bf16[640,640]{1,0:T(8,128)(2,1)S(1)} %collective-permute-done.29.refs_3_, ...), custom_call_target="tpu_custom_call" | custom-call | flops 1677721600 | bytes 17039360 | tf_op jit(solution)/shard_map/project_slots/pallas_call | solution.py:203
  (115 shorter events, 30.0 us)
Async XLA Ops:
  1.2 23.3 %collective-permute-start = (bf16[640,640]{1,0:T(8,128)(2,1)S(1)}, bf16[640,640]{1,0:T(8,128)(2,1)S(1)}, u32[]{:S(2)}, u32[]{:S(2)}) collective-permute-start(bf16[640,640]{1,0:T(8,128)(2,1)S(1)} %constant_dynamic-slice_fusion), channel_id=1, source_target_pairs={{0,1},{1,2},{2,3},{3,0},{4,5},{5,6},{6,7},{7,4},{8,9},{9,10},{10,1... | collective-permute-start | bytes 2457608 | tf_op jit(solution)/shard_map/ppermute | solution.py:24
  24.6 19.5 %collective-permute-start.2 = (bf16[640,640]{1,0:T(8,128)(2,1)S(1)}, bf16[640,640]{1,0:T(8,128)(2,1)}, u32[]{:S(2)}, u32[]{:S(2)}) collective-permute-start(bf16[640,640]{1,0:T(8,128)(2,1)S(1)} %collective-permute-done.refs_5_), channel_id=1, source_target_pairs={{0,8},{4,12},{8,0},{12,4},{16,24},{20,28},{24,16},{28,20},{1,9},{5... | collective-permute-start | bytes 2457608 | tf_op jit(solution)/shard_map/ppermute | solution.py:29
  26.1 21.1 %collective-permute-start.3 = (bf16[640,640]{1,0:T(8,128)(2,1)S(1)}, bf16[640,640]{1,0:T(8,128)(2,1)}, u32[]{:S(2)}, u32[]{:S(2)}) collective-permute-start(bf16[640,640]{1,0:T(8,128)(2,1)S(1)} %collective-permute-done.refs_5_), channel_id=1, source_target_pairs={{0,16},{4,20},{8,24},{12,28},{16,0},{20,4},{24,8},{28,12},{1,17},{... | collective-permute-start | bytes 2457608 | tf_op jit(solution)/shard_map/ppermute | solution.py:29
  27.6 22.9 %collective-permute-start.1 = (bf16[640,640]{1,0:T(8,128)(2,1)S(1)}, bf16[640,640]{1,0:T(8,128)(2,1)}, u32[]{:S(2)}, u32[]{:S(2)}) collective-permute-start(bf16[640,640]{1,0:T(8,128)(2,1)S(1)} %collective-permute-done.refs_5_), channel_id=1, source_target_pairs={{0,1},{1,2},{2,3},{3,0},{4,5},{5,6},{6,7},{7,4},{8,9},{9,10},{10,1... | collective-permute-start | bytes 2457608 | tf_op jit(solution)/shard_map/ppermute | solution.py:24
  27.6 29.6 %collective-permute-start.15 = (bf16[640,640]{1,0:T(8,128)(2,1)S(1)}, bf16[640,640]{1,0:T(8,128)(2,1)}, u32[]{:S(2)}, u32[]{:S(2)}) collective-permute-start(bf16[640,640]{1,0:T(8,128)(2,1)S(1)} %collective-permute-done.refs_5_), channel_id=1, source_target_pairs={{0,4},{4,0},{8,12},{12,8},{16,20},{20,16},{24,28},{28,24},{1,5},{5... | collective-permute-start | bytes 2457608 | tf_op jit(solution)/shard_map/ppermute | solution.py:29
  51.3 19.6 %collective-permute-start.10 = (bf16[512,640]{1,0:T(8,128)(2,1)S(1)}, bf16[512,640]{1,0:T(8,128)(2,1)S(1)}, u32[]{:S(2)}, u32[]{:S(2)}) collective-permute-start(bf16[512,640]{1,0:T(8,128)(2,1)S(1)} %get-tuple-element.16), channel_id=1, source_target_pairs={{1,0},{2,1},{3,2},{5,4},{6,5},{7,6},{9,8},{10,9},{11,10},{13,12},{... | collective-permute-start | bytes 1966088 | tf_op jit(solution)/shard_map/ppermute | solution.py:19
  52.6 19.7 %collective-permute-start.9 = (bf16[512,640]{1,0:T(8,128)(2,1)S(1)}, bf16[512,640]{1,0:T(8,128)(2,1)S(1)}, u32[]{:S(2)}, u32[]{:S(2)}) collective-permute-start(bf16[512,640]{1,0:T(8,128)(2,1)S(1)} %get-tuple-element.15), channel_id=1, source_target_pairs={{0,1},{1,2},{2,3},{4,5},{5,6},{6,7},{8,9},{9,10},{10,11},{12,13},{... | collective-permute-start | bytes 1966088 | tf_op jit(solution)/shard_map/ppermute | solution.py:19
  57.2 18.8 %collective-permute-start.5 = (bf16[640,640]{1,0:T(8,128)(2,1)}, bf16[640,640]{1,0:T(8,128)(2,1)}, u32[]{:S(2)}, u32[]{:S(2)}) collective-permute-start(bf16[640,640]{1,0:T(8,128)(2,1)} %after.2.token_ref.refs_15_), channel_id=1, source_target_pairs={{0,8},{4,12},{8,0},{12,4},{16,24},{20,28},{24,16},{28,20},{1,9},{5... | collective-permute-start | bytes 2457608 | tf_op jit(solution)/shard_map/ppermute | solution.py:29
  57.8 18.2 %collective-permute-start.6 = (bf16[640,640]{1,0:T(8,128)(2,1)}, bf16[640,640]{1,0:T(8,128)(2,1)}, u32[]{:S(2)}, u32[]{:S(2)}) collective-permute-start(bf16[640,640]{1,0:T(8,128)(2,1)} %after.2.token_ref.refs_15_), channel_id=1, source_target_pairs={{0,16},{4,20},{8,24},{12,28},{16,0},{20,4},{24,8},{28,12},{1,17},{... | collective-permute-start | bytes 2457608 | tf_op jit(solution)/shard_map/ppermute | solution.py:29
  59.7 26.5 %collective-permute-start.4 = (bf16[640,640]{1,0:T(8,128)(2,1)}, bf16[640,640]{1,0:T(8,128)(2,1)S(1)}, u32[]{:S(2)}, u32[]{:S(2)}) collective-permute-start(bf16[640,640]{1,0:T(8,128)(2,1)} %after.2.token_ref.refs_15_), channel_id=1, source_target_pairs={{0,1},{1,2},{2,3},{3,0},{4,5},{5,6},{6,7},{7,4},{8,9},{9,10},{10,1... | collective-permute-start | bytes 2457608 | tf_op jit(solution)/shard_map/ppermute | solution.py:24
  71.8 18.4 %collective-permute-start.22 = (bf16[640,640]{1,0:T(8,128)(2,1)}, bf16[640,640]{1,0:T(8,128)(2,1)}, u32[]{:S(2)}, u32[]{:S(2)}) collective-permute-start(bf16[640,640]{1,0:T(8,128)(2,1)} %after.2.token_ref.refs_15_), channel_id=1, source_target_pairs={{0,4},{4,0},{8,12},{12,8},{16,20},{20,16},{24,28},{28,24},{1,5},{5... | collective-permute-start | bytes 2457608 | tf_op jit(solution)/shard_map/ppermute | solution.py:29
  73.2 27.5 %collective-permute-start.16 = (bf16[640,640]{1,0:T(8,128)(2,1)}, bf16[640,640]{1,0:T(8,128)(2,1)}, u32[]{:S(2)}, u32[]{:S(2)}) collective-permute-start(bf16[640,640]{1,0:T(8,128)(2,1)} %collective-permute-done.2.refs_1_.refs_7_), channel_id=1, source_target_pairs={{0,4},{4,0},{8,12},{12,8},{16,20},{20,16},{24,28},{28,24},{1,5},{5... | collective-permute-start | bytes 2457608 | tf_op jit(solution)/shard_map/ppermute | solution.py:29
  76.1 19.3 %collective-permute-start.20 = (bf16[320,640]{1,0:T(8,128)(2,1)}, bf16[320,640]{1,0:T(8,128)(2,1)}, u32[]{:S(2)}, u32[]{:S(2)}) collective-permute-start(bf16[320,640]{1,0:T(8,128)(2,1)} %collective-permute-done.18.refs_11_), channel_id=1, source_target_pairs={{0,4},{4,0},{8,12},{12,8},{16,20},{20,16},{24,28},{28,24},{1,5},{5... | collective-permute-start | bytes 1228808 | tf_op jit(solution)/shard_map/ppermute | solution.py:29
  76.1 26.5 %collective-permute-start.17 = (bf16[640,640]{1,0:T(8,128)(2,1)}, bf16[640,640]{1,0:T(8,128)(2,1)}, u32[]{:S(2)}, u32[]{:S(2)}) collective-permute-start(bf16[640,640]{1,0:T(8,128)(2,1)} %collective-permute-done.3.refs_2_.refs_9_), channel_id=1, source_target_pairs={{0,4},{4,0},{8,12},{12,8},{16,20},{20,16},{24,28},{28,24},{1,5},{5... | collective-permute-start | bytes 2457608 | tf_op jit(solution)/shard_map/ppermute | solution.py:29
  90.2 27.2 %collective-permute-start.13 = (bf16[512,640]{1,0:T(8,128)(2,1)}, bf16[512,640]{1,0:T(8,128)(2,1)}, u32[]{:S(2)}, u32[]{:S(2)}) collective-permute-start(bf16[512,640]{1,0:T(8,128)(2,1)} %get-tuple-element.19), channel_id=1, source_target_pairs={{0,1},{1,2},{2,3},{4,5},{5,6},{6,7},{8,9},{9,10},{10,11},{12,13},{... | collective-permute-start | bytes 1966088 | tf_op jit(solution)/shard_map/ppermute | solution.py:19
  95.3 22.7 %collective-permute-start.14 = (bf16[512,640]{1,0:T(8,128)(2,1)}, bf16[512,640]{1,0:T(8,128)(2,1)}, u32[]{:S(2)}, u32[]{:S(2)}) collective-permute-start(bf16[512,640]{1,0:T(8,128)(2,1)} %get-tuple-element.20), channel_id=1, source_target_pairs={{1,0},{2,1},{3,2},{5,4},{6,5},{7,6},{9,8},{10,9},{11,10},{13,12},{... | collective-permute-start | bytes 1966088 | tf_op jit(solution)/shard_map/ppermute | solution.py:19
  102.6 21.2 %collective-permute-start.11 = (bf16[512,640]{1,0:T(8,128)(2,1)S(1)}, bf16[512,640]{1,0:T(8,128)(2,1)S(1)}, u32[]{:S(2)}, u32[]{:S(2)}) collective-permute-start(bf16[512,640]{1,0:T(8,128)(2,1)S(1)} %get-tuple-element.17), channel_id=1, source_target_pairs={{0,1},{1,2},{2,3},{4,5},{5,6},{6,7},{8,9},{9,10},{10,11},{12,13},{... | collective-permute-start | bytes 1966088 | tf_op jit(solution)/shard_map/ppermute | solution.py:19
  109.5 18.0 %collective-permute-start.12 = (bf16[512,640]{1,0:T(8,128)(2,1)S(1)}, bf16[512,640]{1,0:T(8,128)(2,1)S(1)}, u32[]{:S(2)}, u32[]{:S(2)}) collective-permute-start(bf16[512,640]{1,0:T(8,128)(2,1)S(1)} %get-tuple-element.18), channel_id=1, source_target_pairs={{1,0},{2,1},{3,2},{5,4},{6,5},{7,6},{9,8},{10,9},{11,10},{13,12},{... | collective-permute-start | bytes 1966088 | tf_op jit(solution)/shard_map/ppermute | solution.py:19
  112.4 24.1 %collective-permute-start.7 = (bf16[512,640]{1,0:T(8,128)(2,1)S(1)}, bf16[512,640]{1,0:T(8,128)(2,1)S(1)}, u32[]{:S(2)}, u32[]{:S(2)}) collective-permute-start(bf16[512,640]{1,0:T(8,128)(2,1)S(1)} %get-tuple-element.13), channel_id=1, source_target_pairs={{0,1},{1,2},{2,3},{4,5},{5,6},{6,7},{8,9},{9,10},{10,11},{12,13},{... | collective-permute-start | bytes 1966088 | tf_op jit(solution)/shard_map/ppermute | solution.py:19
  117.4 21.5 %collective-permute-start.30 = (bf16[640,640]{1,0:T(8,128)(2,1)S(1)}, bf16[640,640]{1,0:T(8,128)(2,1)S(1)}, u32[]{:S(2)}, u32[]{:S(2)}) collective-permute-start(bf16[640,640]{1,0:T(8,128)(2,1)S(1)} %copy-done.5), channel_id=1, source_target_pairs={{0,8},{4,12},{8,0},{12,4},{16,24},{20,28},{24,16},{28,20},{1,9},{5... | collective-permute-start | bytes 2457608 | tf_op jit(solution)/shard_map/ppermute | solution.py:29
  118.0 21.0 %collective-permute-start.32 = (bf16[640,640]{1,0:T(8,128)(2,1)S(1)}, bf16[640,640]{1,0:T(8,128)(2,1)S(1)}, u32[]{:S(2)}, u32[]{:S(2)}) collective-permute-start(bf16[640,640]{1,0:T(8,128)(2,1)S(1)} %copy-done.5), channel_id=1, source_target_pairs={{0,16},{4,20},{8,24},{12,28},{16,0},{20,4},{24,8},{28,12},{1,17},{... | collective-permute-start | bytes 2457608 | tf_op jit(solution)/shard_map/ppermute | solution.py:29
  124.7 32.7 %collective-permute-start.23 = (bf16[640,640]{1,0:T(8,128)(2,1)}, bf16[640,640]{1,0:T(8,128)(2,1)}, u32[]{:S(2)}, u32[]{:S(2)}) collective-permute-start(bf16[640,640]{1,0:T(8,128)(2,1)} %collective-permute-done.5.refs_1_.refs_17_), channel_id=1, source_target_pairs={{0,4},{4,0},{8,12},{12,8},{16,20},{20,16},{24,28},{28,24},{1,5},{5... | collective-permute-start | bytes 2457608 | tf_op jit(solution)/shard_map/ppermute | solution.py:29
  128.4 29.0 %collective-permute-start.24 = (bf16[640,640]{1,0:T(8,128)(2,1)}, bf16[640,640]{1,0:T(8,128)(2,1)}, u32[]{:S(2)}, u32[]{:S(2)}) collective-permute-start(bf16[640,640]{1,0:T(8,128)(2,1)} %collective-permute-done.6.refs_2_.refs_19_), channel_id=1, source_target_pairs={{0,4},{4,0},{8,12},{12,8},{16,20},{20,16},{24,28},{28,24},{1,5},{5... | collective-permute-start | bytes 2457608 | tf_op jit(solution)/shard_map/ppermute | solution.py:29
  137.4 18.4 %collective-permute-start.8 = (bf16[512,640]{1,0:T(8,128)(2,1)}, bf16[512,640]{1,0:T(8,128)(2,1)}, u32[]{:S(2)}, u32[]{:S(2)}) collective-permute-start(bf16[512,640]{1,0:T(8,128)(2,1)} %get-tuple-element.14), channel_id=1, source_target_pairs={{1,0},{2,1},{3,2},{5,4},{6,5},{7,6},{9,8},{10,9},{11,10},{13,12},{... | collective-permute-start | bytes 1966088 | tf_op jit(solution)/shard_map/ppermute | solution.py:19
  138.9 16.9 %collective-permute-start.27 = (bf16[320,640]{1,0:T(8,128)(2,1)}, bf16[320,640]{1,0:T(8,128)(2,1)}, u32[]{:S(2)}, u32[]{:S(2)}) collective-permute-start(bf16[320,640]{1,0:T(8,128)(2,1)} %collective-permute-done.25.refs_21_), channel_id=1, source_target_pairs={{0,4},{4,0},{8,12},{12,8},{16,20},{20,16},{24,28},{28,24},{1,5},{5... | collective-permute-start | bytes 1228808 | tf_op jit(solution)/shard_map/ppermute | solution.py:29
  155.8 33.0 %collective-permute-start.29 = (bf16[640,640]{1,0:T(8,128)(2,1)S(1)}, bf16[640,640]{1,0:T(8,128)(2,1)S(1)}, u32[]{:S(2)}, u32[]{:S(2)}) collective-permute-start(bf16[640,640]{1,0:T(8,128)(2,1)S(1)} %copy-done.5), channel_id=1, source_target_pairs={{0,4},{4,0},{8,12},{12,8},{16,20},{20,16},{24,28},{28,24},{1,5},{5... | collective-permute-start | bytes 2457608 | tf_op jit(solution)/shard_map/ppermute | solution.py:29
  155.8 17.0 %collective-permute-start.34 = (bf16[320,640]{1,0:T(8,128)(2,1)S(1)}, bf16[320,640]{1,0:T(8,128)(2,1)S(1)}, u32[]{:S(2)}, u32[]{:S(2)}) collective-permute-start(bf16[320,640]{1,0:T(8,128)(2,1)S(1)} %slice.28), channel_id=1, source_target_pairs={{0,16},{4,20},{8,24},{12,28},{16,0},{20,4},{24,8},{28,12},{1,17},{... | collective-permute-start | bytes 1228808 | tf_op jit(solution)/shard_map/ppermute | solution.py:29
  156.3 16.7 %collective-permute-start.35 = (bf16[320,640]{1,0:T(8,128)(2,1)S(1)}, bf16[320,640]{1,0:T(8,128)(2,1)S(1)}, u32[]{:S(2)}, u32[]{:S(2)}) collective-permute-start(bf16[320,640]{1,0:T(8,128)(2,1)S(1)} %slice.29), channel_id=1, source_target_pairs={{0,8},{4,12},{8,0},{12,4},{16,24},{20,28},{24,16},{28,20},{1,9},{5... | collective-permute-start | bytes 1228808 | tf_op jit(solution)/shard_map/ppermute | solution.py:29
  157.4 31.5 %collective-permute-start.31 = (bf16[640,640]{1,0:T(8,128)(2,1)}, bf16[640,640]{1,0:T(8,128)(2,1)S(1)}, u32[]{:S(2)}, u32[]{:S(2)}) collective-permute-start(bf16[640,640]{1,0:T(8,128)(2,1)} %copy-done.7), channel_id=1, source_target_pairs={{0,4},{4,0},{8,12},{12,8},{16,20},{20,16},{24,28},{28,24},{1,5},{5... | collective-permute-start | bytes 2457608 | tf_op jit(solution)/shard_map/ppermute | solution.py:29
  157.4 31.5 %collective-permute-start.33 = (bf16[640,640]{1,0:T(8,128)(2,1)}, bf16[640,640]{1,0:T(8,128)(2,1)S(1)}, u32[]{:S(2)}, u32[]{:S(2)}) collective-permute-start(bf16[640,640]{1,0:T(8,128)(2,1)} %copy-done.9), channel_id=1, source_target_pairs={{0,4},{4,0},{8,12},{12,8},{16,20},{20,16},{24,28},{28,24},{1,5},{5... | collective-permute-start | bytes 2457608 | tf_op jit(solution)/shard_map/ppermute | solution.py:29
  172.9 16.0 %collective-permute-start.36 = (bf16[320,640]{1,0:T(8,128)(2,1)S(1)}, bf16[320,640]{1,0:T(8,128)(2,1)S(1)}, u32[]{:S(2)}, u32[]{:S(2)}) collective-permute-start(bf16[320,640]{1,0:T(8,128)(2,1)S(1)} %collective-permute-done.34.refs_8_), channel_id=1, source_target_pairs={{0,4},{4,0},{8,12},{12,8},{16,20},{20,16},{24,28},{28,24},{1,5},{5... | collective-permute-start | bytes 1228808 | tf_op jit(solution)/shard_map/ppermute | solution.py:29
  173.0 15.8 %collective-permute-start.37 = (bf16[320,640]{1,0:T(8,128)(2,1)S(1)}, bf16[320,640]{1,0:T(8,128)(2,1)S(1)}, u32[]{:S(2)}, u32[]{:S(2)}) collective-permute-start(bf16[320,640]{1,0:T(8,128)(2,1)S(1)} %collective-permute-done.35.refs_9_), channel_id=1, source_target_pairs={{0,4},{4,0},{8,12},{12,8},{16,20},{20,16},{24,28},{28,24},{1,5},{5... | collective-permute-start | bytes 1228808 | tf_op jit(solution)/shard_map/ppermute | solution.py:29
  (29 other events, 271.9 us)

commit v2 on v0

v2 whole, which is shorter than its diff:
```python
import functools

import jax
import jax.numpy as jnp
from jax import lax
from jax.experimental import pallas as pl
from jax.experimental.pallas import tpu as pltpu
from jax.sharding import PartitionSpec as P

HEAD_SIZE = 128
LOG2_E = 1.4426950408889634
LOW = -1e30
MIB = 1024 * 1024
VMEM_MIB = 60
PAIR_SLOTS, MIDDLE_SLOTS = (4,), (4,)
LINE = 4
LANES = 8
VMEM = pl.BlockSpec(memory_space=pltpu.VMEM)
SMEM = pl.BlockSpec(memory_space=pltpu.SMEM)
ANY = pl.BlockSpec(memory_space=pl.ANY)
HAS_MIDDLE, GROUPS, SENT, OWNERS = 0, 1, 1 + LINE, 1 + 3 * LINE


def passed_along(value, steps):
    count = lax.axis_size("ctx")
    leading, last = (max(0, -steps), min(count, count - steps))
    return lax.ppermute(value, "ctx", [(source, source + steps) for source in range(leading, last)])


PAIR, ACROSS, OUTWARD = {0: 1, 1: 0, 2: 3, 3: 2}, {1: 2, 2: 1}, {1: 0, 2: 3}


def along_line(value, *ways):
    pairs = []
    for lane in range(LANES):
        for source, target in ways[lane % 2].items():
            pairs.append((lane * LINE + source, lane * LINE + target))
    return lax.ppermute(value, ("dp", "ctx"), pairs)


def in_plane(value, *masks):
    return lax.ppermute(value, "dp", [(lane, lane ^ masks[lane % 2]) for lane in range(LANES)])


def big_kernel():
    return pltpu.CompilerParams(vmem_limit_bytes=VMEM_MIB * MIB)


def no_cost():
    return pl.CostEstimate(flops=0, bytes_accessed=0, transcendentals=0)


def step(chain, tokens, operands=()):
    def kernel(*refs):
        del refs

    values = [chain, *operands]
    return pl.pallas_call(
        kernel,
        out_shape=[jax.ShapeDtypeStruct(value.shape, value.dtype) for value in values],
        in_specs=[ANY] * (len(values) + len(tokens)),
        out_specs=[ANY] * len(values),
        input_output_aliases={at: at for at in range(len(values))},
        cost_estimate=no_cost(),
        name="step",
    )(*values, *tokens)


CHIPS = ((0, 2, 4, 6), (0, 4, 2, 6))


def to_neighbours(piece):
    return in_plane(piece, 2, 4), in_plane(piece, 4, 2)


def to_diagonal(first):
    return in_plane(first, 4, 2)


def other_core(pieces):
    return [in_plane(piece, 1, 1) for piece in pieces]


def columns_of(group, width):
    return pl.ds(pl.multiple_of(group * width, HEAD_SIZE), width)


def pack_kernel(place, key_ref, value_ref, chain_ref, *out_refs):
    rows, width = key_ref.shape[0], key_ref.shape[1] // LINE
    chain_ref[...] = jnp.zeros_like(chain_ref)
    at = SENT
    for out_ref in out_refs:
        for column in range(0, out_ref.shape[1], width):
            columns = columns_of(place[at], width)
            out_ref[:rows, column : column + width] = key_ref[:, columns]
            out_ref[rows:, column : column + width] = value_ref[:, columns]
            at += 1


def packed(place, key_frames, value_frames, width, slots):
    rows = key_frames.shape[0]
    shapes = [jax.ShapeDtypeStruct((2 * rows, count * width), key_frames.dtype) for count in slots]
    shapes = [jax.ShapeDtypeStruct((8, HEAD_SIZE), jnp.float32)] + shapes
    whole = pl.BlockSpec(key_frames.shape, lambda at, place: (0, 0))
    return pl.pallas_call(
        pack_kernel,
        out_shape=shapes,
        grid_spec=pltpu.PrefetchScalarGridSpec(
            num_scalar_prefetch=1,
            grid=(1,),
            in_specs=[whole, whole],
            out_specs=[pl.BlockSpec(shape.shape, lambda at, place: (0, 0)) for shape in shapes],
        ),
        compiler_params=big_kernel(),
        cost_estimate=no_cost(),
        name="pack_window",
    )(place, key_frames, value_frames)


def attend(has_middle, query_ref, key_ref, value_ref, pair_ref, middle_ref, context_ref):
    rows, width = query_ref.shape
    ones = jnp.ones((rows, HEAD_SIZE), jnp.bfloat16)
    for at in range(0, width, HEAD_SIZE):
        head = pl.ds(at, HEAD_SIZE)
        query = query_ref[:, head]

        def scores(keys):
            return lax.dot_general(query, keys, (((1,), (1,)), ((), ())), preferred_element_type=jnp.float32)

        parts = [scores(key_ref[:, head]), scores(pair_ref[:rows, head])]
        parts.append(jnp.where(has_middle, scores(middle_ref[:rows, head]), LOW))
        values = [value_ref[:, head], pair_ref[rows:, head], middle_ref[rows:, head]]
        largest = jnp.max(functools.reduce(jnp.maximum, parts), axis=1, keepdims=True)
        sums = 0.0
        for part, value in zip(parts, values):
            expon = jnp.exp2((part - largest) * (HEAD_SIZE ** (-0.5) * LOG2_E)).astype(jnp.bfloat16)
            sums += jnp.dot(expon, jnp.concatenate([value, ones], 1), preferred_element_type=jnp.float32)
        context_ref[:, head] = (sums[:, :HEAD_SIZE] / sums[:, HEAD_SIZE:]).astype(context_ref.dtype)


def slots_kernel(slots, side_at, counts, place, query_ref, key_ref, value_ref, base_ref, *refs):
    refs = list(refs)
    sides = [[refs.pop(0), refs.pop(0)] for _ in slots]
    weights = [[refs.pop(0) for _ in range(count)] for count in counts]
    out_ref, own, beside, held, base, done, context, own_sems, held_sems, block_sems = refs
    depth, width = own.shape[3], held.shape[2]
    columns = [columns_of(place[OWNERS + at], width) for at in range(LANES)]

    def begin(source, target, sem):
        copy = pltpu.make_async_copy(source, target, sem)
        copy.start()
        return copy

    def begin_block(nth):
        found = [begin(base_ref.at[:, columns[nth]], base.at[nth], block_sems.at[0, nth])]
        for at, weight in enumerate(weights):
            owner = place[OWNERS + nth]
            if len(weight) == LANES:
                part = weight[nth]
            elif weight[0].shape[0] == depth:
                part = weight[0].at[:, columns[nth]]
            else:
                part = weight[0].at[pl.ds(pl.multiple_of(owner * depth, depth), depth)]
            found.append(begin(part, held.at[nth, pl.ds(at * depth, depth)], held_sems.at[at, nth]))
        return found

    frames = []
    for at, slot in enumerate(slots):
        group = columns_of(place[GROUPS + slot], depth)
        found = []
        for nth, ref in enumerate((query_ref, key_ref, value_ref)):
            found.append(begin(ref.at[:, group], own.at[at, nth], own_sems.at[at, nth]))
        for nth, ref in enumerate(sides[at]):
            part = ref.at[:, pl.ds(side_at[at][nth] * depth, depth)]
            found.append(begin(part, beside.at[at, nth], own_sems.at[at, 3 + nth]))
        frames.append(found)
    blocks = []
    for at in range(len(slots)):
        for copy in frames[at]:
            copy.wait()
        if at == 0:
            blocks += [begin_block(nth) for nth in range(LANES // 2)]
        part = context.at[:, pl.ds(at * depth, depth)]
        attend(place[HAS_MIDDLE] > 0, *(own.at[at, nth] for nth in range(3)), beside.at[at, 0], beside.at[at, 1], part)
        if at == 0:
            blocks += [begin_block(nth) for nth in range(LANES // 2, LANES)]
    leaving = []
    for nth in range(LANES):
        for copy in blocks[nth]:
            copy.wait()
        product = jnp.dot(context[...], held[nth], preferred_element_type=jnp.float32)
        done[nth] = (base[nth].astype(jnp.float32) + product).astype(done.dtype)
        leaving.append(begin(done.at[nth], out_ref.at[:, columns[nth]], block_sems.at[1, nth]))
    for copy in leaving:
        copy.wait()


def worked_off(slots, place, frames, base, sides, weights, dtype):
    rows, columns = base.shape
    depth, width = frames[0].shape[1] // LINE, columns // LANES
    count = len(slots)
    side_at = [[at for _, at in pair] for pair in sides]
    flat = [buffer for pair in sides for buffer, _ in pair] + [part for weight in weights for part in weight]
    kernel = functools.partial(slots_kernel, slots, side_at, [len(weight) for weight in weights])
    return pl.pallas_call(
        kernel,
        out_shape=jax.ShapeDtypeStruct(base.shape, dtype),
        in_specs=[SMEM] + [ANY] * (4 + len(flat)),
        out_specs=ANY,
        scratch_shapes=[
            pltpu.VMEM((count, 3, rows, depth), jnp.bfloat16),
            pltpu.VMEM((count, 2, 2 * rows, depth), jnp.bfloat16),
            pltpu.VMEM((LANES, count * depth, width), jnp.bfloat16),
            pltpu.VMEM((LANES, rows, width), base.dtype),
            pltpu.VMEM((LANES, rows, width), dtype),
            pltpu.VMEM((rows, count * depth), jnp.bfloat16),
            pltpu.SemaphoreType.DMA((count, 5)),
            pltpu.SemaphoreType.DMA((count, LANES)),
            pltpu.SemaphoreType.DMA((2, LANES)),
        ],
        compiler_params=big_kernel(),
        cost_estimate=pl.CostEstimate(
            flops=2 * rows * depth * count * (columns + 6 * rows),
            bytes_accessed=2 * depth * count * (columns + 7 * rows) + 8 * rows * columns,
            transcendentals=0,
        ),
        name="work_off_slots",
    )(place, *frames, base, *flat)


def by_slots(query_frames, key_frames, value_frames, stream, out_weight):
    width, columns = out_weight.shape
    position, lane = lax.axis_index("ctx"), lax.axis_index("dp")
    edge = (position == 0) | (position == LINE - 1)
    core = lane & 1

    def order(member):
        side = (member >= 2).astype(jnp.int32)
        return jnp.stack([member, member ^ 1, 2 - side, 3 - 3 * side])

    def by_core(one, other):
        return jnp.where(core == 0, one, other)

    to_pair, over_middle = order(position ^ 1), order(LINE - 1 - position)
    has_middle = 1 - edge.astype(jnp.int32)
    chips = by_core(jnp.array(CHIPS[0]), jnp.array(CHIPS[1]))
    other_chips = by_core(jnp.array(CHIPS[1]), jnp.array(CHIPS[0]))
    owners = [lane ^ chips, lane ^ 1 ^ other_chips]
    place = jnp.concatenate([has_middle[None], order(position), to_pair, over_middle, *owners]).astype(jnp.int32)

    share = columns // LANES
    mine = lax.dynamic_slice_in_dim(out_weight, lane * share, share, 1)
    slots = PAIR_SLOTS + MIDDLE_SLOTS
    chain, *packs = packed(place, key_frames, value_frames, width, slots)
    to_pair, over_middle = packs[: len(PAIR_SLOTS)], packs[len(PAIR_SLOTS) :]

    frames = (query_frames, key_frames, value_frames)

    def side(slot, buffers, counts):
        return [(buffer, at) for buffer, count in zip(buffers, counts) for at in range(count)][slot]

    def worked(slots, base, pairs, middles, weights, dtype):
        sides = [(side(slot, pairs, PAIR_SLOTS), side(slot, middles, MIDDLE_SLOTS)) for slot in slots]
        return worked_off(slots, place, frames, base, sides, weights, dtype)

    def to_pairs(value):
        return along_line(value, PAIR, PAIR)

    def to_middle(value):
        return along_line(value, ACROSS, ACROSS)

    first, crossed = to_pairs(mine), to_middle(mine)
    chain, first, crossed = step(chain, [], [first, crossed])
    outer, across = along_line(crossed, OUTWARD, OUTWARD), to_middle(first)
    first_near = to_neighbours(first)

    chain, *operands = step(chain, [], [*first_near, outer, across, *to_pair, *over_middle])
    first_near, (outer, across, *packs) = operands[:2], operands[2:]
    outer_next = along_line(across, OUTWARD, OUTWARD)
    pairs = [to_pairs(pack) for pack in packs[: len(to_pair)]]
    middles = [to_middle(pack) for pack in packs[len(to_pair) :]]
    first_all = [first, *first_near, to_diagonal(first_near[0])]
    second = jnp.where(edge, outer, crossed)
    second_near = to_neighbours(second)

    chain, outer_next, second, *operands = step(chain, [], [outer_next, second, *second_near, *first_all])
    second_near, first_all = operands[:2], operands[2:]
    third = jnp.where(edge, outer_next, across)
    third_near = to_neighbours(third)
    second_all = [second, *second_near, to_diagonal(second_near[0])]
    third_all = [third, *third_near, to_diagonal(third_near[0])]
    first_all += other_core(first_all)
    second_all += other_core(second_all)
    chain, third_all[3], *operands = step(chain, [], [third_all[3], *pairs, *middles])
    pairs, middles = operands[: len(pairs)], operands[len(pairs) :]
    third_all += other_core(third_all)

    weights = [[out_weight], first_all, second_all, third_all]
    return worked([0, 1, 2, 3], stream, pairs, middles, weights, stream.dtype)


def whole_window(query_frames, key_frames, value_frames, stream, out_weight):
    rows, width = query_frames.shape
    heads = width // HEAD_SIZE
    position, members = lax.axis_index("ctx"), lax.axis_size("ctx")
    both = jnp.stack([key_frames, value_frames], 0)
    window = jnp.concatenate([passed_along(both, 1), both, passed_along(both, -1)], 1)
    valid = jnp.repeat(jnp.stack([position > 0, True, position < members - 1]), rows)
    query, key, value = (a.reshape(-1, heads, HEAD_SIZE) for a in (query_frames, window[0], window[1]))
    scores = jnp.einsum("qhd,khd->hqk", query, key, preferred_element_type=jnp.float32) * HEAD_SIZE ** (-0.5)
    probs = jax.nn.softmax(jnp.where(valid[None, None, :], scores, LOW), axis=2).astype(jnp.bfloat16)
    context = jnp.einsum("hqk,khd->qhd", probs, value, preferred_element_type=jnp.float32)
    context = context.astype(jnp.bfloat16).reshape(rows, width)
    weight = lax.all_gather(out_weight, "ctx", axis=0, tiled=True)
    product = jnp.dot(context, weight, preferred_element_type=jnp.float32)
    return (stream.astype(jnp.float32) + product).astype(stream.dtype)


def local(query_frames, key_frames, value_frames, stream, out_weight):
    lanes, members = lax.axis_size("dp"), lax.axis_size("ctx")
    width, columns = out_weight.shape
    arguments = (query_frames, key_frames, value_frames, stream, out_weight)
    fits = width % HEAD_SIZE == 0 and columns % (lanes * HEAD_SIZE) == 0
    if fits and members == LINE and lanes == LANES:
        return by_slots(*arguments)
    return whole_window(*arguments)


def solution(mesh):
    in_specs = (
        P(("dp", "ctx"), None),
        P(("dp", "ctx"), None),
        P(("dp", "ctx"), None),
        P(("dp", "ctx"), None),
        P("ctx", None),
    )
    out_specs = P(("dp", "ctx"), None)
    return jax.shard_map(local, mesh=mesh, in_specs=in_specs, out_specs=out_specs, check_vma=False)
```

time: 521 us -> 162 us (0.31)
  waiting for transfers between devices: 452 us -> 98.4 us
  matrix products: 33.5 us -> 0 us
  Pallas kernels: 0 us -> 26.3 us
  starting transfers between devices: 7.75 us -> 25.3 us
  between operations: 13.5 us -> 0.21 us
    all_gather x1 -> x0, waiting for transfers between devices: 301 us -> none  [local(): lax.all_gather(out_weight, 'ctx', axis=0, tiled=True)]
    ppermute x2 -> x28, waiting for transfers between devices: 151 us -> 98.4 us  [the longest x21 75 us: in_plane(): lax.ppermute(value, 'dp', [(lane, lane ^ masks[lane % 2]) for lane in ran...]
    pallas_call x0 -> x6, Pallas kernels: none -> 26.3 us  [the longest x1 21.2 us: worked_off(): pl.pallas_call(kernel, out_shape=jax.ShapeDtypeStruct(base.shape, dtype),...]
    dot_general x2 -> x0, matrix products: 22.9 us -> none  [the longest x1 13.5 us: local(): jnp.dot(context, lax.all_gather(out_weight, 'ctx', axis=0, tiled=True), p...]
    ppermute x2 -> x28, starting transfers between devices: 7.75 us -> 25.3 us  [the longest x7 12.7 us: along_line(): return lax.ppermute(value, ('dp', 'ctx'), pairs)]
    sub x1 -> x0, matrix products: 10.6 us -> none  [attend_window(): expon = jnp.exp(scores - largest)]
  transfers between devices with their start and end apart: 3 -> 28, of which waited for: 3 -> 16; matrix products, arithmetic and copies ran while one was open for 6% -> 2% of each run, Pallas kernels for 0% -> 3%
where the time goes in v2:
time: 162 us
  waiting for transfers between devices  98.4 us (61%)
  Pallas kernels  26.3 us (16%)
  starting transfers between devices  25.3 us (16%)
  local copies, waits for them, and re-layouts  8.27 us (5%)
  other arithmetic  3.14 us (2%)
    ppermute x21, waiting for transfers between devices, in_plane(): lax.ppermute(value, 'dp', [(lane, lane ^ masks[lane % 2]) for lane in ran...  75 us
    ppermute x7, waiting for transfers between devices, along_line(): return lax.ppermute(value, ('dp', 'ctx'), pairs)  23.3 us
    pallas_call x1, Pallas kernels, worked_off(): pl.pallas_call(kernel, out_shape=jax.ShapeDtypeStruct(base.shape, dtype),...  21.2 us
    ppermute x7, starting transfers between devices, along_line(): return lax.ppermute(value, ('dp', 'ctx'), pairs)  12.7 us
    ppermute x21, starting transfers between devices, in_plane(): lax.ppermute(value, 'dp', [(lane, lane ^ masks[lane % 2]) for lane in ran...  12.6 us
    unnamed x44, local copies, waits for them, and re-layouts  6.44 us
    pallas_call x1, Pallas kernels, packed(): pl.pallas_call(pack_kernel, out_shape=shapes, grid_spec=pltpu.PrefetchSca...  5.14 us
  transfers between devices with their start and end apart: 28, of which 16 were waited for; matrix products, arithmetic and copies ran while one was open for 2% of the time, Pallas kernels for 3%

profile of v2, /device:TPU:0, one launch (start us, length us, event | category | flops | bytes accessed | tf_op | source)
XLA Modules:
  0.0 161.6 jit_solution(15498963658966648174)
XLA Ops:
  0.0 1.2 constant_dynamic-slice_fusion
  1.2 3.1 %collective-permute-start = (bf16[640,640]{1,0:T(8,128)(2,1)S(1)}, bf16[640,640]{1,0:T(8,128)(2,1)S(1)}, u32[]{:S(2)}, u32[]{:S(2)}) collective-permute-start(bf16[640,640]{1,0:T(8,128)(2,1)S(1)} %constant_dynamic-slice_fusion), channel_id=1, source_target_pairs={{0,1},{1,0},{2,3},{3,2},{4,5},{5,4},{6,7},{7,6},{8,9},{9,8},{10,11... | collective-permute-start | bytes 2457608 | tf_op jit(solution)/shard_map/ppermute | solution.py:38
  6.3 5.1 %pack_window.1 = (f32[8,128]{1,0:T(8,128)}, bf16[512,2560]{1,0:T(8,128)(2,1)}, bf16[512,2560]{1,0:T(8,128)(2,1)}) custom-call(s32[21]{0:T(128)} %concatenate.3.place, bf16[256,2560]{1,0:T(8,128)(2,1)} %key_ref.3, bf16[256,2560]{1,0:T(8,128)(2,1)} %value_ref.3), custom_call_target="tpu_custom_call" | custom-call | tf_op jit(solution)/shard_map/pack_window/pallas_call | solution.py:105
  11.5 11.1 %collective-permute-done.refs_1_ = bf16[640,640]{1,0:T(8,128)(2,1)S(1)} collective-permute-done((bf16[640,640]{1,0:T(8,128)(2,1)S(1)}, bf16[640,640]{1,0:T(8,128)(2,1)S(1)}, u32[]{:S(2)}, u32[]{:S(2)}) %collective-permute-start) | collective-permute-done | bytes 819232 | tf_op jit(solution)/shard_map/ppermute | solution.py:38
  22.6 0.9 copy-done.1
  23.7 1.7 %collective-permute-start.2 = (bf16[640,640]{1,0:T(8,128)(2,1)}, bf16[640,640]{1,0:T(8,128)(2,1)S(1)}, u32[]{:S(2)}, u32[]{:S(2)}) collective-permute-start(bf16[640,640]{1,0:T(8,128)(2,1)} %get-tuple-element.32.refs_5_), channel_id=1, source_target_pairs={{0,8},{4,20},{8,0},{12,28},{16,24},{20,4},{24,16},{28,12},{1,9},{5... | collective-permute-start | bytes 2457608 | tf_op jit(solution)/shard_map/ppermute | solution.py:42
  25.4 1.5 collective-permute-start.3
  26.9 1.3 collective-permute-start.4
  28.9 15.5 %collective-permute-done.2.refs_1_ = bf16[640,640]{1,0:T(8,128)(2,1)S(1)} collective-permute-done((bf16[640,640]{1,0:T(8,128)(2,1)}, bf16[640,640]{1,0:T(8,128)(2,1)S(1)}, u32[]{:S(2)}, u32[]{:S(2)}) %collective-permute-start.2) | collective-permute-done | bytes 819232 | tf_op jit(solution)/shard_map/ppermute | solution.py:42
  44.5 5.0 %collective-permute-done.4.refs_3_ = bf16[640,640]{1,0:T(8,128)(2,1)S(1)} collective-permute-done((bf16[640,640]{1,0:T(8,128)(2,1)}, bf16[640,640]{1,0:T(8,128)(2,1)S(1)}, u32[]{:S(2)}, u32[]{:S(2)}) %collective-permute-start.4) | collective-permute-done | bytes 819232 | tf_op jit(solution)/shard_map/ppermute | solution.py:38
  49.5 0.9 copy-done.13
  50.7 1.1 copy-done.6
  51.9 1.2 broadcast_select_fusion.1.refs_2_
  54.2 1.3 collective-permute-start.6
  55.5 1.6 collective-permute-start.9
  57.1 3.5 %collective-permute-start.12 = (bf16[512,2560]{1,0:T(8,128)(2,1)}, bf16[512,2560]{1,0:T(8,128)(2,1)S(1)}, u32[]{:S(2)}, u32[]{:S(2)}) collective-permute-start(bf16[512,2560]{1,0:T(8,128)(2,1)} %get-tuple-element.43), channel_id=1, source_target_pairs={{0,1},{1,0},{2,3},{3,2},{4,5},{5,4},{6,7},{7,6},{8,9},{9,8},{10,11... | collective-permute-start | bytes 7864328 | tf_op jit(solution)/shard_map/ppermute | solution.py:38
  60.6 13.8 %collective-permute-done.7.refs_3_ = bf16[640,640]{1,0:T(8,128)(2,1)S(1)} collective-permute-done((bf16[640,640]{1,0:T(8,128)(2,1)S(1)}, bf16[640,640]{1,0:T(8,128)(2,1)S(1)}, u32[]{:S(2)}, u32[]{:S(2)}) %collective-permute-start.7) | collective-permute-done | bytes 819232 | tf_op jit(solution)/shard_map/ppermute | solution.py:42
  74.4 2.1 %collective-permute-start.13 = (bf16[512,2560]{1,0:T(8,128)(2,1)}, bf16[512,2560]{1,0:T(8,128)(2,1)}, u32[]{:S(2)}, u32[]{:S(2)}) collective-permute-start(bf16[512,2560]{1,0:T(8,128)(2,1)} %get-tuple-element.44), channel_id=1, source_target_pairs={{1,2},{2,1},{5,6},{6,5},{9,10},{10,9},{13,14},{14,13},{17,18},{18,... | collective-permute-start | bytes 7864328 | tf_op jit(solution)/shard_map/ppermute | solution.py:38
  76.5 1.1 collective-permute-done.6.refs_1_
  77.6 2.3 %collective-permute-done.9.refs_8_ = bf16[640,640]{1,0:T(8,128)(2,1)S(1)} collective-permute-done((bf16[640,640]{1,0:T(8,128)(2,1)}, bf16[640,640]{1,0:T(8,128)(2,1)S(1)}, u32[]{:S(2)}, u32[]{:S(2)}) %collective-permute-start.9) | collective-permute-done | bytes 819232 | tf_op jit(solution)/shard_map/ppermute | solution.py:42
  79.9 0.9 copy-done.11
  80.8 1.2 broadcast_select_fusion.refs_25_
  83.2 1.5 collective-permute-start.18
  84.7 18.0 %collective-permute-done.10.refs_26_ = bf16[640,640]{1,0:T(8,128)(2,1)S(1)} collective-permute-done((bf16[640,640]{1,0:T(8,128)(2,1)S(1)}, bf16[640,640]{1,0:T(8,128)(2,1)S(1)}, u32[]{:S(2)}, u32[]{:S(2)}) %collective-permute-start.10) | collective-permute-done | bytes 819232 | tf_op jit(solution)/shard_map/ppermute | solution.py:42
  103.6 7.8 %collective-permute-done.18.refs_20_ = bf16[640,640]{1,0:T(8,128)(2,1)S(1)} collective-permute-done((bf16[640,640]{1,0:T(8,128)(2,1)}, bf16[640,640]{1,0:T(8,128)(2,1)S(1)}, u32[]{:S(2)}, u32[]{:S(2)}) %collective-permute-start.18) | collective-permute-done | bytes 819232 | tf_op jit(solution)/shard_map/ppermute | solution.py:42
  111.4 1.5 collective-permute-start.11
  113.4 10.3 %collective-permute-done.11.refs_1_ = bf16[640,640]{1,0:T(8,128)(2,1)S(1)} collective-permute-done((bf16[640,640]{1,0:T(8,128)(2,1)S(1)}, bf16[640,640]{1,0:T(8,128)(2,1)S(1)}, u32[]{:S(2)}, u32[]{:S(2)}) %collective-permute-start.11) | collective-permute-done | bytes 819232 | tf_op jit(solution)/shard_map/ppermute | solution.py:42
  123.7 6.1 %collective-permute-done.12.refs_2_ = bf16[512,2560]{1,0:T(8,128)(2,1)S(1)} collective-permute-done((bf16[512,2560]{1,0:T(8,128)(2,1)}, bf16[512,2560]{1,0:T(8,128)(2,1)S(1)}, u32[]{:S(2)}, u32[]{:S(2)}) %collective-permute-start.12) | collective-permute-done | bytes 2621472 | tf_op jit(solution)/shard_map/ppermute | solution.py:38
  132.7 1.0 collective-permute-done.20.refs_22_
  134.8 2.3 %collective-permute-done.25.refs_30_ = bf16[640,640]{1,0:T(8,128)(2,1)S(1)} collective-permute-done((bf16[640,640]{1,0:T(8,128)(2,1)}, bf16[640,640]{1,0:T(8,128)(2,1)S(1)}, u32[]{:S(2)}, u32[]{:S(2)}) %collective-permute-start.25) | collective-permute-done | bytes 819232 | tf_op jit(solution)/shard_map/ppermute | solution.py:42
  137.2 2.3 %collective-permute-done.26.refs_31_ = bf16[640,640]{1,0:T(8,128)(2,1)S(1)} collective-permute-done((bf16[640,640]{1,0:T(8,128)(2,1)}, bf16[640,640]{1,0:T(8,128)(2,1)S(1)}, u32[]{:S(2)}, u32[]{:S(2)}) %collective-permute-start.26) | collective-permute-done | bytes 819232 | tf_op jit(solution)/shard_map/ppermute | solution.py:42
  140.4 21.2 %work_off_slots.1 = bf16[256,5120]{1,0:T(8,128)(2,1)} custom-call(s32[21]{0:T(128)} %concatenate.3.place, bf16[256,2560]{1,0:T(8,128)(2,1)} %query_ref.1, bf16[256,2560]{1,0:T(8,128)(2,1)} %key_ref.3, bf16[256,2560]{1,0:T(8,128)(2,1)} %value_ref.3, bf16[256,5120]{1,0:T(8,128)(2,1)} %base_ref.1, ...), custom_call_target="tpu_custom_call" | custom-call | flops 8724152320 | bytes 45875200 | tf_op jit(solution)/shard_map/work_off_slots/pallas_call | solution.py:205
  (79 shorter events, 11.7 us)
Async XLA Ops:
  1.2 21.3 %collective-permute-start = (bf16[640,640]{1,0:T(8,128)(2,1)S(1)}, bf16[640,640]{1,0:T(8,128)(2,1)S(1)}, u32[]{:S(2)}, u32[]{:S(2)}) collective-permute-start(bf16[640,640]{1,0:T(8,128)(2,1)S(1)} %constant_dynamic-slice_fusion), channel_id=1, source_target_pairs={{0,1},{1,0},{2,3},{3,2},{4,5},{5,4},{6,7},{7,6},{8,9},{9,8},{10,11... | collective-permute-start | bytes 2457608 | tf_op jit(solution)/shard_map/ppermute | solution.py:38
  4.3 18.2 %collective-permute-start.1 = (bf16[640,640]{1,0:T(8,128)(2,1)S(1)}, bf16[640,640]{1,0:T(8,128)(2,1)S(1)}, u32[]{:S(2)}, u32[]{:S(2)}) collective-permute-start(bf16[640,640]{1,0:T(8,128)(2,1)S(1)} %constant_dynamic-slice_fusion), channel_id=1, source_target_pairs={{1,2},{2,1},{5,6},{6,5},{9,10},{10,9},{13,14},{14,13},{17,18},{18,... | collective-permute-start | bytes 2457608 | tf_op jit(solution)/shard_map/ppermute | solution.py:38
  23.7 20.7 %collective-permute-start.2 = (bf16[640,640]{1,0:T(8,128)(2,1)}, bf16[640,640]{1,0:T(8,128)(2,1)S(1)}, u32[]{:S(2)}, u32[]{:S(2)}) collective-permute-start(bf16[640,640]{1,0:T(8,128)(2,1)} %get-tuple-element.32.refs_5_), channel_id=1, source_target_pairs={{0,8},{4,20},{8,0},{12,28},{16,24},{20,4},{24,16},{28,12},{1,9},{5... | collective-permute-start | bytes 2457608 | tf_op jit(solution)/shard_map/ppermute | solution.py:42
  25.4 19.1 %collective-permute-start.3 = (bf16[640,640]{1,0:T(8,128)(2,1)}, bf16[640,640]{1,0:T(8,128)(2,1)S(1)}, u32[]{:S(2)}, u32[]{:S(2)}) collective-permute-start(bf16[640,640]{1,0:T(8,128)(2,1)} %get-tuple-element.32.refs_5_), channel_id=1, source_target_pairs={{0,16},{4,12},{8,24},{12,4},{16,0},{20,28},{24,8},{28,20},{1,17},{... | collective-permute-start | bytes 2457608 | tf_op jit(solution)/shard_map/ppermute | solution.py:42
  26.9 22.6 %collective-permute-start.4 = (bf16[640,640]{1,0:T(8,128)(2,1)}, bf16[640,640]{1,0:T(8,128)(2,1)S(1)}, u32[]{:S(2)}, u32[]{:S(2)}) collective-permute-start(bf16[640,640]{1,0:T(8,128)(2,1)} %get-tuple-element.33), channel_id=1, source_target_pairs={{1,0},{2,3},{5,4},{6,7},{9,8},{10,11},{13,12},{14,15},{17,16},{18,... | collective-permute-start | bytes 2457608 | tf_op jit(solution)/shard_map/ppermute | solution.py:38
  28.2 21.3 %collective-permute-start.5 = (bf16[640,640]{1,0:T(8,128)(2,1)}, bf16[640,640]{1,0:T(8,128)(2,1)S(1)}, u32[]{:S(2)}, u32[]{:S(2)}) collective-permute-start(bf16[640,640]{1,0:T(8,128)(2,1)} %get-tuple-element.32.refs_5_), channel_id=1, source_target_pairs={{1,2},{2,1},{5,6},{6,5},{9,10},{10,9},{13,14},{14,13},{17,18},{18,... | collective-permute-start | bytes 2457608 | tf_op jit(solution)/shard_map/ppermute | solution.py:38
  53.1 27.7 %copy-start.2 = (bf16[640,640]{1,0:T(8,128)(2,1)}, bf16[640,640]{1,0:T(8,128)(2,1)S(1)}, u32[]{:S(2)}) copy-start(bf16[640,640]{1,0:T(8,128)(2,1)S(1)} %broadcast_select_fusion.1.refs_2_) | copy-start | bytes 2457604
  53.1 21.2 %collective-permute-start.7 = (bf16[640,640]{1,0:T(8,128)(2,1)S(1)}, bf16[640,640]{1,0:T(8,128)(2,1)S(1)}, u32[]{:S(2)}, u32[]{:S(2)}) collective-permute-start(bf16[640,640]{1,0:T(8,128)(2,1)S(1)} %broadcast_select_fusion.1.refs_2_), channel_id=1, source_target_pairs={{0,8},{4,20},{8,0},{12,28},{16,24},{20,4},{24,16},{28,12},{1,9},{5... | collective-permute-start | bytes 2457608 | tf_op jit(solution)/shard_map/ppermute | solution.py:42
  53.7 22.8 %collective-permute-start.8 = (bf16[640,640]{1,0:T(8,128)(2,1)S(1)}, bf16[640,640]{1,0:T(8,128)(2,1)S(1)}, u32[]{:S(2)}, u32[]{:S(2)}) collective-permute-start(bf16[640,640]{1,0:T(8,128)(2,1)S(1)} %broadcast_select_fusion.1.refs_2_), channel_id=1, source_target_pairs={{0,16},{4,12},{8,24},{12,4},{16,0},{20,28},{24,8},{28,20},{1,17},{... | collective-permute-start | bytes 2457608 | tf_op jit(solution)/shard_map/ppermute | solution.py:42
  54.2 23.4 %collective-permute-start.6 = (bf16[640,640]{1,0:T(8,128)(2,1)}, bf16[640,640]{1,0:T(8,128)(2,1)}, u32[]{:S(2)}, u32[]{:S(2)}) collective-permute-start(bf16[640,640]{1,0:T(8,128)(2,1)} %get-tuple-element.37), channel_id=1, source_target_pairs={{1,0},{2,3},{5,4},{6,7},{9,8},{10,11},{13,12},{14,15},{17,16},{18,... | collective-permute-start | bytes 2457608 | tf_op jit(solution)/shard_map/ppermute | solution.py:38
  55.5 24.4 %collective-permute-start.9 = (bf16[640,640]{1,0:T(8,128)(2,1)}, bf16[640,640]{1,0:T(8,128)(2,1)S(1)}, u32[]{:S(2)}, u32[]{:S(2)}) collective-permute-start(bf16[640,640]{1,0:T(8,128)(2,1)} %get-tuple-element.39.refs_6_), channel_id=1, source_target_pairs={{0,16},{4,12},{8,24},{12,4},{16,0},{20,28},{24,8},{28,20},{1,17},{... | collective-permute-start | bytes 2457608 | tf_op jit(solution)/shard_map/ppermute | solution.py:42
  57.1 72.7 %collective-permute-start.12 = (bf16[512,2560]{1,0:T(8,128)(2,1)}, bf16[512,2560]{1,0:T(8,128)(2,1)S(1)}, u32[]{:S(2)}, u32[]{:S(2)}) collective-permute-start(bf16[512,2560]{1,0:T(8,128)(2,1)} %get-tuple-element.43), channel_id=1, source_target_pairs={{0,1},{1,0},{2,3},{3,2},{4,5},{5,4},{6,7},{7,6},{8,9},{9,8},{10,11... | collective-permute-start | bytes 7864328 | tf_op jit(solution)/shard_map/ppermute | solution.py:38
  74.4 55.6 %collective-permute-start.13 = (bf16[512,2560]{1,0:T(8,128)(2,1)}, bf16[512,2560]{1,0:T(8,128)(2,1)}, u32[]{:S(2)}, u32[]{:S(2)}) collective-permute-start(bf16[512,2560]{1,0:T(8,128)(2,1)} %get-tuple-element.44), channel_id=1, source_target_pairs={{1,2},{2,1},{5,6},{6,5},{9,10},{10,9},{13,14},{14,13},{17,18},{18,... | collective-permute-start | bytes 7864328 | tf_op jit(solution)/shard_map/ppermute | solution.py:38
  82.0 57.6 %copy-start.7 = (bf16[640,640]{1,0:T(8,128)(2,1)}, bf16[640,640]{1,0:T(8,128)(2,1)S(1)}, u32[]{:S(2)}) copy-start(bf16[640,640]{1,0:T(8,128)(2,1)S(1)} %broadcast_select_fusion.refs_25_) | copy-start | bytes 2457604
  82.0 20.6 %collective-permute-start.10 = (bf16[640,640]{1,0:T(8,128)(2,1)S(1)}, bf16[640,640]{1,0:T(8,128)(2,1)S(1)}, u32[]{:S(2)}, u32[]{:S(2)}) collective-permute-start(bf16[640,640]{1,0:T(8,128)(2,1)S(1)} %broadcast_select_fusion.refs_25_), channel_id=1, source_target_pairs={{0,8},{4,20},{8,0},{12,28},{16,24},{20,4},{24,16},{28,12},{1,9},{5... | collective-permute-start | bytes 2457608 | tf_op jit(solution)/shard_map/ppermute | solution.py:42
  82.7 20.0 %collective-permute-start.23 = (bf16[640,640]{1,0:T(8,128)(2,1)S(1)}, bf16[640,640]{1,0:T(8,128)(2,1)S(1)}, u32[]{:S(2)}, u32[]{:S(2)}) collective-permute-start(bf16[640,640]{1,0:T(8,128)(2,1)S(1)} %broadcast_select_fusion.refs_25_), channel_id=1, source_target_pairs={{0,16},{4,12},{8,24},{12,4},{16,0},{20,28},{24,8},{28,20},{1,17},{... | collective-permute-start | bytes 2457608 | tf_op jit(solution)/shard_map/ppermute | solution.py:42
  83.2 28.2 %collective-permute-start.18 = (bf16[640,640]{1,0:T(8,128)(2,1)}, bf16[640,640]{1,0:T(8,128)(2,1)S(1)}, u32[]{:S(2)}, u32[]{:S(2)}) collective-permute-start(bf16[640,640]{1,0:T(8,128)(2,1)} %get-tuple-element.52.refs_18_), channel_id=1, source_target_pairs={{0,16},{4,12},{8,24},{12,4},{16,0},{20,28},{24,8},{28,20},{1,17},{... | collective-permute-start | bytes 2457608 | tf_op jit(solution)/shard_map/ppermute | solution.py:42
  102.7 27.2 %copy-start.14 = (bf16[640,640]{1,0:T(8,128)(2,1)}, bf16[640,640]{1,0:T(8,128)(2,1)S(1)}, u32[]{:S(2)}) copy-start(bf16[640,640]{1,0:T(8,128)(2,1)S(1)} %collective-permute-done.10.refs_26_) | copy-start | bytes 2457604
  102.7 10.2 %collective-permute-start.24 = (bf16[640,640]{1,0:T(8,128)(2,1)S(1)}, bf16[640,640]{1,0:T(8,128)(2,1)S(1)}, u32[]{:S(2)}, u32[]{:S(2)}) collective-permute-start(bf16[640,640]{1,0:T(8,128)(2,1)S(1)} %broadcast_select_fusion.refs_25_), channel_id=1, source_target_pairs={{0,4},{4,0},{8,12},{12,8},{16,20},{20,16},{24,28},{28,24},{1,5},{5... | collective-permute-start | bytes 2457608 | tf_op jit(solution)/shard_map/ppermute | solution.py:42
  102.7 10.2 %collective-permute-start.14 = (bf16[640,640]{1,0:T(8,128)(2,1)}, bf16[640,640]{1,0:T(8,128)(2,1)S(1)}, u32[]{:S(2)}, u32[]{:S(2)}) collective-permute-start(bf16[640,640]{1,0:T(8,128)(2,1)} %get-tuple-element.47.refs_9_), channel_id=1, source_target_pairs={{0,4},{4,0},{8,12},{12,8},{16,20},{20,16},{24,28},{28,24},{1,5},{5... | collective-permute-start | bytes 2457608 | tf_op jit(solution)/shard_map/ppermute | solution.py:42
  111.4 18.6 %copy-start.16 = (bf16[640,640]{1,0:T(8,128)(2,1)}, bf16[640,640]{1,0:T(8,128)(2,1)S(1)}, u32[]{:S(2)}) copy-start(bf16[640,640]{1,0:T(8,128)(2,1)S(1)} %collective-permute-done.18.refs_20_) | copy-start | bytes 2457604
  111.4 12.3 %collective-permute-start.11 = (bf16[640,640]{1,0:T(8,128)(2,1)S(1)}, bf16[640,640]{1,0:T(8,128)(2,1)S(1)}, u32[]{:S(2)}, u32[]{:S(2)}) collective-permute-start(bf16[640,640]{1,0:T(8,128)(2,1)S(1)} %collective-permute-done.10.refs_26_), channel_id=1, source_target_pairs={{0,16},{4,12},{8,24},{12,4},{16,0},{20,28},{24,8},{28,20},{1,17},{... | collective-permute-start | bytes 2457608 | tf_op jit(solution)/shard_map/ppermute | solution.py:42
  112.9 18.5 %collective-permute-start.15 = (bf16[640,640]{1,0:T(8,128)(2,1)}, bf16[640,640]{1,0:T(8,128)(2,1)}, u32[]{:S(2)}, u32[]{:S(2)}) collective-permute-start(bf16[640,640]{1,0:T(8,128)(2,1)} %get-tuple-element.48.refs_10_), channel_id=1, source_target_pairs={{0,4},{4,0},{8,12},{12,8},{16,20},{20,16},{24,28},{28,24},{1,5},{5... | collective-permute-start | bytes 2457608 | tf_op jit(solution)/shard_map/ppermute | solution.py:42
  112.9 18.5 %collective-permute-start.16 = (bf16[640,640]{1,0:T(8,128)(2,1)}, bf16[640,640]{1,0:T(8,128)(2,1)}, u32[]{:S(2)}, u32[]{:S(2)}) collective-permute-start(bf16[640,640]{1,0:T(8,128)(2,1)} %get-tuple-element.49.refs_11_), channel_id=1, source_target_pairs={{0,4},{4,0},{8,12},{12,8},{16,20},{20,16},{24,28},{28,24},{1,5},{5... | collective-permute-start | bytes 2457608 | tf_op jit(solution)/shard_map/ppermute | solution.py:42
  123.7 8.2 %collective-permute-start.17 = (bf16[640,640]{1,0:T(8,128)(2,1)}, bf16[640,640]{1,0:T(8,128)(2,1)}, u32[]{:S(2)}, u32[]{:S(2)}) collective-permute-start(bf16[640,640]{1,0:T(8,128)(2,1)} %get-tuple-element.50.refs_12_), channel_id=1, source_target_pairs={{0,4},{4,0},{8,12},{12,8},{16,20},{20,16},{24,28},{28,24},{1,5},{5... | collective-permute-start | bytes 2457608 | tf_op jit(solution)/shard_map/ppermute | solution.py:42
  129.9 2.7 %collective-permute-start.19 = (bf16[640,640]{1,0:T(8,128)(2,1)}, bf16[640,640]{1,0:T(8,128)(2,1)}, u32[]{:S(2)}, u32[]{:S(2)}) collective-permute-start(bf16[640,640]{1,0:T(8,128)(2,1)} %get-tuple-element.51.refs_17_), channel_id=1, source_target_pairs={{0,4},{4,0},{8,12},{12,8},{16,20},{20,16},{24,28},{28,24},{1,5},{5... | collective-permute-start | bytes 2457608 | tf_op jit(solution)/shard_map/ppermute | solution.py:42
  130.0 3.8 %collective-permute-start.20 = (bf16[640,640]{1,0:T(8,128)(2,1)}, bf16[640,640]{1,0:T(8,128)(2,1)}, u32[]{:S(2)}, u32[]{:S(2)}) collective-permute-start(bf16[640,640]{1,0:T(8,128)(2,1)} %get-tuple-element.52.refs_18_), channel_id=1, source_target_pairs={{0,4},{4,0},{8,12},{12,8},{16,20},{20,16},{24,28},{28,24},{1,5},{5... | collective-permute-start | bytes 2457608 | tf_op jit(solution)/shard_map/ppermute | solution.py:42
  131.4 3.4 %collective-permute-start.21 = (bf16[640,640]{1,0:T(8,128)(2,1)}, bf16[640,640]{1,0:T(8,128)(2,1)S(1)}, u32[]{:S(2)}, u32[]{:S(2)}) collective-permute-start(bf16[640,640]{1,0:T(8,128)(2,1)} %get-tuple-element.53.refs_19_), channel_id=1, source_target_pairs={{0,4},{4,0},{8,12},{12,8},{16,20},{20,16},{24,28},{28,24},{1,5},{5... | collective-permute-start | bytes 2457608 | tf_op jit(solution)/shard_map/ppermute | solution.py:42
  131.4 5.7 %collective-permute-start.25 = (bf16[640,640]{1,0:T(8,128)(2,1)}, bf16[640,640]{1,0:T(8,128)(2,1)S(1)}, u32[]{:S(2)}, u32[]{:S(2)}) collective-permute-start(bf16[640,640]{1,0:T(8,128)(2,1)} %copy-done.14), channel_id=1, source_target_pairs={{0,4},{4,0},{8,12},{12,8},{16,20},{20,16},{24,28},{28,24},{1,5},{5... | collective-permute-start | bytes 2457608 | tf_op jit(solution)/shard_map/ppermute | solution.py:42
  131.9 7.6 %collective-permute-start.26 = (bf16[640,640]{1,0:T(8,128)(2,1)}, bf16[640,640]{1,0:T(8,128)(2,1)S(1)}, u32[]{:S(2)}, u32[]{:S(2)}) collective-permute-start(bf16[640,640]{1,0:T(8,128)(2,1)} %copy-done.15), channel_id=1, source_target_pairs={{0,4},{4,0},{8,12},{12,8},{16,20},{20,16},{24,28},{28,24},{1,5},{5... | collective-permute-start | bytes 2457608 | tf_op jit(solution)/shard_map/ppermute | solution.py:42
  132.6 6.9 %collective-permute-start.22 = (bf16[640,640]{1,0:T(8,128)(2,1)}, bf16[640,640]{1,0:T(8,128)(2,1)}, u32[]{:S(2)}, u32[]{:S(2)}) collective-permute-start(bf16[640,640]{1,0:T(8,128)(2,1)} %copy-done.16), channel_id=1, source_target_pairs={{0,4},{4,0},{8,12},{12,8},{16,20},{20,16},{24,28},{28,24},{1,5},{5... | collective-permute-start | bytes 2457608 | tf_op jit(solution)/shard_map/ppermute | solution.py:42
  133.8 5.9 %collective-permute-start.27 = (bf16[640,640]{1,0:T(8,128)(2,1)}, bf16[640,640]{1,0:T(8,128)(2,1)}, u32[]{:S(2)}, u32[]{:S(2)}) collective-permute-start(bf16[640,640]{1,0:T(8,128)(2,1)} %get-tuple-element.54.refs_28_), channel_id=1, source_target_pairs={{0,4},{4,0},{8,12},{12,8},{16,20},{20,16},{24,28},{28,24},{1,5},{5... | collective-permute-start | bytes 2457608 | tf_op jit(solution)/shard_map/ppermute | solution.py:42
  (18 other events, 73.0 us)

commit v3 on v2

--- a/solution.py
+++ b/solution.py
@@ -12,7 +12,7 @@
 LOW = -1e30
 MIB = 1024 * 1024
 VMEM_MIB = 60
-PAIR_SLOTS, MIDDLE_SLOTS = (4,), (4,)
+PAIR_SLOTS, MIDDLE_SLOTS = (3, 1), (3, 1)
 LINE = 4
 LANES = 8
 VMEM = pl.BlockSpec(memory_space=pltpu.VMEM)
@@ -274,29 +274,35 @@
     outer, across = along_line(crossed, OUTWARD, OUTWARD), to_middle(first)
     first_near = to_neighbours(first)
 
-    chain, *operands = step(chain, [], [*first_near, outer, across, *to_pair, *over_middle])
+    operands = [*first_near, outer, across, to_pair[0], over_middle[0]]
+    chain, *operands = step(chain, [], operands)
     first_near, (outer, across, *packs) = operands[:2], operands[2:]
     outer_next = along_line(across, OUTWARD, OUTWARD)
-    pairs = [to_pairs(pack) for pack in packs[: len(to_pair)]]
-    middles = [to_middle(pack) for pack in packs[len(to_pair) :]]
+    pairs, middles = [to_pairs(packs[0])], [to_middle(packs[1])]
     first_all = [first, *first_near, to_diagonal(first_near[0])]
     second = jnp.where(edge, outer, crossed)
     second_near = to_neighbours(second)
 
-    chain, outer_next, second, *operands = step(chain, [], [outer_next, second, *second_near, *first_all])
+    operands = [outer_next, second, *second_near, *first_all]
+    chain, *operands = step(chain, [], operands)
+    outer_next, second, *operands = operands
     second_near, first_all = operands[:2], operands[2:]
     third = jnp.where(edge, outer_next, across)
     third_near = to_neighbours(third)
     second_all = [second, *second_near, to_diagonal(second_near[0])]
     third_all = [third, *third_near, to_diagonal(third_near[0])]
     first_all += other_core(first_all)
+    operands = [pairs[0], middles[0], to_pair[1], over_middle[1], *second_all]
+    chain, pairs[0], middles[0], pair_pack, pack, *second_all = step(chain, third_near, operands)
+    pairs.append(to_pairs(pair_pack))
+    middles.append(to_middle(pack))
     second_all += other_core(second_all)
-    chain, third_all[3], *operands = step(chain, [], [third_all[3], *pairs, *middles])
-    pairs, middles = operands[: len(pairs)], operands[len(pairs) :]
+    sums = worked([0, 1, 2], stream, pairs, middles, [[out_weight], first_all, second_all], jnp.float32)
+
+    tokens = []
+    chain, sums, pairs[1], middles[1], third_all[3] = step(chain, tokens, [sums, pairs[1], middles[1], third_all[3]])
     third_all += other_core(third_all)
-
-    weights = [[out_weight], first_all, second_all, third_all]
-    return worked([0, 1, 2, 3], stream, pairs, middles, weights, stream.dtype)
+    return worked([3], sums, pairs, middles, [third_all], stream.dtype)
 
 
 def whole_window(query_frames, key_frames, value_frames, stream, out_weight):

time: 162 us -> 157 us (0.969)
  waiting for transfers between devices: 98.4 us -> 87.6 us
  Pallas kernels: 26.3 us -> 31.3 us
    ppermute x21, waiting for transfers between devices: 75 us -> 63.1 us  [in_plane(): lax.ppermute(value, 'dp', [(lane, lane ^ masks[lane % 2]) for lane in ran...]
    pallas_call x1 -> x2, Pallas kernels: 21.2 us -> 26.1 us  [worked_off(): pl.pallas_call(kernel, out_shape=jax.ShapeDtypeStruct(base.shape, dtype),...]
    ppermute x7 -> x9, waiting for transfers between devices: 23.3 us -> 24.5 us  [along_line(): return lax.ppermute(value, ('dp', 'ctx'), pairs)]
    unnamed x44 -> x46, local copies, waits for them, and re-layouts: 6.44 us -> 5.81 us
    ppermute x7 -> x9, starting transfers between devices: 12.7 us -> 12.6 us  [along_line(): return lax.ppermute(value, ('dp', 'ctx'), pairs)]
  transfers between devices with their start and end apart: 28 -> 30, of which waited for: 16 -> 15; matrix products, arithmetic and copies ran while one was open for 2% -> 2% of each run, Pallas kernels for 3% -> 14%
where the time goes in v3:
time: 157 us; the launch traced here: 156 us
  waiting for transfers between devices  87.6 us (56%)
  Pallas kernels  31.3 us (20%)
  starting transfers between devices  25.9 us (16%)
  local copies, waits for them, and re-layouts  7.7 us (5%)
  other arithmetic  3.3 us (2%)
    ppermute x21, waiting for transfers between devices, in_plane(): lax.ppermute(value, 'dp', [(lane, lane ^ masks[lane % 2]) for lane in ran...  63.1 us
    pallas_call x2, Pallas kernels, worked_off(): pl.pallas_call(kernel, out_shape=jax.ShapeDtypeStruct(base.shape, dtype),...  26.1 us
    ppermute x9, waiting for transfers between devices, along_line(): return lax.ppermute(value, ('dp', 'ctx'), pairs)  24.5 us
    ppermute x21, starting transfers between devices, in_plane(): lax.ppermute(value, 'dp', [(lane, lane ^ masks[lane % 2]) for lane in ran...  13.3 us
    ppermute x9, starting transfers between devices, along_line(): return lax.ppermute(value, ('dp', 'ctx'), pairs)  12.6 us
    unnamed x46, local copies, waits for them, and re-layouts  5.81 us
    pallas_call x1, Pallas kernels, packed(): pl.pallas_call(pack_kernel, out_shape=shapes, grid_spec=pltpu.PrefetchSca...  5.12 us
  transfers between devices with their start and end apart: 30, of which 15 were waited for; matrix products, arithmetic and copies ran while one was open for 2% of the time, Pallas kernels for 14%

profile of v3, /device:TPU:0, one launch (start us, length us, event | category | flops | bytes accessed | tf_op | source)
XLA Modules:
  0.0 156.1 jit_solution(13165140116934034298)
XLA Ops:
  0.0 1.2 constant_dynamic-slice_fusion
  1.2 3.1 %collective-permute-start = (bf16[640,640]{1,0:T(8,128)(2,1)S(1)}, bf16[640,640]{1,0:T(8,128)(2,1)}, u32[]{:S(2)}, u32[]{:S(2)}) collective-permute-start(bf16[640,640]{1,0:T(8,128)(2,1)S(1)} %constant_dynamic-slice_fusion), channel_id=1, source_target_pairs={{0,1},{1,0},{2,3},{3,2},{4,5},{5,4},{6,7},{7,6},{8,9},{9,8},{10,11... | collective-permute-start | bytes 2457608 | tf_op jit(solution)/shard_map/ppermute | solution.py:38
  6.4 5.1 %pack_window.1 = (f32[8,128]{1,0:T(8,128)}, bf16[512,1920]{1,0:T(8,128)(2,1)}, bf16[512,640]{1,0:T(8,128)(2,1)}, bf16[512,1920]{1,0:T(8,128)(2,1)}, bf16[512,640]{1,0:T(8,128)(2,1)}) custom-call(s32[21]{0:T(128)} %concatenate.3.place, bf16[256,2560]{1,0:T(8,128)(2,1)} %key_ref.5, bf16[256,2560]{1,0:T(8,128)(2,1)} %value_ref.5), custom_call_target="tpu_custom_call" | custom-call | tf_op jit(solution)/shard_map/pack_window/pallas_call | solution.py:105
  11.5 11.1 %collective-permute-done.refs_1_ = bf16[640,640]{1,0:T(8,128)(2,1)} collective-permute-done((bf16[640,640]{1,0:T(8,128)(2,1)S(1)}, bf16[640,640]{1,0:T(8,128)(2,1)}, u32[]{:S(2)}, u32[]{:S(2)}) %collective-permute-start) | collective-permute-done | bytes 819232 | tf_op jit(solution)/shard_map/ppermute | solution.py:38
  22.7 0.9 copy-done.8
  23.6 1.7 %collective-permute-start.2 = (bf16[640,640]{1,0:T(8,128)(2,1)}, bf16[640,640]{1,0:T(8,128)(2,1)}, u32[]{:S(2)}, u32[]{:S(2)}) collective-permute-start(bf16[640,640]{1,0:T(8,128)(2,1)} %get-tuple-element.44.refs_5_), channel_id=1, source_target_pairs={{0,8},{4,20},{8,0},{12,28},{16,24},{20,4},{24,16},{28,12},{1,9},{5... | collective-permute-start | bytes 2457608 | tf_op jit(solution)/shard_map/ppermute | solution.py:42
  25.2 1.5 collective-permute-start.3
  27.5 1.3 collective-permute-start.4
  28.8 15.6 %collective-permute-done.2.refs_1_ = bf16[640,640]{1,0:T(8,128)(2,1)} collective-permute-done((bf16[640,640]{1,0:T(8,128)(2,1)}, bf16[640,640]{1,0:T(8,128)(2,1)}, u32[]{:S(2)}, u32[]{:S(2)}) %collective-permute-start.2) | collective-permute-done | bytes 819232 | tf_op jit(solution)/shard_map/ppermute | solution.py:42
  44.4 8.2 %collective-permute-done.4.refs_3_ = bf16[640,640]{1,0:T(8,128)(2,1)S(1)} collective-permute-done((bf16[640,640]{1,0:T(8,128)(2,1)}, bf16[640,640]{1,0:T(8,128)(2,1)S(1)}, u32[]{:S(2)}, u32[]{:S(2)}) %collective-permute-start.4) | collective-permute-done | bytes 819232 | tf_op jit(solution)/shard_map/ppermute | solution.py:38
  52.6 0.9 copy-done.7
  53.5 1.3 broadcast_select_fusion.1.refs_2_
  55.9 1.3 collective-permute-start.6
  57.2 1.6 %collective-permute-start.9 = (bf16[640,640]{1,0:T(8,128)(2,1)}, bf16[640,640]{1,0:T(8,128)(2,1)}, u32[]{:S(2)}, u32[]{:S(2)}) collective-permute-start(bf16[640,640]{1,0:T(8,128)(2,1)} %get-tuple-element.51.refs_6_), channel_id=1, source_target_pairs={{0,16},{4,12},{8,24},{12,4},{16,0},{20,28},{24,8},{28,20},{1,17},{... | collective-permute-start | bytes 2457608 | tf_op jit(solution)/shard_map/ppermute | solution.py:42
  58.8 2.7 %collective-permute-start.10 = (bf16[512,1920]{1,0:T(8,128)(2,1)}, bf16[512,1920]{1,0:T(8,128)(2,1)S(1)}, u32[]{:S(2)}, u32[]{:S(2)}) collective-permute-start(bf16[512,1920]{1,0:T(8,128)(2,1)} %get-tuple-element.54), channel_id=1, source_target_pairs={{0,1},{1,0},{2,3},{3,2},{4,5},{5,4},{6,7},{7,6},{8,9},{9,8},{10,11... | collective-permute-start | bytes 5898248 | tf_op jit(solution)/shard_map/ppermute | solution.py:38
  61.5 14.6 %collective-permute-done.7.refs_3_ = bf16[640,640]{1,0:T(8,128)(2,1)S(1)} collective-permute-done((bf16[640,640]{1,0:T(8,128)(2,1)S(1)}, bf16[640,640]{1,0:T(8,128)(2,1)S(1)}, u32[]{:S(2)}, u32[]{:S(2)}) %collective-permute-start.7) | collective-permute-done | bytes 819232 | tf_op jit(solution)/shard_map/ppermute | solution.py:42
  76.1 1.9 %collective-permute-start.11 = (bf16[512,1920]{1,0:T(8,128)(2,1)}, bf16[512,1920]{1,0:T(8,128)(2,1)}, u32[]{:S(2)}, u32[]{:S(2)}) collective-permute-start(bf16[512,1920]{1,0:T(8,128)(2,1)} %get-tuple-element.55), channel_id=1, source_target_pairs={{1,2},{2,1},{5,6},{6,5},{9,10},{10,9},{13,14},{14,13},{17,18},{18,... | collective-permute-start | bytes 5898248 | tf_op jit(solution)/shard_map/ppermute | solution.py:38
  78.0 1.0 collective-permute-done.6.refs_1_
  79.0 2.1 %collective-permute-done.9.refs_8_ = bf16[640,640]{1,0:T(8,128)(2,1)} collective-permute-done((bf16[640,640]{1,0:T(8,128)(2,1)}, bf16[640,640]{1,0:T(8,128)(2,1)}, u32[]{:S(2)}, u32[]{:S(2)}) %collective-permute-start.9) | collective-permute-done | bytes 819232 | tf_op jit(solution)/shard_map/ppermute | solution.py:42
  81.1 1.3 broadcast_select_fusion.refs_2_
  83.0 1.3 collective-permute-start.14
  85.0 18.1 %collective-permute-done.13.refs_9_.refs_3_ = bf16[640,640]{1,0:T(8,128)(2,1)S(1)} collective-permute-done((bf16[640,640]{1,0:T(8,128)(2,1)S(1)}, bf16[640,640]{1,0:T(8,128)(2,1)S(1)}, u32[]{:S(2)}, u32[]{:S(2)}) %collective-permute-start.13) | collective-permute-done | bytes 819232 | tf_op jit(solution)/shard_map/ppermute | solution.py:42
  103.7 7.9 %collective-permute-done.12.refs_8_ = bf16[640,640]{1,0:T(8,128)(2,1)S(1)} collective-permute-done((bf16[640,640]{1,0:T(8,128)(2,1)S(1)}, bf16[640,640]{1,0:T(8,128)(2,1)S(1)}, u32[]{:S(2)}, u32[]{:S(2)}) %collective-permute-start.12) | collective-permute-done | bytes 819232 | tf_op jit(solution)/shard_map/ppermute | solution.py:42
  112.5 4.2 %collective-permute-done.10.refs_1_ = bf16[512,1920]{1,0:T(8,128)(2,1)S(1)} collective-permute-done((bf16[512,1920]{1,0:T(8,128)(2,1)}, bf16[512,1920]{1,0:T(8,128)(2,1)S(1)}, u32[]{:S(2)}, u32[]{:S(2)}) %collective-permute-start.10) | collective-permute-done | bytes 1966112 | tf_op jit(solution)/shard_map/ppermute | solution.py:38
  116.8 1.2 copy-done
  119.4 1.5 collective-permute-start.25
  123.0 1.0 collective-permute-done.22.refs_22_
  124.9 17.2 %work_off_slots.2.refs_1_ = f32[256,5120]{1,0:T(8,128)} custom-call(s32[21]{0:T(128)} %concatenate.3.place, bf16[256,2560]{1,0:T(8,128)(2,1)} %query_ref.3, bf16[256,2560]{1,0:T(8,128)(2,1)} %key_ref.5, bf16[256,2560]{1,0:T(8,128)(2,1)} %value_ref.5, bf16[256,5120]{1,0:T(8,128)(2,1)} %base_ref.1, ...), custom_call_target="tpu_custom_call" | custom-call | flops 6543114240 | bytes 37027840 | tf_op jit(solution)/shard_map/work_off_slots/pallas_call | solution.py:205
  143.8 0.9 collective-permute-done.28.refs_8_
  144.7 1.4 collective-permute-done.29.refs_9_
  146.0 0.9 copy-done.22
  147.0 8.9 %work_off_slots.3 = bf16[256,5120]{1,0:T(8,128)(2,1)} custom-call(s32[21]{0:T(128)} %concatenate.3.place, bf16[256,2560]{1,0:T(8,128)(2,1)} %query_ref.3, bf16[256,2560]{1,0:T(8,128)(2,1)} %key_ref.5, bf16[256,2560]{1,0:T(8,128)(2,1)} %value_ref.5, f32[256,5120]{1,0:T(8,128)} %get-tuple-element.75.base_ref, bf16[512,640]{1,0:T(8,128)(2,1)} %get-tuple-element.76.refs_0_, ...), custom_call_target="tpu_custom_call" | custom-call | flops 2181038080 | bytes 19333120 | tf_op jit(solution)/shard_map/work_off_slots/pallas_call | solution.py:205
  (87 shorter events, 12.8 us)
Async XLA Ops:
  1.2 21.4 %collective-permute-start = (bf16[640,640]{1,0:T(8,128)(2,1)S(1)}, bf16[640,640]{1,0:T(8,128)(2,1)}, u32[]{:S(2)}, u32[]{:S(2)}) collective-permute-start(bf16[640,640]{1,0:T(8,128)(2,1)S(1)} %constant_dynamic-slice_fusion), channel_id=1, source_target_pairs={{0,1},{1,0},{2,3},{3,2},{4,5},{5,4},{6,7},{7,6},{8,9},{9,8},{10,11... | collective-permute-start | bytes 2457608 | tf_op jit(solution)/shard_map/ppermute | solution.py:38
  4.3 18.4 %collective-permute-start.1 = (bf16[640,640]{1,0:T(8,128)(2,1)S(1)}, bf16[640,640]{1,0:T(8,128)(2,1)S(1)}, u32[]{:S(2)}, u32[]{:S(2)}) collective-permute-start(bf16[640,640]{1,0:T(8,128)(2,1)S(1)} %constant_dynamic-slice_fusion), channel_id=1, source_target_pairs={{1,2},{2,1},{5,6},{6,5},{9,10},{10,9},{13,14},{14,13},{17,18},{18,... | collective-permute-start | bytes 2457608 | tf_op jit(solution)/shard_map/ppermute | solution.py:38
  23.6 20.8 %collective-permute-start.2 = (bf16[640,640]{1,0:T(8,128)(2,1)}, bf16[640,640]{1,0:T(8,128)(2,1)}, u32[]{:S(2)}, u32[]{:S(2)}) collective-permute-start(bf16[640,640]{1,0:T(8,128)(2,1)} %get-tuple-element.44.refs_5_), channel_id=1, source_target_pairs={{0,8},{4,20},{8,0},{12,28},{16,24},{20,4},{24,16},{28,12},{1,9},{5... | collective-permute-start | bytes 2457608 | tf_op jit(solution)/shard_map/ppermute | solution.py:42
  25.2 19.2 %collective-permute-start.3 = (bf16[640,640]{1,0:T(8,128)(2,1)}, bf16[640,640]{1,0:T(8,128)(2,1)}, u32[]{:S(2)}, u32[]{:S(2)}) collective-permute-start(bf16[640,640]{1,0:T(8,128)(2,1)} %get-tuple-element.44.refs_5_), channel_id=1, source_target_pairs={{0,16},{4,12},{8,24},{12,4},{16,0},{20,28},{24,8},{28,20},{1,17},{... | collective-permute-start | bytes 2457608 | tf_op jit(solution)/shard_map/ppermute | solution.py:42
  26.8 17.7 %collective-permute-start.5 = (bf16[640,640]{1,0:T(8,128)(2,1)}, bf16[640,640]{1,0:T(8,128)(2,1)S(1)}, u32[]{:S(2)}, u32[]{:S(2)}) collective-permute-start(bf16[640,640]{1,0:T(8,128)(2,1)} %get-tuple-element.44.refs_5_), channel_id=1, source_target_pairs={{1,2},{2,1},{5,6},{6,5},{9,10},{10,9},{13,14},{14,13},{17,18},{18,... | collective-permute-start | bytes 2457608 | tf_op jit(solution)/shard_map/ppermute | solution.py:38
  27.5 25.1 %collective-permute-start.4 = (bf16[640,640]{1,0:T(8,128)(2,1)}, bf16[640,640]{1,0:T(8,128)(2,1)S(1)}, u32[]{:S(2)}, u32[]{:S(2)}) collective-permute-start(bf16[640,640]{1,0:T(8,128)(2,1)} %get-tuple-element.45), channel_id=1, source_target_pairs={{1,0},{2,3},{5,4},{6,7},{9,8},{10,11},{13,12},{14,15},{17,16},{18,... | collective-permute-start | bytes 2457608 | tf_op jit(solution)/shard_map/ppermute | solution.py:38
  54.8 26.3 %copy-start.1 = (bf16[640,640]{1,0:T(8,128)(2,1)}, bf16[640,640]{1,0:T(8,128)(2,1)S(1)}, u32[]{:S(2)}) copy-start(bf16[640,640]{1,0:T(8,128)(2,1)S(1)} %broadcast_select_fusion.1.refs_2_) | copy-start | bytes 2457604
  54.8 21.2 %collective-permute-start.7 = (bf16[640,640]{1,0:T(8,128)(2,1)S(1)}, bf16[640,640]{1,0:T(8,128)(2,1)S(1)}, u32[]{:S(2)}, u32[]{:S(2)}) collective-permute-start(bf16[640,640]{1,0:T(8,128)(2,1)S(1)} %broadcast_select_fusion.1.refs_2_), channel_id=1, source_target_pairs={{0,8},{4,20},{8,0},{12,28},{16,24},{20,4},{24,16},{28,12},{1,9},{5... | collective-permute-start | bytes 2457608 | tf_op jit(solution)/shard_map/ppermute | solution.py:42
  55.4 22.6 %collective-permute-start.8 = (bf16[640,640]{1,0:T(8,128)(2,1)S(1)}, bf16[640,640]{1,0:T(8,128)(2,1)S(1)}, u32[]{:S(2)}, u32[]{:S(2)}) collective-permute-start(bf16[640,640]{1,0:T(8,128)(2,1)S(1)} %broadcast_select_fusion.1.refs_2_), channel_id=1, source_target_pairs={{0,16},{4,12},{8,24},{12,4},{16,0},{20,28},{24,8},{28,20},{1,17},{... | collective-permute-start | bytes 2457608 | tf_op jit(solution)/shard_map/ppermute | solution.py:42
  55.9 23.1 %collective-permute-start.6 = (bf16[640,640]{1,0:T(8,128)(2,1)S(1)}, bf16[640,640]{1,0:T(8,128)(2,1)S(1)}, u32[]{:S(2)}, u32[]{:S(2)}) collective-permute-start(bf16[640,640]{1,0:T(8,128)(2,1)S(1)} %copy-done.6), channel_id=1, source_target_pairs={{1,0},{2,3},{5,4},{6,7},{9,8},{10,11},{13,12},{14,15},{17,16},{18,... | collective-permute-start | bytes 2457608 | tf_op jit(solution)/shard_map/ppermute | solution.py:38
  57.2 23.9 %collective-permute-start.9 = (bf16[640,640]{1,0:T(8,128)(2,1)}, bf16[640,640]{1,0:T(8,128)(2,1)}, u32[]{:S(2)}, u32[]{:S(2)}) collective-permute-start(bf16[640,640]{1,0:T(8,128)(2,1)} %get-tuple-element.51.refs_6_), channel_id=1, source_target_pairs={{0,16},{4,12},{8,24},{12,4},{16,0},{20,28},{24,8},{28,20},{1,17},{... | collective-permute-start | bytes 2457608 | tf_op jit(solution)/shard_map/ppermute | solution.py:42
  58.8 57.9 %collective-permute-start.10 = (bf16[512,1920]{1,0:T(8,128)(2,1)}, bf16[512,1920]{1,0:T(8,128)(2,1)S(1)}, u32[]{:S(2)}, u32[]{:S(2)}) collective-permute-start(bf16[512,1920]{1,0:T(8,128)(2,1)} %get-tuple-element.54), channel_id=1, source_target_pairs={{0,1},{1,0},{2,3},{3,2},{4,5},{5,4},{6,7},{7,6},{8,9},{9,8},{10,11... | collective-permute-start | bytes 5898248 | tf_op jit(solution)/shard_map/ppermute | solution.py:38
  76.1 40.7 %collective-permute-start.11 = (bf16[512,1920]{1,0:T(8,128)(2,1)}, bf16[512,1920]{1,0:T(8,128)(2,1)}, u32[]{:S(2)}, u32[]{:S(2)}) collective-permute-start(bf16[512,1920]{1,0:T(8,128)(2,1)} %get-tuple-element.55), channel_id=1, source_target_pairs={{1,2},{2,1},{5,6},{6,5},{9,10},{10,9},{13,14},{14,13},{17,18},{18,... | collective-permute-start | bytes 5898248 | tf_op jit(solution)/shard_map/ppermute | solution.py:38
  82.4 34.4 %copy-start.15 = (bf16[640,640]{1,0:T(8,128)(2,1)}, bf16[640,640]{1,0:T(8,128)(2,1)S(1)}, u32[]{:S(2)}) copy-start(bf16[640,640]{1,0:T(8,128)(2,1)S(1)} %broadcast_select_fusion.refs_2_) | copy-start | bytes 2457604
  82.4 20.7 %collective-permute-start.13 = (bf16[640,640]{1,0:T(8,128)(2,1)S(1)}, bf16[640,640]{1,0:T(8,128)(2,1)S(1)}, u32[]{:S(2)}, u32[]{:S(2)}) collective-permute-start(bf16[640,640]{1,0:T(8,128)(2,1)S(1)} %broadcast_select_fusion.refs_2_), channel_id=1, source_target_pairs={{0,8},{4,20},{8,0},{12,28},{16,24},{20,4},{24,16},{28,12},{1,9},{5... | collective-permute-start | bytes 2457608 | tf_op jit(solution)/shard_map/ppermute | solution.py:42
  83.0 20.2 %collective-permute-start.14 = (bf16[640,640]{1,0:T(8,128)(2,1)S(1)}, bf16[640,640]{1,0:T(8,128)(2,1)S(1)}, u32[]{:S(2)}, u32[]{:S(2)}) collective-permute-start(bf16[640,640]{1,0:T(8,128)(2,1)S(1)} %broadcast_select_fusion.refs_2_), channel_id=1, source_target_pairs={{0,16},{4,12},{8,24},{12,4},{16,0},{20,28},{24,8},{28,20},{1,17},{... | collective-permute-start | bytes 2457608 | tf_op jit(solution)/shard_map/ppermute | solution.py:42
  84.3 27.4 %collective-permute-start.12 = (bf16[640,640]{1,0:T(8,128)(2,1)S(1)}, bf16[640,640]{1,0:T(8,128)(2,1)S(1)}, u32[]{:S(2)}, u32[]{:S(2)}) collective-permute-start(bf16[640,640]{1,0:T(8,128)(2,1)S(1)} %copy-done.3), channel_id=1, source_target_pairs={{0,16},{4,12},{8,24},{12,4},{16,0},{20,28},{24,8},{28,20},{1,17},{... | collective-permute-start | bytes 2457608 | tf_op jit(solution)/shard_map/ppermute | solution.py:42
  103.2 14.8 %collective-permute-start.15 = (bf16[640,640]{1,0:T(8,128)(2,1)}, bf16[640,640]{1,0:T(8,128)(2,1)}, u32[]{:S(2)}, u32[]{:S(2)}) collective-permute-start(bf16[640,640]{1,0:T(8,128)(2,1)} %get-tuple-element.65.refs_7_), channel_id=1, source_target_pairs={{0,4},{4,0},{8,12},{12,8},{16,20},{20,16},{24,28},{28,24},{1,5},{5... | collective-permute-start | bytes 2457608 | tf_op jit(solution)/shard_map/ppermute | solution.py:42
  103.2 15.3 %collective-permute-start.16 = (bf16[640,640]{1,0:T(8,128)(2,1)}, bf16[640,640]{1,0:T(8,128)(2,1)}, u32[]{:S(2)}, u32[]{:S(2)}) collective-permute-start(bf16[640,640]{1,0:T(8,128)(2,1)} %get-tuple-element.66.refs_8_), channel_id=1, source_target_pairs={{0,4},{4,0},{8,12},{12,8},{16,20},{20,16},{24,28},{28,24},{1,5},{5... | collective-permute-start | bytes 2457608 | tf_op jit(solution)/shard_map/ppermute | solution.py:42
  111.6 6.9 %collective-permute-start.17 = (bf16[640,640]{1,0:T(8,128)(2,1)}, bf16[640,640]{1,0:T(8,128)(2,1)}, u32[]{:S(2)}, u32[]{:S(2)}) collective-permute-start(bf16[640,640]{1,0:T(8,128)(2,1)} %get-tuple-element.67.refs_9_), channel_id=1, source_target_pairs={{0,4},{4,0},{8,12},{12,8},{16,20},{20,16},{24,28},{28,24},{1,5},{5... | collective-permute-start | bytes 2457608 | tf_op jit(solution)/shard_map/ppermute | solution.py:42
  116.7 2.7 %collective-permute-start.18 = (bf16[640,640]{1,0:T(8,128)(2,1)}, bf16[640,640]{1,0:T(8,128)(2,1)}, u32[]{:S(2)}, u32[]{:S(2)}) collective-permute-start(bf16[640,640]{1,0:T(8,128)(2,1)} %get-tuple-element.68.refs_10_), channel_id=1, source_target_pairs={{0,4},{4,0},{8,12},{12,8},{16,20},{20,16},{24,28},{28,24},{1,5},{5... | collective-permute-start | bytes 2457608 | tf_op jit(solution)/shard_map/ppermute | solution.py:42
  118.0 3.0 %collective-permute-start.19 = (bf16[640,640]{1,0:T(8,128)(2,1)}, bf16[640,640]{1,0:T(8,128)(2,1)S(1)}, u32[]{:S(2)}, u32[]{:S(2)}) collective-permute-start(bf16[640,640]{1,0:T(8,128)(2,1)} %get-tuple-element.69.refs_15_), channel_id=1, source_target_pairs={{0,4},{4,0},{8,12},{12,8},{16,20},{20,16},{24,28},{28,24},{1,5},{5... | collective-permute-start | bytes 2457608 | tf_op jit(solution)/shard_map/ppermute | solution.py:42
  118.0 3.7 %collective-permute-start.20 = (bf16[640,640]{1,0:T(8,128)(2,1)}, bf16[640,640]{1,0:T(8,128)(2,1)S(1)}, u32[]{:S(2)}, u32[]{:S(2)}) collective-permute-start(bf16[640,640]{1,0:T(8,128)(2,1)} %get-tuple-element.70.refs_16_), channel_id=1, source_target_pairs={{0,4},{4,0},{8,12},{12,8},{16,20},{20,16},{24,28},{28,24},{1,5},{5... | collective-permute-start | bytes 2457608 | tf_op jit(solution)/shard_map/ppermute | solution.py:42
  118.5 4.4 %collective-permute-start.21 = (bf16[640,640]{1,0:T(8,128)(2,1)}, bf16[640,640]{1,0:T(8,128)(2,1)S(1)}, u32[]{:S(2)}, u32[]{:S(2)}) collective-permute-start(bf16[640,640]{1,0:T(8,128)(2,1)} %get-tuple-element.71.refs_17_), channel_id=1, source_target_pairs={{0,4},{4,0},{8,12},{12,8},{16,20},{20,16},{24,28},{28,24},{1,5},{5... | collective-permute-start | bytes 2457608 | tf_op jit(solution)/shard_map/ppermute | solution.py:42
  118.6 5.5 %collective-permute-start.22 = (bf16[640,640]{1,0:T(8,128)(2,1)}, bf16[640,640]{1,0:T(8,128)(2,1)S(1)}, u32[]{:S(2)}, u32[]{:S(2)}) collective-permute-start(bf16[640,640]{1,0:T(8,128)(2,1)} %get-tuple-element.72.refs_18_), channel_id=1, source_target_pairs={{0,4},{4,0},{8,12},{12,8},{16,20},{20,16},{24,28},{28,24},{1,5},{5... | collective-permute-start | bytes 2457608 | tf_op jit(solution)/shard_map/ppermute | solution.py:42
  119.4 22.7 %collective-permute-start.25 = (bf16[640,640]{1,0:T(8,128)(2,1)}, bf16[640,640]{1,0:T(8,128)(2,1)S(1)}, u32[]{:S(2)}, u32[]{:S(2)}) collective-permute-start(bf16[640,640]{1,0:T(8,128)(2,1)} %copy-done.9), channel_id=1, source_target_pairs={{0,16},{4,12},{8,24},{12,4},{16,0},{20,28},{24,8},{28,20},{1,17},{... | collective-permute-start | bytes 2457608 | tf_op jit(solution)/shard_map/ppermute | solution.py:42
  121.0 21.4 %collective-permute-start.23 = (bf16[512,640]{1,0:T(8,128)(2,1)}, bf16[512,640]{1,0:T(8,128)(2,1)S(1)}, u32[]{:S(2)}, u32[]{:S(2)}) collective-permute-start(bf16[512,640]{1,0:T(8,128)(2,1)} %get-tuple-element.73), channel_id=1, source_target_pairs={{0,1},{1,0},{2,3},{3,2},{4,5},{5,4},{6,7},{7,6},{8,9},{9,8},{10,11... | collective-permute-start | bytes 1966088 | tf_op jit(solution)/shard_map/ppermute | solution.py:38
  121.7 20.7 %collective-permute-start.24 = (bf16[512,640]{1,0:T(8,128)(2,1)}, bf16[512,640]{1,0:T(8,128)(2,1)S(1)}, u32[]{:S(2)}, u32[]{:S(2)}) collective-permute-start(bf16[512,640]{1,0:T(8,128)(2,1)} %get-tuple-element.74), channel_id=1, source_target_pairs={{1,2},{2,1},{5,6},{6,5},{9,10},{10,9},{13,14},{14,13},{17,18},{18,... | collective-permute-start | bytes 1966088 | tf_op jit(solution)/shard_map/ppermute | solution.py:38
  122.8 21.0 %collective-permute-start.26 = (bf16[640,640]{1,0:T(8,128)(2,1)}, bf16[640,640]{1,0:T(8,128)(2,1)}, u32[]{:S(2)}, u32[]{:S(2)}) collective-permute-start(bf16[640,640]{1,0:T(8,128)(2,1)} %copy-done.15), channel_id=1, source_target_pairs={{0,4},{4,0},{8,12},{12,8},{16,20},{20,16},{24,28},{28,24},{1,5},{5... | collective-permute-start | bytes 2457608 | tf_op jit(solution)/shard_map/ppermute | solution.py:42
  124.0 19.8 %collective-permute-start.27 = (bf16[640,640]{1,0:T(8,128)(2,1)}, bf16[640,640]{1,0:T(8,128)(2,1)}, u32[]{:S(2)}, u32[]{:S(2)}) collective-permute-start(bf16[640,640]{1,0:T(8,128)(2,1)} %copy-done.9), channel_id=1, source_target_pairs={{0,4},{4,0},{8,12},{12,8},{16,20},{20,16},{24,28},{28,24},{1,5},{5... | collective-permute-start | bytes 2457608 | tf_op jit(solution)/shard_map/ppermute | solution.py:42
  142.2 2.5 %collective-permute-start.28 = (bf16[640,640]{1,0:T(8,128)(2,1)S(1)}, bf16[640,640]{1,0:T(8,128)(2,1)}, u32[]{:S(2)}, u32[]{:S(2)}) collective-permute-start(bf16[640,640]{1,0:T(8,128)(2,1)S(1)} %copy-done.11), channel_id=1, source_target_pairs={{0,4},{4,0},{8,12},{12,8},{16,20},{20,16},{24,28},{28,24},{1,5},{5... | collective-permute-start | bytes 2457608 | tf_op jit(solution)/shard_map/ppermute | solution.py:42
  143.5 2.5 %collective-permute-start.29 = (bf16[640,640]{1,0:T(8,128)(2,1)}, bf16[640,640]{1,0:T(8,128)(2,1)S(1)}, u32[]{:S(2)}, u32[]{:S(2)}) collective-permute-start(bf16[640,640]{1,0:T(8,128)(2,1)} %get-tuple-element.78.refs_5_), channel_id=1, source_target_pairs={{0,4},{4,0},{8,12},{12,8},{16,20},{20,16},{24,28},{28,24},{1,5},{5... | collective-permute-start | bytes 2457608 | tf_op jit(solution)/shard_map/ppermute | solution.py:42
  (21 other events, 83.1 us)

commit v4 on v3

--- a/solution.py
+++ b/solution.py
@@ -11,8 +11,8 @@
 LOG2_E = 1.4426950408889634
 LOW = -1e30
 MIB = 1024 * 1024
-VMEM_MIB = 60
-PAIR_SLOTS, MIDDLE_SLOTS = (3, 1), (3, 1)
+VMEM_MIB = 64
+PAIR_SLOTS, MIDDLE_SLOTS = (3, 1), (4,)
 LINE = 4
 LANES = 8
 VMEM = pl.BlockSpec(memory_space=pltpu.VMEM)
@@ -50,7 +50,7 @@
     return pl.CostEstimate(flops=0, bytes_accessed=0, transcendentals=0)
 
 
-def step(chain, tokens, operands=()):
+def step(chain, tokens, operands=(), cost=0):
     def kernel(*refs):
         del refs
 
@@ -61,7 +61,8 @@
         in_specs=[ANY] * (len(values) + len(tokens)),
         out_specs=[ANY] * len(values),
         input_output_aliases={at: at for at in range(len(values))},
-        cost_estimate=no_cost(),
+        compiler_params=big_kernel(),
+        cost_estimate=pl.CostEstimate(flops=0, bytes_accessed=cost, transcendentals=0),
         name="step",
     )(*values, *tokens)
 
@@ -274,33 +275,30 @@
     outer, across = along_line(crossed, OUTWARD, OUTWARD), to_middle(first)
     first_near = to_neighbours(first)
 
-    operands = [*first_near, outer, across, to_pair[0], over_middle[0]]
-    chain, *operands = step(chain, [], operands)
-    first_near, (outer, across, *packs) = operands[:2], operands[2:]
+    chain, outer, across, *packs = step(chain, [], [outer, across, to_pair[0], over_middle[0]])
+    chain, *first_near = step(chain, [], first_near)
     outer_next = along_line(across, OUTWARD, OUTWARD)
     pairs, middles = [to_pairs(packs[0])], [to_middle(packs[1])]
     first_all = [first, *first_near, to_diagonal(first_near[0])]
     second = jnp.where(edge, outer, crossed)
     second_near = to_neighbours(second)
 
-    operands = [outer_next, second, *second_near, *first_all]
-    chain, *operands = step(chain, [], operands)
-    outer_next, second, *operands = operands
+    chain, outer_next = step(chain, [], [outer_next])
+    chain, second, *operands = step(chain, [], [second, *second_near, *first_all], 8 * MIB)
     second_near, first_all = operands[:2], operands[2:]
     third = jnp.where(edge, outer_next, across)
     third_near = to_neighbours(third)
     second_all = [second, *second_near, to_diagonal(second_near[0])]
     third_all = [third, *third_near, to_diagonal(third_near[0])]
     first_all += other_core(first_all)
-    operands = [pairs[0], middles[0], to_pair[1], over_middle[1], *second_all]
-    chain, pairs[0], middles[0], pair_pack, pack, *second_all = step(chain, third_near, operands)
+    operands = [pairs[0], middles[0], to_pair[1], *second_all]
+    chain, pairs[0], middles[0], pair_pack, *second_all = step(chain, third_near, operands)
     pairs.append(to_pairs(pair_pack))
-    middles.append(to_middle(pack))
     second_all += other_core(second_all)
     sums = worked([0, 1, 2], stream, pairs, middles, [[out_weight], first_all, second_all], jnp.float32)
 
     tokens = []
-    chain, sums, pairs[1], middles[1], third_all[3] = step(chain, tokens, [sums, pairs[1], middles[1], third_all[3]])
+    chain, sums, pairs[1], third_all[3] = step(chain, tokens, [sums, pairs[1], third_all[3]])
     third_all += other_core(third_all)
     return worked([3], sums, pairs, middles, [third_all], stream.dtype)
 

time: 157 us -> 149 us (0.949)
  waiting for transfers between devices: 87.6 us -> 79.6 us
  local copies, waits for them, and re-layouts: 7.7 us -> 2.74 us
  starting transfers between devices: 25.9 us -> 30.5 us
  other arithmetic: 3.3 us -> 4.94 us
    ppermute x21, waiting for transfers between devices: 63.1 us -> 35.2 us  [in_plane(): lax.ppermute(value, 'dp', [(lane, lane ^ masks[lane % 2]) for lane in ran...]
    ppermute x9 -> x8, waiting for transfers between devices: 24.5 us -> 44.3 us  [along_line(): return lax.ppermute(value, ('dp', 'ctx'), pairs)]
    unnamed x46 -> x0, local copies, waits for them, and re-layouts: 5.81 us -> none
    ppermute x21, starting transfers between devices: 13.3 us -> 17.8 us  [in_plane(): lax.ppermute(value, 'dp', [(lane, lane ^ masks[lane % 2]) for lane in ran...]
    ppermute x9 -> x8, starting transfers between devices: 12.6 us -> 12.8 us  [along_line(): return lax.ppermute(value, ('dp', 'ctx'), pairs)]
  transfers between devices with their start and end apart: 30 -> 29, of which waited for: 15 -> 12; matrix products, arithmetic and copies ran while one was open for 2% -> 4% of each run, Pallas kernels for 14% -> 15%
where the time goes in v4:
time: 149 us
  waiting for transfers between devices  79.6 us (53%)
  Pallas kernels  31.1 us (21%)
  starting transfers between devices  30.5 us (20%)
  other arithmetic  4.94 us (3%)
  local copies, waits for them, and re-layouts  2.74 us (2%)
    ppermute x8, waiting for transfers between devices, along_line(): return lax.ppermute(value, ('dp', 'ctx'), pairs)  44.3 us
    ppermute x21, waiting for transfers between devices, in_plane(): lax.ppermute(value, 'dp', [(lane, lane ^ masks[lane % 2]) for lane in ran...  35.2 us
    pallas_call x2, Pallas kernels, worked_off(): pl.pallas_call(kernel, out_shape=jax.ShapeDtypeStruct(base.shape, dtype),...  25.9 us
    ppermute x21, starting transfers between devices, in_plane(): lax.ppermute(value, 'dp', [(lane, lane ^ masks[lane % 2]) for lane in ran...  17.8 us
    ppermute x8, starting transfers between devices, along_line(): return lax.ppermute(value, ('dp', 'ctx'), pairs)  12.8 us
    pallas_call x1, Pallas kernels, packed(): pl.pallas_call(pack_kernel, out_shape=shapes, grid_spec=pltpu.PrefetchSca...  5.13 us
  transfers between devices with their start and end apart: 29, of which 12 were waited for; matrix products, arithmetic and copies ran while one was open for 4% of the time, Pallas kernels for 15%

profile of v4, /device:TPU:0, one launch (start us, length us, event | category | flops | bytes accessed | tf_op | source)
XLA Modules:
  0.0 149.1 jit_solution(9709107440850254664)
XLA Ops:
  0.0 2.1 %constant_dynamic-slice_fusion = bf16[640,640]{1,0:T(8,128)(2,1)} fusion(bf16[640,5120]{1,0:T(8,128)(2,1)} %refs_6_.1, s32[]{:T(128)S(6)} %select_n.30), kind=kLoop, calls=%fused_computation.7 | loop fusion | bytes 1638404 | tf_op jit(solution)/shard_map/dynamic_slice | solution.py:253
  2.1 3.0 %collective-permute-start = (bf16[640,640]{1,0:T(8,128)(2,1)}, bf16[640,640]{1,0:T(8,128)(2,1)}, u32[]{:S(2)}, u32[]{:S(2)}) collective-permute-start(bf16[640,640]{1,0:T(8,128)(2,1)} %constant_dynamic-slice_fusion), channel_id=1, source_target_pairs={{0,1},{1,0},{2,3},{3,2},{4,5},{5,4},{6,7},{7,6},{8,9},{9,8},{10,11... | collective-permute-start | bytes 2457608 | tf_op jit(solution)/shard_map/ppermute | solution.py:38
  5.1 1.6 %collective-permute-start.1 = (bf16[640,640]{1,0:T(8,128)(2,1)}, bf16[640,640]{1,0:T(8,128)(2,1)}, u32[]{:S(2)}, u32[]{:S(2)}) collective-permute-start(bf16[640,640]{1,0:T(8,128)(2,1)} %constant_dynamic-slice_fusion), channel_id=1, source_target_pairs={{1,2},{2,1},{5,6},{6,5},{9,10},{10,9},{13,14},{14,13},{17,18},{18,... | collective-permute-start | bytes 2457608 | tf_op jit(solution)/shard_map/ppermute | solution.py:38
  8.0 5.1 %pack_window.1 = (f32[8,128]{1,0:T(8,128)}, bf16[512,1920]{1,0:T(8,128)(2,1)}, bf16[512,640]{1,0:T(8,128)(2,1)}, bf16[512,2560]{1,0:T(8,128)(2,1)}) custom-call(s32[21]{0:T(128)} %concatenate.3.place, bf16[256,2560]{1,0:T(8,128)(2,1)} %key_ref.5, bf16[256,2560]{1,0:T(8,128)(2,1)} %value_ref.5), custom_call_target="tpu_custom_call" | custom-call | tf_op jit(solution)/shard_map/pack_window/pallas_call | solution.py:106
  13.1 10.6 %collective-permute-done.refs_1_ = bf16[640,640]{1,0:T(8,128)(2,1)} collective-permute-done((bf16[640,640]{1,0:T(8,128)(2,1)}, bf16[640,640]{1,0:T(8,128)(2,1)}, u32[]{:S(2)}, u32[]{:S(2)}) %collective-permute-start) | collective-permute-done | bytes 819232 | tf_op jit(solution)/shard_map/ppermute | solution.py:38
  23.7 1.6 %collective-permute-start.3 = (bf16[640,640]{1,0:T(8,128)(2,1)}, bf16[640,640]{1,0:T(8,128)(2,1)}, u32[]{:S(2)}, u32[]{:S(2)}) collective-permute-start(bf16[640,640]{1,0:T(8,128)(2,1)} %get-tuple-element.44.refs_4_), channel_id=1, source_target_pairs={{1,2},{2,1},{5,6},{6,5},{9,10},{10,9},{13,14},{14,13},{17,18},{18,... | collective-permute-start | bytes 2457608 | tf_op jit(solution)/shard_map/ppermute | solution.py:38
  26.6 1.7 %collective-permute-start.4 = (bf16[640,640]{1,0:T(8,128)(2,1)}, bf16[640,640]{1,0:T(8,128)(2,1)}, u32[]{:S(2)}, u32[]{:S(2)}) collective-permute-start(bf16[640,640]{1,0:T(8,128)(2,1)} %get-tuple-element.44.refs_4_), channel_id=1, source_target_pairs={{0,8},{4,20},{8,0},{12,28},{16,24},{20,4},{24,16},{28,12},{1,9},{5... | collective-permute-start | bytes 2457608 | tf_op jit(solution)/shard_map/ppermute | solution.py:42
  28.3 1.5 %collective-permute-start.5 = (bf16[640,640]{1,0:T(8,128)(2,1)}, bf16[640,640]{1,0:T(8,128)(2,1)}, u32[]{:S(2)}, u32[]{:S(2)}) collective-permute-start(bf16[640,640]{1,0:T(8,128)(2,1)} %get-tuple-element.44.refs_4_), channel_id=1, source_target_pairs={{0,16},{4,12},{8,24},{12,4},{16,0},{20,28},{24,8},{28,20},{1,17},{... | collective-permute-start | bytes 2457608 | tf_op jit(solution)/shard_map/ppermute | solution.py:42
  29.8 20.7 %collective-permute-done.2.refs_1_ = bf16[640,640]{1,0:T(8,128)(2,1)} collective-permute-done((bf16[640,640]{1,0:T(8,128)(2,1)}, bf16[640,640]{1,0:T(8,128)(2,1)}, u32[]{:S(2)}, u32[]{:S(2)}) %collective-permute-start.2) | collective-permute-done | bytes 819232 | tf_op jit(solution)/shard_map/ppermute | solution.py:38
  51.8 2.2 %collective-permute-start.11 = (bf16[512,2560]{1,0:T(8,128)(2,1)}, bf16[512,2560]{1,0:T(8,128)(2,1)}, u32[]{:S(2)}, u32[]{:S(2)}) collective-permute-start(bf16[512,2560]{1,0:T(8,128)(2,1)} %get-tuple-element.56), channel_id=1, source_target_pairs={{1,2},{2,1},{5,6},{6,5},{9,10},{10,9},{13,14},{14,13},{17,18},{18,... | collective-permute-start | bytes 7864328 | tf_op jit(solution)/shard_map/ppermute | solution.py:38
  53.9 2.1 %broadcast_select_fusion.1.refs_1_ = bf16[640,640]{1,0:T(8,128)(2,1)} fusion(bf16[640,640]{1,0:T(8,128)(2,1)} %get-tuple-element.51, bf16[640,640]{1,0:T(8,128)(2,1)} %get-tuple-element.43, pred[]{:T(512)S(6)} %or.3), kind=kLoop, calls=%fused_computation.1 | loop fusion | flops 409600 | bytes 2457601 | tf_op jit(solution)/shard_map/jit(_where)/select_n | solution.py:283
  56.1 1.5 %collective-permute-start.7 = (bf16[640,640]{1,0:T(8,128)(2,1)}, bf16[640,640]{1,0:T(8,128)(2,1)}, u32[]{:S(2)}, u32[]{:S(2)}) collective-permute-start(bf16[640,640]{1,0:T(8,128)(2,1)} %broadcast_select_fusion.1.refs_1_), channel_id=1, source_target_pairs={{0,8},{4,20},{8,0},{12,28},{16,24},{20,4},{24,16},{28,12},{1,9},{5... | collective-permute-start | bytes 2457608 | tf_op jit(solution)/shard_map/ppermute | solution.py:42
  57.6 1.5 %collective-permute-start.8 = (bf16[640,640]{1,0:T(8,128)(2,1)}, bf16[640,640]{1,0:T(8,128)(2,1)}, u32[]{:S(2)}, u32[]{:S(2)}) collective-permute-start(bf16[640,640]{1,0:T(8,128)(2,1)} %broadcast_select_fusion.1.refs_1_), channel_id=1, source_target_pairs={{0,16},{4,12},{8,24},{12,4},{16,0},{20,28},{24,8},{28,20},{1,17},{... | collective-permute-start | bytes 2457608 | tf_op jit(solution)/shard_map/ppermute | solution.py:42
  59.6 11.1 %collective-permute-done.6.refs_1_ = bf16[640,640]{1,0:T(8,128)(2,1)} collective-permute-done((bf16[640,640]{1,0:T(8,128)(2,1)}, bf16[640,640]{1,0:T(8,128)(2,1)}, u32[]{:S(2)}, u32[]{:S(2)}) %collective-permute-start.6) | collective-permute-done | bytes 819232 | tf_op jit(solution)/shard_map/ppermute | solution.py:38
  70.8 2.1 %broadcast_select_fusion.refs_2_ = bf16[640,640]{1,0:T(8,128)(2,1)} fusion(bf16[640,640]{1,0:T(8,128)(2,1)} %get-tuple-element.61, bf16[640,640]{1,0:T(8,128)(2,1)} %get-tuple-element.49, pred[]{:T(512)S(6)} %or.3), kind=kLoop, calls=%fused_computation | loop fusion | flops 409600 | bytes 2457601 | tf_op jit(solution)/shard_map/jit(_where)/select_n | solution.py:289
  72.9 4.7 %collective-permute-done.7.refs_2_ = bf16[640,640]{1,0:T(8,128)(2,1)} collective-permute-done((bf16[640,640]{1,0:T(8,128)(2,1)}, bf16[640,640]{1,0:T(8,128)(2,1)}, u32[]{:S(2)}, u32[]{:S(2)}) %collective-permute-start.7) | collective-permute-done | bytes 819232 | tf_op jit(solution)/shard_map/ppermute | solution.py:42
  77.6 1.5 %collective-permute-start.13 = (bf16[640,640]{1,0:T(8,128)(2,1)}, bf16[640,640]{1,0:T(8,128)(2,1)}, u32[]{:S(2)}, u32[]{:S(2)}) collective-permute-start(bf16[640,640]{1,0:T(8,128)(2,1)} %broadcast_select_fusion.refs_2_), channel_id=1, source_target_pairs={{0,8},{4,20},{8,0},{12,28},{16,24},{20,4},{24,16},{28,12},{1,9},{5... | collective-permute-start | bytes 2457608 | tf_op jit(solution)/shard_map/ppermute | solution.py:42
  79.1 1.5 %collective-permute-start.14 = (bf16[640,640]{1,0:T(8,128)(2,1)}, bf16[640,640]{1,0:T(8,128)(2,1)}, u32[]{:S(2)}, u32[]{:S(2)}) collective-permute-start(bf16[640,640]{1,0:T(8,128)(2,1)} %broadcast_select_fusion.refs_2_), channel_id=1, source_target_pairs={{0,16},{4,12},{8,24},{12,4},{16,0},{20,28},{24,8},{28,20},{1,17},{... | collective-permute-start | bytes 2457608 | tf_op jit(solution)/shard_map/ppermute | solution.py:42
  80.6 11.2 %collective-permute-done.9.refs_7_ = bf16[640,640]{1,0:T(8,128)(2,1)} collective-permute-done((bf16[640,640]{1,0:T(8,128)(2,1)}, bf16[640,640]{1,0:T(8,128)(2,1)}, u32[]{:S(2)}, u32[]{:S(2)}) %collective-permute-start.9) | collective-permute-done | bytes 819232 | tf_op jit(solution)/shard_map/ppermute | solution.py:42
  91.8 1.5 %collective-permute-start.12 = (bf16[640,640]{1,0:T(8,128)(2,1)}, bf16[640,640]{1,0:T(8,128)(2,1)}, u32[]{:S(2)}, u32[]{:S(2)}) collective-permute-start(bf16[640,640]{1,0:T(8,128)(2,1)} %get-tuple-element.59.refs_5_), channel_id=1, source_target_pairs={{0,16},{4,12},{8,24},{12,4},{16,0},{20,28},{24,8},{28,20},{1,17},{... | collective-permute-start | bytes 2457608 | tf_op jit(solution)/shard_map/ppermute | solution.py:42
  93.4 5.7 %collective-permute-done.13.refs_8_.refs_3_ = bf16[640,640]{1,0:T(8,128)(2,1)} collective-permute-done((bf16[640,640]{1,0:T(8,128)(2,1)}, bf16[640,640]{1,0:T(8,128)(2,1)}, u32[]{:S(2)}, u32[]{:S(2)}) %collective-permute-start.13) | collective-permute-done | bytes 819232 | tf_op jit(solution)/shard_map/ppermute | solution.py:42
  99.1 1.5 %collective-permute-done.14.refs_9_.refs_4_ = bf16[640,640]{1,0:T(8,128)(2,1)} collective-permute-done((bf16[640,640]{1,0:T(8,128)(2,1)}, bf16[640,640]{1,0:T(8,128)(2,1)}, u32[]{:S(2)}, u32[]{:S(2)}) %collective-permute-start.14) | collective-permute-done | bytes 819232 | tf_op jit(solution)/shard_map/ppermute | solution.py:42
  100.6 1.4 collective-permute-start.16
  102.0 7.4 %collective-permute-done.12.refs_7_ = bf16[640,640]{1,0:T(8,128)(2,1)} collective-permute-done((bf16[640,640]{1,0:T(8,128)(2,1)}, bf16[640,640]{1,0:T(8,128)(2,1)}, u32[]{:S(2)}, u32[]{:S(2)}) %collective-permute-start.12) | collective-permute-done | bytes 819232 | tf_op jit(solution)/shard_map/ppermute | solution.py:42
  109.4 1.4 collective-permute-start.17
  110.7 1.9 %collective-permute-done.10.refs_1_ = bf16[512,1920]{1,0:T(8,128)(2,1)} collective-permute-done((bf16[512,1920]{1,0:T(8,128)(2,1)}, bf16[512,1920]{1,0:T(8,128)(2,1)}, u32[]{:S(2)}, u32[]{:S(2)}) %collective-permute-start.10) | collective-permute-done | bytes 1966112 | tf_op jit(solution)/shard_map/ppermute | solution.py:38
  113.8 1.6 %collective-permute-done.18.refs_14_ = bf16[640,640]{1,0:T(8,128)(2,1)} collective-permute-done((bf16[640,640]{1,0:T(8,128)(2,1)}, bf16[640,640]{1,0:T(8,128)(2,1)}, u32[]{:S(2)}, u32[]{:S(2)}) %collective-permute-start.18) | collective-permute-done | bytes 819232 | tf_op jit(solution)/shard_map/ppermute | solution.py:42
  115.4 1.5 %collective-permute-start.24 = (bf16[640,640]{1,0:T(8,128)(2,1)}, bf16[640,640]{1,0:T(8,128)(2,1)}, u32[]{:S(2)}, u32[]{:S(2)}) collective-permute-start(bf16[640,640]{1,0:T(8,128)(2,1)} %collective-permute-done.13.refs_8_.refs_3_), channel_id=1, source_target_pairs={{0,16},{4,12},{8,24},{12,4},{16,0},{20,28},{24,8},{28,20},{1,17},{... | collective-permute-start | bytes 2457608 | tf_op jit(solution)/shard_map/ppermute | solution.py:42
  116.9 1.9 %collective-permute-start.23 = (bf16[512,640]{1,0:T(8,128)(2,1)}, bf16[512,640]{1,0:T(8,128)(2,1)}, u32[]{:S(2)}, u32[]{:S(2)}) collective-permute-start(bf16[512,640]{1,0:T(8,128)(2,1)} %get-tuple-element.73), channel_id=1, source_target_pairs={{0,1},{1,0},{2,3},{3,2},{4,5},{5,4},{6,7},{7,6},{8,9},{9,8},{10,11... | collective-permute-start | bytes 1966088 | tf_op jit(solution)/shard_map/ppermute | solution.py:38
  120.2 17.0 %work_off_slots.2.refs_1_ = f32[256,5120]{1,0:T(8,128)} custom-call(s32[21]{0:T(128)} %concatenate.3.place, bf16[256,2560]{1,0:T(8,128)(2,1)} %query_ref.3, bf16[256,2560]{1,0:T(8,128)(2,1)} %key_ref.5, bf16[256,2560]{1,0:T(8,128)(2,1)} %value_ref.5, bf16[256,5120]{1,0:T(8,128)(2,1)} %base_ref.1, ...), custom_call_target="tpu_custom_call" | custom-call | flops 6543114240 | bytes 37027840 | tf_op jit(solution)/shard_map/work_off_slots/pallas_call | solution.py:206
  137.8 2.3 %collective-permute-done.28.refs_9_ = bf16[640,640]{1,0:T(8,128)(2,1)} collective-permute-done((bf16[640,640]{1,0:T(8,128)(2,1)}, bf16[640,640]{1,0:T(8,128)(2,1)}, u32[]{:S(2)}, u32[]{:S(2)}) %collective-permute-start.28) | collective-permute-done | bytes 819232 | tf_op jit(solution)/shard_map/ppermute | solution.py:42
  140.0 8.9 %work_off_slots.3 = bf16[256,5120]{1,0:T(8,128)(2,1)} custom-call(s32[21]{0:T(128)} %concatenate.3.place, bf16[256,2560]{1,0:T(8,128)(2,1)} %query_ref.3, bf16[256,2560]{1,0:T(8,128)(2,1)} %key_ref.5, bf16[256,2560]{1,0:T(8,128)(2,1)} %value_ref.5, f32[256,5120]{1,0:T(8,128)} %get-tuple-element.74.base_ref, bf16[512,640]{1,0:T(8,128)(2,1)} %get-tuple-element.75.refs_0_, ...), custom_call_target="tpu_custom_call" | custom-call | flops 2181038080 | bytes 19333120 | tf_op jit(solution)/shard_map/work_off_slots/pallas_call | solution.py:206
  (41 shorter events, 7.4 us)
Async XLA Ops:
  2.1 21.6 %collective-permute-start = (bf16[640,640]{1,0:T(8,128)(2,1)}, bf16[640,640]{1,0:T(8,128)(2,1)}, u32[]{:S(2)}, u32[]{:S(2)}) collective-permute-start(bf16[640,640]{1,0:T(8,128)(2,1)} %constant_dynamic-slice_fusion), channel_id=1, source_target_pairs={{0,1},{1,0},{2,3},{3,2},{4,5},{5,4},{6,7},{7,6},{8,9},{9,8},{10,11... | collective-permute-start | bytes 2457608 | tf_op jit(solution)/shard_map/ppermute | solution.py:38
  5.1 18.6 %collective-permute-start.1 = (bf16[640,640]{1,0:T(8,128)(2,1)}, bf16[640,640]{1,0:T(8,128)(2,1)}, u32[]{:S(2)}, u32[]{:S(2)}) collective-permute-start(bf16[640,640]{1,0:T(8,128)(2,1)} %constant_dynamic-slice_fusion), channel_id=1, source_target_pairs={{1,2},{2,1},{5,6},{6,5},{9,10},{10,9},{13,14},{14,13},{17,18},{18,... | collective-permute-start | bytes 2457608 | tf_op jit(solution)/shard_map/ppermute | solution.py:38
  23.7 6.1 %collective-permute-start.3 = (bf16[640,640]{1,0:T(8,128)(2,1)}, bf16[640,640]{1,0:T(8,128)(2,1)}, u32[]{:S(2)}, u32[]{:S(2)}) collective-permute-start(bf16[640,640]{1,0:T(8,128)(2,1)} %get-tuple-element.44.refs_4_), channel_id=1, source_target_pairs={{1,2},{2,1},{5,6},{6,5},{9,10},{10,9},{13,14},{14,13},{17,18},{18,... | collective-permute-start | bytes 2457608 | tf_op jit(solution)/shard_map/ppermute | solution.py:38
  25.3 25.2 %collective-permute-start.2 = (bf16[640,640]{1,0:T(8,128)(2,1)}, bf16[640,640]{1,0:T(8,128)(2,1)}, u32[]{:S(2)}, u32[]{:S(2)}) collective-permute-start(bf16[640,640]{1,0:T(8,128)(2,1)} %get-tuple-element.43), channel_id=1, source_target_pairs={{1,0},{2,3},{5,4},{6,7},{9,8},{10,11},{13,12},{14,15},{17,16},{18,... | collective-permute-start | bytes 2457608 | tf_op jit(solution)/shard_map/ppermute | solution.py:38
  26.6 31.0 %collective-permute-start.4 = (bf16[640,640]{1,0:T(8,128)(2,1)}, bf16[640,640]{1,0:T(8,128)(2,1)}, u32[]{:S(2)}, u32[]{:S(2)}) collective-permute-start(bf16[640,640]{1,0:T(8,128)(2,1)} %get-tuple-element.44.refs_4_), channel_id=1, source_target_pairs={{0,8},{4,20},{8,0},{12,28},{16,24},{20,4},{24,16},{28,12},{1,9},{5... | collective-permute-start | bytes 2457608 | tf_op jit(solution)/shard_map/ppermute | solution.py:42
  28.3 30.8 %collective-permute-start.5 = (bf16[640,640]{1,0:T(8,128)(2,1)}, bf16[640,640]{1,0:T(8,128)(2,1)}, u32[]{:S(2)}, u32[]{:S(2)}) collective-permute-start(bf16[640,640]{1,0:T(8,128)(2,1)} %get-tuple-element.44.refs_4_), channel_id=1, source_target_pairs={{0,16},{4,12},{8,24},{12,4},{16,0},{20,28},{24,8},{28,20},{1,17},{... | collective-permute-start | bytes 2457608 | tf_op jit(solution)/shard_map/ppermute | solution.py:42
  50.5 20.3 %collective-permute-start.6 = (bf16[640,640]{1,0:T(8,128)(2,1)}, bf16[640,640]{1,0:T(8,128)(2,1)}, u32[]{:S(2)}, u32[]{:S(2)}) collective-permute-start(bf16[640,640]{1,0:T(8,128)(2,1)} %get-tuple-element.49), channel_id=1, source_target_pairs={{1,0},{2,3},{5,4},{6,7},{9,8},{10,11},{13,12},{14,15},{17,16},{18,... | collective-permute-start | bytes 2457608 | tf_op jit(solution)/shard_map/ppermute | solution.py:38
  51.8 60.9 %collective-permute-start.11 = (bf16[512,2560]{1,0:T(8,128)(2,1)}, bf16[512,2560]{1,0:T(8,128)(2,1)}, u32[]{:S(2)}, u32[]{:S(2)}) collective-permute-start(bf16[512,2560]{1,0:T(8,128)(2,1)} %get-tuple-element.56), channel_id=1, source_target_pairs={{1,2},{2,1},{5,6},{6,5},{9,10},{10,9},{13,14},{14,13},{17,18},{18,... | collective-permute-start | bytes 7864328 | tf_op jit(solution)/shard_map/ppermute | solution.py:38
  56.1 21.5 %collective-permute-start.7 = (bf16[640,640]{1,0:T(8,128)(2,1)}, bf16[640,640]{1,0:T(8,128)(2,1)}, u32[]{:S(2)}, u32[]{:S(2)}) collective-permute-start(bf16[640,640]{1,0:T(8,128)(2,1)} %broadcast_select_fusion.1.refs_1_), channel_id=1, source_target_pairs={{0,8},{4,20},{8,0},{12,28},{16,24},{20,4},{24,16},{28,12},{1,9},{5... | collective-permute-start | bytes 2457608 | tf_op jit(solution)/shard_map/ppermute | solution.py:42
  57.6 21.5 %collective-permute-start.8 = (bf16[640,640]{1,0:T(8,128)(2,1)}, bf16[640,640]{1,0:T(8,128)(2,1)}, u32[]{:S(2)}, u32[]{:S(2)}) collective-permute-start(bf16[640,640]{1,0:T(8,128)(2,1)} %broadcast_select_fusion.1.refs_1_), channel_id=1, source_target_pairs={{0,16},{4,12},{8,24},{12,4},{16,0},{20,28},{24,8},{28,20},{1,17},{... | collective-permute-start | bytes 2457608 | tf_op jit(solution)/shard_map/ppermute | solution.py:42
  59.1 32.7 %collective-permute-start.9 = (bf16[640,640]{1,0:T(8,128)(2,1)}, bf16[640,640]{1,0:T(8,128)(2,1)}, u32[]{:S(2)}, u32[]{:S(2)}) collective-permute-start(bf16[640,640]{1,0:T(8,128)(2,1)} %get-tuple-element.52.refs_5_), channel_id=1, source_target_pairs={{0,16},{4,12},{8,24},{12,4},{16,0},{20,28},{24,8},{28,20},{1,17},{... | collective-permute-start | bytes 2457608 | tf_op jit(solution)/shard_map/ppermute | solution.py:42
  70.8 41.9 %collective-permute-start.10 = (bf16[512,1920]{1,0:T(8,128)(2,1)}, bf16[512,1920]{1,0:T(8,128)(2,1)}, u32[]{:S(2)}, u32[]{:S(2)}) collective-permute-start(bf16[512,1920]{1,0:T(8,128)(2,1)} %get-tuple-element.55), channel_id=1, source_target_pairs={{0,1},{1,0},{2,3},{3,2},{4,5},{5,4},{6,7},{7,6},{8,9},{9,8},{10,11... | collective-permute-start | bytes 5898248 | tf_op jit(solution)/shard_map/ppermute | solution.py:38
  77.6 21.5 %collective-permute-start.13 = (bf16[640,640]{1,0:T(8,128)(2,1)}, bf16[640,640]{1,0:T(8,128)(2,1)}, u32[]{:S(2)}, u32[]{:S(2)}) collective-permute-start(bf16[640,640]{1,0:T(8,128)(2,1)} %broadcast_select_fusion.refs_2_), channel_id=1, source_target_pairs={{0,8},{4,20},{8,0},{12,28},{16,24},{20,4},{24,16},{28,12},{1,9},{5... | collective-permute-start | bytes 2457608 | tf_op jit(solution)/shard_map/ppermute | solution.py:42
  79.1 21.5 %collective-permute-start.14 = (bf16[640,640]{1,0:T(8,128)(2,1)}, bf16[640,640]{1,0:T(8,128)(2,1)}, u32[]{:S(2)}, u32[]{:S(2)}) collective-permute-start(bf16[640,640]{1,0:T(8,128)(2,1)} %broadcast_select_fusion.refs_2_), channel_id=1, source_target_pairs={{0,16},{4,12},{8,24},{12,4},{16,0},{20,28},{24,8},{28,20},{1,17},{... | collective-permute-start | bytes 2457608 | tf_op jit(solution)/shard_map/ppermute | solution.py:42
  91.8 17.6 %collective-permute-start.12 = (bf16[640,640]{1,0:T(8,128)(2,1)}, bf16[640,640]{1,0:T(8,128)(2,1)}, u32[]{:S(2)}, u32[]{:S(2)}) collective-permute-start(bf16[640,640]{1,0:T(8,128)(2,1)} %get-tuple-element.59.refs_5_), channel_id=1, source_target_pairs={{0,16},{4,12},{8,24},{12,4},{16,0},{20,28},{24,8},{28,20},{1,17},{... | collective-permute-start | bytes 2457608 | tf_op jit(solution)/shard_map/ppermute | solution.py:42
  99.1 14.1 %collective-permute-start.15 = (bf16[640,640]{1,0:T(8,128)(2,1)}, bf16[640,640]{1,0:T(8,128)(2,1)}, u32[]{:S(2)}, u32[]{:S(2)}) collective-permute-start(bf16[640,640]{1,0:T(8,128)(2,1)} %get-tuple-element.65.refs_7_), channel_id=1, source_target_pairs={{0,4},{4,0},{8,12},{12,8},{16,20},{20,16},{24,28},{28,24},{1,5},{5... | collective-permute-start | bytes 2457608 | tf_op jit(solution)/shard_map/ppermute | solution.py:42
  100.6 12.7 %collective-permute-start.16 = (bf16[640,640]{1,0:T(8,128)(2,1)}, bf16[640,640]{1,0:T(8,128)(2,1)}, u32[]{:S(2)}, u32[]{:S(2)}) collective-permute-start(bf16[640,640]{1,0:T(8,128)(2,1)} %get-tuple-element.66.refs_8_), channel_id=1, source_target_pairs={{0,4},{4,0},{8,12},{12,8},{16,20},{20,16},{24,28},{28,24},{1,5},{5... | collective-permute-start | bytes 2457608 | tf_op jit(solution)/shard_map/ppermute | solution.py:42
  109.4 4.3 %collective-permute-start.17 = (bf16[640,640]{1,0:T(8,128)(2,1)}, bf16[640,640]{1,0:T(8,128)(2,1)}, u32[]{:S(2)}, u32[]{:S(2)}) collective-permute-start(bf16[640,640]{1,0:T(8,128)(2,1)} %get-tuple-element.67.refs_9_), channel_id=1, source_target_pairs={{0,4},{4,0},{8,12},{12,8},{16,20},{20,16},{24,28},{28,24},{1,5},{5... | collective-permute-start | bytes 2457608 | tf_op jit(solution)/shard_map/ppermute | solution.py:42
  112.7 2.7 %collective-permute-start.18 = (bf16[640,640]{1,0:T(8,128)(2,1)}, bf16[640,640]{1,0:T(8,128)(2,1)}, u32[]{:S(2)}, u32[]{:S(2)}) collective-permute-start(bf16[640,640]{1,0:T(8,128)(2,1)} %get-tuple-element.68.refs_10_), channel_id=1, source_target_pairs={{0,4},{4,0},{8,12},{12,8},{16,20},{20,16},{24,28},{28,24},{1,5},{5... | collective-permute-start | bytes 2457608 | tf_op jit(solution)/shard_map/ppermute | solution.py:42
  112.7 4.2 %collective-permute-start.19 = (bf16[640,640]{1,0:T(8,128)(2,1)}, bf16[640,640]{1,0:T(8,128)(2,1)}, u32[]{:S(2)}, u32[]{:S(2)}) collective-permute-start(bf16[640,640]{1,0:T(8,128)(2,1)} %get-tuple-element.69.refs_15_), channel_id=1, source_target_pairs={{0,4},{4,0},{8,12},{12,8},{16,20},{20,16},{24,28},{28,24},{1,5},{5... | collective-permute-start | bytes 2457608 | tf_op jit(solution)/shard_map/ppermute | solution.py:42
  113.2 5.6 %collective-permute-start.20 = (bf16[640,640]{1,0:T(8,128)(2,1)}, bf16[640,640]{1,0:T(8,128)(2,1)}, u32[]{:S(2)}, u32[]{:S(2)}) collective-permute-start(bf16[640,640]{1,0:T(8,128)(2,1)} %get-tuple-element.70.refs_16_), channel_id=1, source_target_pairs={{0,4},{4,0},{8,12},{12,8},{16,20},{20,16},{24,28},{28,24},{1,5},{5... | collective-permute-start | bytes 2457608 | tf_op jit(solution)/shard_map/ppermute | solution.py:42
  113.3 5.6 %collective-permute-start.21 = (bf16[640,640]{1,0:T(8,128)(2,1)}, bf16[640,640]{1,0:T(8,128)(2,1)}, u32[]{:S(2)}, u32[]{:S(2)}) collective-permute-start(bf16[640,640]{1,0:T(8,128)(2,1)} %get-tuple-element.71.refs_17_), channel_id=1, source_target_pairs={{0,4},{4,0},{8,12},{12,8},{16,20},{20,16},{24,28},{28,24},{1,5},{5... | collective-permute-start | bytes 2457608 | tf_op jit(solution)/shard_map/ppermute | solution.py:42
  113.7 6.3 %collective-permute-start.22 = (bf16[640,640]{1,0:T(8,128)(2,1)}, bf16[640,640]{1,0:T(8,128)(2,1)}, u32[]{:S(2)}, u32[]{:S(2)}) collective-permute-start(bf16[640,640]{1,0:T(8,128)(2,1)} %get-tuple-element.72.refs_18_), channel_id=1, source_target_pairs={{0,4},{4,0},{8,12},{12,8},{16,20},{20,16},{24,28},{28,24},{1,5},{5... | collective-permute-start | bytes 2457608 | tf_op jit(solution)/shard_map/ppermute | solution.py:42
  115.4 21.9 %collective-permute-start.24 = (bf16[640,640]{1,0:T(8,128)(2,1)}, bf16[640,640]{1,0:T(8,128)(2,1)}, u32[]{:S(2)}, u32[]{:S(2)}) collective-permute-start(bf16[640,640]{1,0:T(8,128)(2,1)} %collective-permute-done.13.refs_8_.refs_3_), channel_id=1, source_target_pairs={{0,16},{4,12},{8,24},{12,4},{16,0},{20,28},{24,8},{28,20},{1,17},{... | collective-permute-start | bytes 2457608 | tf_op jit(solution)/shard_map/ppermute | solution.py:42
  116.9 20.4 %collective-permute-start.23 = (bf16[512,640]{1,0:T(8,128)(2,1)}, bf16[512,640]{1,0:T(8,128)(2,1)}, u32[]{:S(2)}, u32[]{:S(2)}) collective-permute-start(bf16[512,640]{1,0:T(8,128)(2,1)} %get-tuple-element.73), channel_id=1, source_target_pairs={{0,1},{1,0},{2,3},{3,2},{4,5},{5,4},{6,7},{7,6},{8,9},{9,8},{10,11... | collective-permute-start | bytes 1966088 | tf_op jit(solution)/shard_map/ppermute | solution.py:38
  118.8 19.0 %collective-permute-start.25 = (bf16[640,640]{1,0:T(8,128)(2,1)}, bf16[640,640]{1,0:T(8,128)(2,1)}, u32[]{:S(2)}, u32[]{:S(2)}) collective-permute-start(bf16[640,640]{1,0:T(8,128)(2,1)} %broadcast_select_fusion.refs_2_), channel_id=1, source_target_pairs={{0,4},{4,0},{8,12},{12,8},{16,20},{20,16},{24,28},{28,24},{1,5},{5... | collective-permute-start | bytes 2457608 | tf_op jit(solution)/shard_map/ppermute | solution.py:42
  118.9 18.8 %collective-permute-start.26 = (bf16[640,640]{1,0:T(8,128)(2,1)}, bf16[640,640]{1,0:T(8,128)(2,1)}, u32[]{:S(2)}, u32[]{:S(2)}) collective-permute-start(bf16[640,640]{1,0:T(8,128)(2,1)} %collective-permute-done.13.refs_8_.refs_3_), channel_id=1, source_target_pairs={{0,4},{4,0},{8,12},{12,8},{16,20},{20,16},{24,28},{28,24},{1,5},{5... | collective-permute-start | bytes 2457608 | tf_op jit(solution)/shard_map/ppermute | solution.py:42
  120.0 17.7 %collective-permute-start.27 = (bf16[640,640]{1,0:T(8,128)(2,1)}, bf16[640,640]{1,0:T(8,128)(2,1)}, u32[]{:S(2)}, u32[]{:S(2)}) collective-permute-start(bf16[640,640]{1,0:T(8,128)(2,1)} %collective-permute-done.14.refs_9_.refs_4_), channel_id=1, source_target_pairs={{0,4},{4,0},{8,12},{12,8},{16,20},{20,16},{24,28},{28,24},{1,5},{5... | collective-permute-start | bytes 2457608 | tf_op jit(solution)/shard_map/ppermute | solution.py:42
  137.3 2.8 %collective-permute-start.28 = (bf16[640,640]{1,0:T(8,128)(2,1)}, bf16[640,640]{1,0:T(8,128)(2,1)}, u32[]{:S(2)}, u32[]{:S(2)}) collective-permute-start(bf16[640,640]{1,0:T(8,128)(2,1)} %get-tuple-element.76.refs_5_), channel_id=1, source_target_pairs={{0,4},{4,0},{8,12},{12,8},{16,20},{20,16},{24,28},{28,24},{1,5},{5... | collective-permute-start | bytes 2457608 | tf_op jit(solution)/shard_map/ppermute | solution.py:42

commit v5 on v4

--- a/solution.py
+++ b/solution.py
@@ -175,16 +175,16 @@
             part = ref.at[:, pl.ds(side_at[at][nth] * depth, depth)]
             found.append(begin(part, beside.at[at, nth], own_sems.at[at, 3 + nth]))
         frames.append(found)
-    blocks = []
+    blocks, ahead = [], LANES // (len(slots) + 1)
     for at in range(len(slots)):
         for copy in frames[at]:
             copy.wait()
         if at == 0:
-            blocks += [begin_block(nth) for nth in range(LANES // 2)]
+            blocks += [begin_block(nth) for nth in range(ahead)]
         part = context.at[:, pl.ds(at * depth, depth)]
         attend(place[HAS_MIDDLE] > 0, *(own.at[at, nth] for nth in range(3)), beside.at[at, 0], beside.at[at, 1], part)
-        if at == 0:
-            blocks += [begin_block(nth) for nth in range(LANES // 2, LANES)]
+        until = LANES if at == len(slots) - 1 else ahead * (at + 2)
+        blocks += [begin_block(nth) for nth in range(len(blocks), until)]
     leaving = []
     for nth in range(LANES):
         for copy in blocks[nth]:
@@ -291,8 +291,8 @@
     second_all = [second, *second_near, to_diagonal(second_near[0])]
     third_all = [third, *third_near, to_diagonal(third_near[0])]
     first_all += other_core(first_all)
-    operands = [pairs[0], middles[0], to_pair[1], *second_all]
-    chain, pairs[0], middles[0], pair_pack, *second_all = step(chain, third_near, operands)
+    operands = [pairs[0], middles[0], to_pair[1], second_all[3]]
+    chain, pairs[0], middles[0], pair_pack, second_all[3] = step(chain, third_near, operands)
     pairs.append(to_pairs(pair_pack))
     second_all += other_core(second_all)
     sums = worked([0, 1, 2], stream, pairs, middles, [[out_weight], first_all, second_all], jnp.float32)

time: 149 us -> 149 us (level)
    ppermute x8, waiting for transfers between devices: 44.3 us -> 45.9 us  [along_line(): return lax.ppermute(value, ('dp', 'ctx'), pairs)]
  transfers between devices with their start and end apart: 29 -> 29, of which waited for: 12 -> 13; matrix products, arithmetic and copies ran while one was open for 4% -> 4% of each run, Pallas kernels for 15% -> 14%
where the time goes in v5:
time: 149 us; the launch traced here: 148 us
  waiting for transfers between devices  79.7 us (53%)
  Pallas kernels  30.3 us (20%)
  starting transfers between devices  30.2 us (20%)
  other arithmetic  4.91 us (3%)
  local copies, waits for them, and re-layouts  2.74 us (2%)
    ppermute x8, waiting for transfers between devices, along_line(): return lax.ppermute(value, ('dp', 'ctx'), pairs)  45.9 us
    ppermute x21, waiting for transfers between devices, in_plane(): lax.ppermute(value, 'dp', [(lane, lane ^ masks[lane % 2]) for lane in ran...  33.8 us
    pallas_call x2, Pallas kernels, worked_off(): pl.pallas_call(kernel, out_shape=jax.ShapeDtypeStruct(base.shape, dtype),...  25.2 us
    ppermute x21, starting transfers between devices, in_plane(): lax.ppermute(value, 'dp', [(lane, lane ^ masks[lane % 2]) for lane in ran...  17.6 us
    ppermute x8, starting transfers between devices, along_line(): return lax.ppermute(value, ('dp', 'ctx'), pairs)  12.6 us
    pallas_call x1, Pallas kernels, packed(): pl.pallas_call(pack_kernel, out_shape=shapes, grid_spec=pltpu.PrefetchSca...  5.13 us
  transfers between devices with their start and end apart: 29, of which 13 were waited for; matrix products, arithmetic and copies ran while one was open for 4% of the time, Pallas kernels for 14%

profile of v5, /device:TPU:0, one launch (start us, length us, event | category | flops | bytes accessed | tf_op | source)
XLA Modules:
  0.0 148.1 jit_solution(15147559301771403365)
XLA Ops:
  0.0 2.1 %constant_dynamic-slice_fusion = bf16[640,640]{1,0:T(8,128)(2,1)} fusion(bf16[640,5120]{1,0:T(8,128)(2,1)} %refs_6_.1, s32[]{:T(128)S(6)} %select_n.30), kind=kLoop, calls=%fused_computation.7 | loop fusion | bytes 1638404 | tf_op jit(solution)/shard_map/dynamic_slice | solution.py:253
  2.1 3.0 %collective-permute-start = (bf16[640,640]{1,0:T(8,128)(2,1)}, bf16[640,640]{1,0:T(8,128)(2,1)}, u32[]{:S(2)}, u32[]{:S(2)}) collective-permute-start(bf16[640,640]{1,0:T(8,128)(2,1)} %constant_dynamic-slice_fusion), channel_id=1, source_target_pairs={{0,1},{1,0},{2,3},{3,2},{4,5},{5,4},{6,7},{7,6},{8,9},{9,8},{10,11... | collective-permute-start | bytes 2457608 | tf_op jit(solution)/shard_map/ppermute | solution.py:38
  5.1 1.6 %collective-permute-start.1 = (bf16[640,640]{1,0:T(8,128)(2,1)}, bf16[640,640]{1,0:T(8,128)(2,1)}, u32[]{:S(2)}, u32[]{:S(2)}) collective-permute-start(bf16[640,640]{1,0:T(8,128)(2,1)} %constant_dynamic-slice_fusion), channel_id=1, source_target_pairs={{1,2},{2,1},{5,6},{6,5},{9,10},{10,9},{13,14},{14,13},{17,18},{18,... | collective-permute-start | bytes 2457608 | tf_op jit(solution)/shard_map/ppermute | solution.py:38
  8.0 5.1 %pack_window.1 = (f32[8,128]{1,0:T(8,128)}, bf16[512,1920]{1,0:T(8,128)(2,1)}, bf16[512,640]{1,0:T(8,128)(2,1)}, bf16[512,2560]{1,0:T(8,128)(2,1)}) custom-call(s32[21]{0:T(128)} %concatenate.3.place, bf16[256,2560]{1,0:T(8,128)(2,1)} %key_ref.5, bf16[256,2560]{1,0:T(8,128)(2,1)} %value_ref.5), custom_call_target="tpu_custom_call" | custom-call | tf_op jit(solution)/shard_map/pack_window/pallas_call | solution.py:106
  13.1 10.6 %collective-permute-done.refs_1_ = bf16[640,640]{1,0:T(8,128)(2,1)} collective-permute-done((bf16[640,640]{1,0:T(8,128)(2,1)}, bf16[640,640]{1,0:T(8,128)(2,1)}, u32[]{:S(2)}, u32[]{:S(2)}) %collective-permute-start) | collective-permute-done | bytes 819232 | tf_op jit(solution)/shard_map/ppermute | solution.py:38
  25.0 1.6 %collective-permute-start.3 = (bf16[640,640]{1,0:T(8,128)(2,1)}, bf16[640,640]{1,0:T(8,128)(2,1)}, u32[]{:S(2)}, u32[]{:S(2)}) collective-permute-start(bf16[640,640]{1,0:T(8,128)(2,1)} %get-tuple-element.41.refs_4_), channel_id=1, source_target_pairs={{1,2},{2,1},{5,6},{6,5},{9,10},{10,9},{13,14},{14,13},{17,18},{18,... | collective-permute-start | bytes 2457608 | tf_op jit(solution)/shard_map/ppermute | solution.py:38
  26.6 1.7 %collective-permute-start.4 = (bf16[640,640]{1,0:T(8,128)(2,1)}, bf16[640,640]{1,0:T(8,128)(2,1)}, u32[]{:S(2)}, u32[]{:S(2)}) collective-permute-start(bf16[640,640]{1,0:T(8,128)(2,1)} %get-tuple-element.41.refs_4_), channel_id=1, source_target_pairs={{0,8},{4,20},{8,0},{12,28},{16,24},{20,4},{24,16},{28,12},{1,9},{5... | collective-permute-start | bytes 2457608 | tf_op jit(solution)/shard_map/ppermute | solution.py:42
  28.2 1.5 %collective-permute-start.5 = (bf16[640,640]{1,0:T(8,128)(2,1)}, bf16[640,640]{1,0:T(8,128)(2,1)}, u32[]{:S(2)}, u32[]{:S(2)}) collective-permute-start(bf16[640,640]{1,0:T(8,128)(2,1)} %get-tuple-element.41.refs_4_), channel_id=1, source_target_pairs={{0,16},{4,12},{8,24},{12,4},{16,0},{20,28},{24,8},{28,20},{1,17},{... | collective-permute-start | bytes 2457608 | tf_op jit(solution)/shard_map/ppermute | solution.py:42
  29.7 17.7 %collective-permute-done.2.refs_1_ = bf16[640,640]{1,0:T(8,128)(2,1)} collective-permute-done((bf16[640,640]{1,0:T(8,128)(2,1)}, bf16[640,640]{1,0:T(8,128)(2,1)}, u32[]{:S(2)}, u32[]{:S(2)}) %collective-permute-start.2) | collective-permute-done | bytes 819232 | tf_op jit(solution)/shard_map/ppermute | solution.py:38
  48.7 2.2 %collective-permute-start.11 = (bf16[512,2560]{1,0:T(8,128)(2,1)}, bf16[512,2560]{1,0:T(8,128)(2,1)}, u32[]{:S(2)}, u32[]{:S(2)}) collective-permute-start(bf16[512,2560]{1,0:T(8,128)(2,1)} %get-tuple-element.53), channel_id=1, source_target_pairs={{1,2},{2,1},{5,6},{6,5},{9,10},{10,9},{13,14},{14,13},{17,18},{18,... | collective-permute-start | bytes 7864328 | tf_op jit(solution)/shard_map/ppermute | solution.py:38
  50.9 2.1 %broadcast_select_fusion.1.refs_1_ = bf16[640,640]{1,0:T(8,128)(2,1)} fusion(bf16[640,640]{1,0:T(8,128)(2,1)} %get-tuple-element.48, bf16[640,640]{1,0:T(8,128)(2,1)} %get-tuple-element.40, pred[]{:T(512)S(6)} %or.3), kind=kLoop, calls=%fused_computation.1 | loop fusion | flops 409600 | bytes 2457601 | tf_op jit(solution)/shard_map/jit(_where)/select_n | solution.py:283
  53.0 1.5 %collective-permute-start.7 = (bf16[640,640]{1,0:T(8,128)(2,1)}, bf16[640,640]{1,0:T(8,128)(2,1)}, u32[]{:S(2)}, u32[]{:S(2)}) collective-permute-start(bf16[640,640]{1,0:T(8,128)(2,1)} %broadcast_select_fusion.1.refs_1_), channel_id=1, source_target_pairs={{0,8},{4,20},{8,0},{12,28},{16,24},{20,4},{24,16},{28,12},{1,9},{5... | collective-permute-start | bytes 2457608 | tf_op jit(solution)/shard_map/ppermute | solution.py:42
  54.5 1.5 %collective-permute-start.8 = (bf16[640,640]{1,0:T(8,128)(2,1)}, bf16[640,640]{1,0:T(8,128)(2,1)}, u32[]{:S(2)}, u32[]{:S(2)}) collective-permute-start(bf16[640,640]{1,0:T(8,128)(2,1)} %broadcast_select_fusion.1.refs_1_), channel_id=1, source_target_pairs={{0,16},{4,12},{8,24},{12,4},{16,0},{20,28},{24,8},{28,20},{1,17},{... | collective-permute-start | bytes 2457608 | tf_op jit(solution)/shard_map/ppermute | solution.py:42
  56.5 13.5 %collective-permute-done.6.refs_1_ = bf16[640,640]{1,0:T(8,128)(2,1)} collective-permute-done((bf16[640,640]{1,0:T(8,128)(2,1)}, bf16[640,640]{1,0:T(8,128)(2,1)}, u32[]{:S(2)}, u32[]{:S(2)}) %collective-permute-start.6) | collective-permute-done | bytes 819232 | tf_op jit(solution)/shard_map/ppermute | solution.py:38
  70.0 2.1 %broadcast_select_fusion.refs_2_ = bf16[640,640]{1,0:T(8,128)(2,1)} fusion(bf16[640,640]{1,0:T(8,128)(2,1)} %get-tuple-element.56, bf16[640,640]{1,0:T(8,128)(2,1)} %get-tuple-element.46, pred[]{:T(512)S(6)} %or.3), kind=kLoop, calls=%fused_computation | loop fusion | flops 409600 | bytes 2457601 | tf_op jit(solution)/shard_map/jit(_where)/select_n | solution.py:289
  72.1 2.4 %collective-permute-done.7.refs_2_ = bf16[640,640]{1,0:T(8,128)(2,1)} collective-permute-done((bf16[640,640]{1,0:T(8,128)(2,1)}, bf16[640,640]{1,0:T(8,128)(2,1)}, u32[]{:S(2)}, u32[]{:S(2)}) %collective-permute-start.7) | collective-permute-done | bytes 819232 | tf_op jit(solution)/shard_map/ppermute | solution.py:42
  74.5 1.5 %collective-permute-start.13 = (bf16[640,640]{1,0:T(8,128)(2,1)}, bf16[640,640]{1,0:T(8,128)(2,1)}, u32[]{:S(2)}, u32[]{:S(2)}) collective-permute-start(bf16[640,640]{1,0:T(8,128)(2,1)} %broadcast_select_fusion.refs_2_), channel_id=1, source_target_pairs={{0,8},{4,20},{8,0},{12,28},{16,24},{20,4},{24,16},{28,12},{1,9},{5... | collective-permute-start | bytes 2457608 | tf_op jit(solution)/shard_map/ppermute | solution.py:42
  76.0 1.5 %collective-permute-start.14 = (bf16[640,640]{1,0:T(8,128)(2,1)}, bf16[640,640]{1,0:T(8,128)(2,1)}, u32[]{:S(2)}, u32[]{:S(2)}) collective-permute-start(bf16[640,640]{1,0:T(8,128)(2,1)} %broadcast_select_fusion.refs_2_), channel_id=1, source_target_pairs={{0,16},{4,12},{8,24},{12,4},{16,0},{20,28},{24,8},{28,20},{1,17},{... | collective-permute-start | bytes 2457608 | tf_op jit(solution)/shard_map/ppermute | solution.py:42
  77.5 11.1 %collective-permute-done.9.refs_7_ = bf16[640,640]{1,0:T(8,128)(2,1)} collective-permute-done((bf16[640,640]{1,0:T(8,128)(2,1)}, bf16[640,640]{1,0:T(8,128)(2,1)}, u32[]{:S(2)}, u32[]{:S(2)}) %collective-permute-start.9) | collective-permute-done | bytes 819232 | tf_op jit(solution)/shard_map/ppermute | solution.py:42
  88.6 1.5 %collective-permute-start.12 = (bf16[640,640]{1,0:T(8,128)(2,1)}, bf16[640,640]{1,0:T(8,128)(2,1)}, u32[]{:S(2)}, u32[]{:S(2)}) collective-permute-start(bf16[640,640]{1,0:T(8,128)(2,1)} %get-tuple-element.55.refs_16_), channel_id=1, source_target_pairs={{0,16},{4,12},{8,24},{12,4},{16,0},{20,28},{24,8},{28,20},{1,17},{... | collective-permute-start | bytes 2457608 | tf_op jit(solution)/shard_map/ppermute | solution.py:42
  90.2 5.8 %collective-permute-done.13.refs_5_.refs_3_ = bf16[640,640]{1,0:T(8,128)(2,1)} collective-permute-done((bf16[640,640]{1,0:T(8,128)(2,1)}, bf16[640,640]{1,0:T(8,128)(2,1)}, u32[]{:S(2)}, u32[]{:S(2)}) %collective-permute-start.13) | collective-permute-done | bytes 819232 | tf_op jit(solution)/shard_map/ppermute | solution.py:42
  96.0 2.1 %collective-permute-done.14.refs_6_.refs_4_ = bf16[640,640]{1,0:T(8,128)(2,1)} collective-permute-done((bf16[640,640]{1,0:T(8,128)(2,1)}, bf16[640,640]{1,0:T(8,128)(2,1)}, u32[]{:S(2)}, u32[]{:S(2)}) %collective-permute-start.14) | collective-permute-done | bytes 819232 | tf_op jit(solution)/shard_map/ppermute | solution.py:42
  98.1 1.4 collective-permute-start.16
  99.5 7.4 %collective-permute-done.12.refs_4_ = bf16[640,640]{1,0:T(8,128)(2,1)} collective-permute-done((bf16[640,640]{1,0:T(8,128)(2,1)}, bf16[640,640]{1,0:T(8,128)(2,1)}, u32[]{:S(2)}, u32[]{:S(2)}) %collective-permute-start.12) | collective-permute-done | bytes 819232 | tf_op jit(solution)/shard_map/ppermute | solution.py:42
  106.9 1.4 collective-permute-start.17
  108.3 4.2 %collective-permute-done.10.refs_1_ = bf16[512,1920]{1,0:T(8,128)(2,1)} collective-permute-done((bf16[512,1920]{1,0:T(8,128)(2,1)}, bf16[512,1920]{1,0:T(8,128)(2,1)}, u32[]{:S(2)}, u32[]{:S(2)}) %collective-permute-start.10) | collective-permute-done | bytes 1966112 | tf_op jit(solution)/shard_map/ppermute | solution.py:38
  113.6 1.6 %collective-permute-done.18.refs_14_ = bf16[640,640]{1,0:T(8,128)(2,1)} collective-permute-done((bf16[640,640]{1,0:T(8,128)(2,1)}, bf16[640,640]{1,0:T(8,128)(2,1)}, u32[]{:S(2)}, u32[]{:S(2)}) %collective-permute-start.18) | collective-permute-done | bytes 819232 | tf_op jit(solution)/shard_map/ppermute | solution.py:42
  115.1 1.5 %collective-permute-start.24 = (bf16[640,640]{1,0:T(8,128)(2,1)}, bf16[640,640]{1,0:T(8,128)(2,1)}, u32[]{:S(2)}, u32[]{:S(2)}) collective-permute-start(bf16[640,640]{1,0:T(8,128)(2,1)} %collective-permute-done.13.refs_5_.refs_3_), channel_id=1, source_target_pairs={{0,16},{4,12},{8,24},{12,4},{16,0},{20,28},{24,8},{28,20},{1,17},{... | collective-permute-start | bytes 2457608 | tf_op jit(solution)/shard_map/ppermute | solution.py:42
  116.7 1.7 %collective-permute-start.23 = (bf16[512,640]{1,0:T(8,128)(2,1)}, bf16[512,640]{1,0:T(8,128)(2,1)}, u32[]{:S(2)}, u32[]{:S(2)}) collective-permute-start(bf16[512,640]{1,0:T(8,128)(2,1)} %get-tuple-element.67), channel_id=1, source_target_pairs={{0,1},{1,0},{2,3},{3,2},{4,5},{5,4},{6,7},{7,6},{8,9},{9,8},{10,11... | collective-permute-start | bytes 1966088 | tf_op jit(solution)/shard_map/ppermute | solution.py:38
  120.0 16.3 %work_off_slots.2.refs_1_ = f32[256,5120]{1,0:T(8,128)} custom-call(s32[21]{0:T(128)} %concatenate.3.place, bf16[256,2560]{1,0:T(8,128)(2,1)} %query_ref.3, bf16[256,2560]{1,0:T(8,128)(2,1)} %key_ref.5, bf16[256,2560]{1,0:T(8,128)(2,1)} %value_ref.5, bf16[256,5120]{1,0:T(8,128)(2,1)} %base_ref.1, ...), custom_call_target="tpu_custom_call" | custom-call | flops 6543114240 | bytes 37027840 | tf_op jit(solution)/shard_map/work_off_slots/pallas_call | solution.py:206
  136.8 2.3 %collective-permute-done.28.refs_9_ = bf16[640,640]{1,0:T(8,128)(2,1)} collective-permute-done((bf16[640,640]{1,0:T(8,128)(2,1)}, bf16[640,640]{1,0:T(8,128)(2,1)}, u32[]{:S(2)}, u32[]{:S(2)}) %collective-permute-start.28) | collective-permute-done | bytes 819232 | tf_op jit(solution)/shard_map/ppermute | solution.py:42
  139.1 8.9 %work_off_slots.3 = bf16[256,5120]{1,0:T(8,128)(2,1)} custom-call(s32[21]{0:T(128)} %concatenate.3.place, bf16[256,2560]{1,0:T(8,128)(2,1)} %query_ref.3, bf16[256,2560]{1,0:T(8,128)(2,1)} %key_ref.5, bf16[256,2560]{1,0:T(8,128)(2,1)} %value_ref.5, f32[256,5120]{1,0:T(8,128)} %get-tuple-element.68.base_ref, bf16[512,640]{1,0:T(8,128)(2,1)} %get-tuple-element.69.refs_0_, ...), custom_call_target="tpu_custom_call" | custom-call | flops 2181038080 | bytes 19333120 | tf_op jit(solution)/shard_map/work_off_slots/pallas_call | solution.py:206
  (41 shorter events, 7.6 us)
Async XLA Ops:
  2.1 21.6 %collective-permute-start = (bf16[640,640]{1,0:T(8,128)(2,1)}, bf16[640,640]{1,0:T(8,128)(2,1)}, u32[]{:S(2)}, u32[]{:S(2)}) collective-permute-start(bf16[640,640]{1,0:T(8,128)(2,1)} %constant_dynamic-slice_fusion), channel_id=1, source_target_pairs={{0,1},{1,0},{2,3},{3,2},{4,5},{5,4},{6,7},{7,6},{8,9},{9,8},{10,11... | collective-permute-start | bytes 2457608 | tf_op jit(solution)/shard_map/ppermute | solution.py:38
  5.1 18.6 %collective-permute-start.1 = (bf16[640,640]{1,0:T(8,128)(2,1)}, bf16[640,640]{1,0:T(8,128)(2,1)}, u32[]{:S(2)}, u32[]{:S(2)}) collective-permute-start(bf16[640,640]{1,0:T(8,128)(2,1)} %constant_dynamic-slice_fusion), channel_id=1, source_target_pairs={{1,2},{2,1},{5,6},{6,5},{9,10},{10,9},{13,14},{14,13},{17,18},{18,... | collective-permute-start | bytes 2457608 | tf_op jit(solution)/shard_map/ppermute | solution.py:38
  23.7 23.7 %collective-permute-start.2 = (bf16[640,640]{1,0:T(8,128)(2,1)}, bf16[640,640]{1,0:T(8,128)(2,1)}, u32[]{:S(2)}, u32[]{:S(2)}) collective-permute-start(bf16[640,640]{1,0:T(8,128)(2,1)} %get-tuple-element.40), channel_id=1, source_target_pairs={{1,0},{2,3},{5,4},{6,7},{9,8},{10,11},{13,12},{14,15},{17,16},{18,... | collective-permute-start | bytes 2457608 | tf_op jit(solution)/shard_map/ppermute | solution.py:38
  25.0 22.4 %collective-permute-start.3 = (bf16[640,640]{1,0:T(8,128)(2,1)}, bf16[640,640]{1,0:T(8,128)(2,1)}, u32[]{:S(2)}, u32[]{:S(2)}) collective-permute-start(bf16[640,640]{1,0:T(8,128)(2,1)} %get-tuple-element.41.refs_4_), channel_id=1, source_target_pairs={{1,2},{2,1},{5,6},{6,5},{9,10},{10,9},{13,14},{14,13},{17,18},{18,... | collective-permute-start | bytes 2457608 | tf_op jit(solution)/shard_map/ppermute | solution.py:38
  26.6 28.0 %collective-permute-start.4 = (bf16[640,640]{1,0:T(8,128)(2,1)}, bf16[640,640]{1,0:T(8,128)(2,1)}, u32[]{:S(2)}, u32[]{:S(2)}) collective-permute-start(bf16[640,640]{1,0:T(8,128)(2,1)} %get-tuple-element.41.refs_4_), channel_id=1, source_target_pairs={{0,8},{4,20},{8,0},{12,28},{16,24},{20,4},{24,16},{28,12},{1,9},{5... | collective-permute-start | bytes 2457608 | tf_op jit(solution)/shard_map/ppermute | solution.py:42
  28.2 27.8 %collective-permute-start.5 = (bf16[640,640]{1,0:T(8,128)(2,1)}, bf16[640,640]{1,0:T(8,128)(2,1)}, u32[]{:S(2)}, u32[]{:S(2)}) collective-permute-start(bf16[640,640]{1,0:T(8,128)(2,1)} %get-tuple-element.41.refs_4_), channel_id=1, source_target_pairs={{0,16},{4,12},{8,24},{12,4},{16,0},{20,28},{24,8},{28,20},{1,17},{... | collective-permute-start | bytes 2457608 | tf_op jit(solution)/shard_map/ppermute | solution.py:42
  47.4 22.6 %collective-permute-start.6 = (bf16[640,640]{1,0:T(8,128)(2,1)}, bf16[640,640]{1,0:T(8,128)(2,1)}, u32[]{:S(2)}, u32[]{:S(2)}) collective-permute-start(bf16[640,640]{1,0:T(8,128)(2,1)} %get-tuple-element.46), channel_id=1, source_target_pairs={{1,0},{2,3},{5,4},{6,7},{9,8},{10,11},{13,12},{14,15},{17,16},{18,... | collective-permute-start | bytes 2457608 | tf_op jit(solution)/shard_map/ppermute | solution.py:38
  48.7 63.7 %collective-permute-start.11 = (bf16[512,2560]{1,0:T(8,128)(2,1)}, bf16[512,2560]{1,0:T(8,128)(2,1)}, u32[]{:S(2)}, u32[]{:S(2)}) collective-permute-start(bf16[512,2560]{1,0:T(8,128)(2,1)} %get-tuple-element.53), channel_id=1, source_target_pairs={{1,2},{2,1},{5,6},{6,5},{9,10},{10,9},{13,14},{14,13},{17,18},{18,... | collective-permute-start | bytes 7864328 | tf_op jit(solution)/shard_map/ppermute | solution.py:38
  53.0 21.5 %collective-permute-start.7 = (bf16[640,640]{1,0:T(8,128)(2,1)}, bf16[640,640]{1,0:T(8,128)(2,1)}, u32[]{:S(2)}, u32[]{:S(2)}) collective-permute-start(bf16[640,640]{1,0:T(8,128)(2,1)} %broadcast_select_fusion.1.refs_1_), channel_id=1, source_target_pairs={{0,8},{4,20},{8,0},{12,28},{16,24},{20,4},{24,16},{28,12},{1,9},{5... | collective-permute-start | bytes 2457608 | tf_op jit(solution)/shard_map/ppermute | solution.py:42
  54.5 21.5 %collective-permute-start.8 = (bf16[640,640]{1,0:T(8,128)(2,1)}, bf16[640,640]{1,0:T(8,128)(2,1)}, u32[]{:S(2)}, u32[]{:S(2)}) collective-permute-start(bf16[640,640]{1,0:T(8,128)(2,1)} %broadcast_select_fusion.1.refs_1_), channel_id=1, source_target_pairs={{0,16},{4,12},{8,24},{12,4},{16,0},{20,28},{24,8},{28,20},{1,17},{... | collective-permute-start | bytes 2457608 | tf_op jit(solution)/shard_map/ppermute | solution.py:42
  56.0 32.6 %collective-permute-start.9 = (bf16[640,640]{1,0:T(8,128)(2,1)}, bf16[640,640]{1,0:T(8,128)(2,1)}, u32[]{:S(2)}, u32[]{:S(2)}) collective-permute-start(bf16[640,640]{1,0:T(8,128)(2,1)} %get-tuple-element.49.refs_5_), channel_id=1, source_target_pairs={{0,16},{4,12},{8,24},{12,4},{16,0},{20,28},{24,8},{28,20},{1,17},{... | collective-permute-start | bytes 2457608 | tf_op jit(solution)/shard_map/ppermute | solution.py:42
  70.0 42.4 %collective-permute-start.10 = (bf16[512,1920]{1,0:T(8,128)(2,1)}, bf16[512,1920]{1,0:T(8,128)(2,1)}, u32[]{:S(2)}, u32[]{:S(2)}) collective-permute-start(bf16[512,1920]{1,0:T(8,128)(2,1)} %get-tuple-element.52), channel_id=1, source_target_pairs={{0,1},{1,0},{2,3},{3,2},{4,5},{5,4},{6,7},{7,6},{8,9},{9,8},{10,11... | collective-permute-start | bytes 5898248 | tf_op jit(solution)/shard_map/ppermute | solution.py:38
  74.5 21.5 %collective-permute-start.13 = (bf16[640,640]{1,0:T(8,128)(2,1)}, bf16[640,640]{1,0:T(8,128)(2,1)}, u32[]{:S(2)}, u32[]{:S(2)}) collective-permute-start(bf16[640,640]{1,0:T(8,128)(2,1)} %broadcast_select_fusion.refs_2_), channel_id=1, source_target_pairs={{0,8},{4,20},{8,0},{12,28},{16,24},{20,4},{24,16},{28,12},{1,9},{5... | collective-permute-start | bytes 2457608 | tf_op jit(solution)/shard_map/ppermute | solution.py:42
  76.0 22.1 %collective-permute-start.14 = (bf16[640,640]{1,0:T(8,128)(2,1)}, bf16[640,640]{1,0:T(8,128)(2,1)}, u32[]{:S(2)}, u32[]{:S(2)}) collective-permute-start(bf16[640,640]{1,0:T(8,128)(2,1)} %broadcast_select_fusion.refs_2_), channel_id=1, source_target_pairs={{0,16},{4,12},{8,24},{12,4},{16,0},{20,28},{24,8},{28,20},{1,17},{... | collective-permute-start | bytes 2457608 | tf_op jit(solution)/shard_map/ppermute | solution.py:42
  88.6 18.3 %collective-permute-start.12 = (bf16[640,640]{1,0:T(8,128)(2,1)}, bf16[640,640]{1,0:T(8,128)(2,1)}, u32[]{:S(2)}, u32[]{:S(2)}) collective-permute-start(bf16[640,640]{1,0:T(8,128)(2,1)} %get-tuple-element.55.refs_16_), channel_id=1, source_target_pairs={{0,16},{4,12},{8,24},{12,4},{16,0},{20,28},{24,8},{28,20},{1,17},{... | collective-permute-start | bytes 2457608 | tf_op jit(solution)/shard_map/ppermute | solution.py:42
  96.0 17.0 %collective-permute-start.15 = (bf16[640,640]{1,0:T(8,128)(2,1)}, bf16[640,640]{1,0:T(8,128)(2,1)}, u32[]{:S(2)}, u32[]{:S(2)}) collective-permute-start(bf16[640,640]{1,0:T(8,128)(2,1)} %get-tuple-element.60.refs_7_), channel_id=1, source_target_pairs={{0,4},{4,0},{8,12},{12,8},{16,20},{20,16},{24,28},{28,24},{1,5},{5... | collective-permute-start | bytes 2457608 | tf_op jit(solution)/shard_map/ppermute | solution.py:42
  98.1 14.9 %collective-permute-start.16 = (bf16[640,640]{1,0:T(8,128)(2,1)}, bf16[640,640]{1,0:T(8,128)(2,1)}, u32[]{:S(2)}, u32[]{:S(2)}) collective-permute-start(bf16[640,640]{1,0:T(8,128)(2,1)} %get-tuple-element.61.refs_8_), channel_id=1, source_target_pairs={{0,4},{4,0},{8,12},{12,8},{16,20},{20,16},{24,28},{28,24},{1,5},{5... | collective-permute-start | bytes 2457608 | tf_op jit(solution)/shard_map/ppermute | solution.py:42
  106.9 6.6 %collective-permute-start.17 = (bf16[640,640]{1,0:T(8,128)(2,1)}, bf16[640,640]{1,0:T(8,128)(2,1)}, u32[]{:S(2)}, u32[]{:S(2)}) collective-permute-start(bf16[640,640]{1,0:T(8,128)(2,1)} %get-tuple-element.62.refs_9_), channel_id=1, source_target_pairs={{0,4},{4,0},{8,12},{12,8},{16,20},{20,16},{24,28},{28,24},{1,5},{5... | collective-permute-start | bytes 2457608 | tf_op jit(solution)/shard_map/ppermute | solution.py:42
  112.5 2.7 %collective-permute-start.18 = (bf16[640,640]{1,0:T(8,128)(2,1)}, bf16[640,640]{1,0:T(8,128)(2,1)}, u32[]{:S(2)}, u32[]{:S(2)}) collective-permute-start(bf16[640,640]{1,0:T(8,128)(2,1)} %get-tuple-element.63.refs_10_), channel_id=1, source_target_pairs={{0,4},{4,0},{8,12},{12,8},{16,20},{20,16},{24,28},{28,24},{1,5},{5... | collective-permute-start | bytes 2457608 | tf_op jit(solution)/shard_map/ppermute | solution.py:42
  112.5 4.2 %collective-permute-start.19 = (bf16[640,640]{1,0:T(8,128)(2,1)}, bf16[640,640]{1,0:T(8,128)(2,1)}, u32[]{:S(2)}, u32[]{:S(2)}) collective-permute-start(bf16[640,640]{1,0:T(8,128)(2,1)} %get-tuple-element.64.refs_15_), channel_id=1, source_target_pairs={{0,4},{4,0},{8,12},{12,8},{16,20},{20,16},{24,28},{28,24},{1,5},{5... | collective-permute-start | bytes 2457608 | tf_op jit(solution)/shard_map/ppermute | solution.py:42
  113.0 5.4 %collective-permute-start.20 = (bf16[640,640]{1,0:T(8,128)(2,1)}, bf16[640,640]{1,0:T(8,128)(2,1)}, u32[]{:S(2)}, u32[]{:S(2)}) collective-permute-start(bf16[640,640]{1,0:T(8,128)(2,1)} %get-tuple-element.55.refs_16_), channel_id=1, source_target_pairs={{0,4},{4,0},{8,12},{12,8},{16,20},{20,16},{24,28},{28,24},{1,5},{5... | collective-permute-start | bytes 2457608 | tf_op jit(solution)/shard_map/ppermute | solution.py:42
  113.0 5.6 %collective-permute-start.21 = (bf16[640,640]{1,0:T(8,128)(2,1)}, bf16[640,640]{1,0:T(8,128)(2,1)}, u32[]{:S(2)}, u32[]{:S(2)}) collective-permute-start(bf16[640,640]{1,0:T(8,128)(2,1)} %get-tuple-element.65.refs_17_), channel_id=1, source_target_pairs={{0,4},{4,0},{8,12},{12,8},{16,20},{20,16},{24,28},{28,24},{1,5},{5... | collective-permute-start | bytes 2457608 | tf_op jit(solution)/shard_map/ppermute | solution.py:42
  113.5 6.3 %collective-permute-start.22 = (bf16[640,640]{1,0:T(8,128)(2,1)}, bf16[640,640]{1,0:T(8,128)(2,1)}, u32[]{:S(2)}, u32[]{:S(2)}) collective-permute-start(bf16[640,640]{1,0:T(8,128)(2,1)} %get-tuple-element.66.refs_18_), channel_id=1, source_target_pairs={{0,4},{4,0},{8,12},{12,8},{16,20},{20,16},{24,28},{28,24},{1,5},{5... | collective-permute-start | bytes 2457608 | tf_op jit(solution)/shard_map/ppermute | solution.py:42
  115.1 21.1 %collective-permute-start.24 = (bf16[640,640]{1,0:T(8,128)(2,1)}, bf16[640,640]{1,0:T(8,128)(2,1)}, u32[]{:S(2)}, u32[]{:S(2)}) collective-permute-start(bf16[640,640]{1,0:T(8,128)(2,1)} %collective-permute-done.13.refs_5_.refs_3_), channel_id=1, source_target_pairs={{0,16},{4,12},{8,24},{12,4},{16,0},{20,28},{24,8},{28,20},{1,17},{... | collective-permute-start | bytes 2457608 | tf_op jit(solution)/shard_map/ppermute | solution.py:42
  116.7 19.6 %collective-permute-start.23 = (bf16[512,640]{1,0:T(8,128)(2,1)}, bf16[512,640]{1,0:T(8,128)(2,1)}, u32[]{:S(2)}, u32[]{:S(2)}) collective-permute-start(bf16[512,640]{1,0:T(8,128)(2,1)} %get-tuple-element.67), channel_id=1, source_target_pairs={{0,1},{1,0},{2,3},{3,2},{4,5},{5,4},{6,7},{7,6},{8,9},{9,8},{10,11... | collective-permute-start | bytes 1966088 | tf_op jit(solution)/shard_map/ppermute | solution.py:38
  118.4 18.4 %collective-permute-start.25 = (bf16[640,640]{1,0:T(8,128)(2,1)}, bf16[640,640]{1,0:T(8,128)(2,1)}, u32[]{:S(2)}, u32[]{:S(2)}) collective-permute-start(bf16[640,640]{1,0:T(8,128)(2,1)} %broadcast_select_fusion.refs_2_), channel_id=1, source_target_pairs={{0,4},{4,0},{8,12},{12,8},{16,20},{20,16},{24,28},{28,24},{1,5},{5... | collective-permute-start | bytes 2457608 | tf_op jit(solution)/shard_map/ppermute | solution.py:42
  118.6 18.1 %collective-permute-start.26 = (bf16[640,640]{1,0:T(8,128)(2,1)}, bf16[640,640]{1,0:T(8,128)(2,1)}, u32[]{:S(2)}, u32[]{:S(2)}) collective-permute-start(bf16[640,640]{1,0:T(8,128)(2,1)} %collective-permute-done.13.refs_5_.refs_3_), channel_id=1, source_target_pairs={{0,4},{4,0},{8,12},{12,8},{16,20},{20,16},{24,28},{28,24},{1,5},{5... | collective-permute-start | bytes 2457608 | tf_op jit(solution)/shard_map/ppermute | solution.py:42
  119.8 17.0 %collective-permute-start.27 = (bf16[640,640]{1,0:T(8,128)(2,1)}, bf16[640,640]{1,0:T(8,128)(2,1)}, u32[]{:S(2)}, u32[]{:S(2)}) collective-permute-start(bf16[640,640]{1,0:T(8,128)(2,1)} %collective-permute-done.14.refs_6_.refs_4_), channel_id=1, source_target_pairs={{0,4},{4,0},{8,12},{12,8},{16,20},{20,16},{24,28},{28,24},{1,5},{5... | collective-permute-start | bytes 2457608 | tf_op jit(solution)/shard_map/ppermute | solution.py:42
  136.3 2.8 %collective-permute-start.28 = (bf16[640,640]{1,0:T(8,128)(2,1)}, bf16[640,640]{1,0:T(8,128)(2,1)}, u32[]{:S(2)}, u32[]{:S(2)}) collective-permute-start(bf16[640,640]{1,0:T(8,128)(2,1)} %get-tuple-element.70.refs_5_), channel_id=1, source_target_pairs={{0,4},{4,0},{8,12},{12,8},{16,20},{20,16},{24,28},{28,24},{1,5},{5... | collective-permute-start | bytes 2457608 | tf_op jit(solution)/shard_map/ppermute | solution.py:42

commit v6 on v5

--- a/solution.py
+++ b/solution.py
@@ -175,7 +175,7 @@
             part = ref.at[:, pl.ds(side_at[at][nth] * depth, depth)]
             found.append(begin(part, beside.at[at, nth], own_sems.at[at, 3 + nth]))
         frames.append(found)
-    blocks, ahead = [], LANES // (len(slots) + 1)
+    blocks, ahead = [], 3 if len(slots) > 1 else LANES // 2
     for at in range(len(slots)):
         for copy in frames[at]:
             copy.wait()
@@ -183,7 +183,7 @@
             blocks += [begin_block(nth) for nth in range(ahead)]
         part = context.at[:, pl.ds(at * depth, depth)]
         attend(place[HAS_MIDDLE] > 0, *(own.at[at, nth] for nth in range(3)), beside.at[at, 0], beside.at[at, 1], part)
-        until = LANES if at == len(slots) - 1 else ahead * (at + 2)
+        until = LANES if at == len(slots) - 1 else min(LANES, ahead * (at + 2))
         blocks += [begin_block(nth) for nth in range(len(blocks), until)]
     leaving = []
     for nth in range(LANES):

time: 149 us -> 149 us (level)
  no operation moved by 1% of the time
where the time goes in v6:
time: 149 us; the launch traced here: 148 us
  waiting for transfers between devices  79.7 us (53%)
  Pallas kernels  30.3 us (20%)
  starting transfers between devices  30.2 us (20%)
  other arithmetic  4.91 us (3%)
  local copies, waits for them, and re-layouts  2.74 us (2%)
    ppermute x8, waiting for transfers between devices, along_line(): return lax.ppermute(value, ('dp', 'ctx'), pairs)  45.9 us
    ppermute x21, waiting for transfers between devices, in_plane(): lax.ppermute(value, 'dp', [(lane, lane ^ masks[lane % 2]) for lane in ran...  33.8 us
    pallas_call x2, Pallas kernels, worked_off(): pl.pallas_call(kernel, out_shape=jax.ShapeDtypeStruct(base.shape, dtype),...  25.2 us
    ppermute x21, starting transfers between devices, in_plane(): lax.ppermute(value, 'dp', [(lane, lane ^ masks[lane % 2]) for lane in ran...  17.6 us
    ppermute x8, starting transfers between devices, along_line(): return lax.ppermute(value, ('dp', 'ctx'), pairs)  12.6 us
    pallas_call x1, Pallas kernels, packed(): pl.pallas_call(pack_kernel, out_shape=shapes, grid_spec=pltpu.PrefetchSca...  5.13 us
  transfers between devices with their start and end apart: 29, of which 13 were waited for; matrix products, arithmetic and copies ran while one was open for 4% of the time, Pallas kernels for 14%

profile of v6, /device:TPU:0, one launch (start us, length us, event | category | flops | bytes accessed | tf_op | source)
XLA Modules:
  0.0 148.1 jit_solution(16318600354896829876)
XLA Ops:
  0.0 2.1 %constant_dynamic-slice_fusion = bf16[640,640]{1,0:T(8,128)(2,1)} fusion(bf16[640,5120]{1,0:T(8,128)(2,1)} %refs_6_.1, s32[]{:T(128)S(6)} %select_n.30), kind=kLoop, calls=%fused_computation.7 | loop fusion | bytes 1638404 | tf_op jit(solution)/shard_map/dynamic_slice | solution.py:253
  2.1 3.0 %collective-permute-start = (bf16[640,640]{1,0:T(8,128)(2,1)}, bf16[640,640]{1,0:T(8,128)(2,1)}, u32[]{:S(2)}, u32[]{:S(2)}) collective-permute-start(bf16[640,640]{1,0:T(8,128)(2,1)} %constant_dynamic-slice_fusion), channel_id=1, source_target_pairs={{0,1},{1,0},{2,3},{3,2},{4,5},{5,4},{6,7},{7,6},{8,9},{9,8},{10,11... | collective-permute-start | bytes 2457608 | tf_op jit(solution)/shard_map/ppermute | solution.py:38
  5.1 1.6 %collective-permute-start.1 = (bf16[640,640]{1,0:T(8,128)(2,1)}, bf16[640,640]{1,0:T(8,128)(2,1)}, u32[]{:S(2)}, u32[]{:S(2)}) collective-permute-start(bf16[640,640]{1,0:T(8,128)(2,1)} %constant_dynamic-slice_fusion), channel_id=1, source_target_pairs={{1,2},{2,1},{5,6},{6,5},{9,10},{10,9},{13,14},{14,13},{17,18},{18,... | collective-permute-start | bytes 2457608 | tf_op jit(solution)/shard_map/ppermute | solution.py:38
  8.0 5.1 %pack_window.1 = (f32[8,128]{1,0:T(8,128)}, bf16[512,1920]{1,0:T(8,128)(2,1)}, bf16[512,640]{1,0:T(8,128)(2,1)}, bf16[512,2560]{1,0:T(8,128)(2,1)}) custom-call(s32[21]{0:T(128)} %concatenate.3.place, bf16[256,2560]{1,0:T(8,128)(2,1)} %key_ref.5, bf16[256,2560]{1,0:T(8,128)(2,1)} %value_ref.5), custom_call_target="tpu_custom_call" | custom-call | tf_op jit(solution)/shard_map/pack_window/pallas_call | solution.py:106
  13.1 10.6 %collective-permute-done.refs_1_ = bf16[640,640]{1,0:T(8,128)(2,1)} collective-permute-done((bf16[640,640]{1,0:T(8,128)(2,1)}, bf16[640,640]{1,0:T(8,128)(2,1)}, u32[]{:S(2)}, u32[]{:S(2)}) %collective-permute-start) | collective-permute-done | bytes 819232 | tf_op jit(solution)/shard_map/ppermute | solution.py:38
  25.0 1.6 %collective-permute-start.3 = (bf16[640,640]{1,0:T(8,128)(2,1)}, bf16[640,640]{1,0:T(8,128)(2,1)}, u32[]{:S(2)}, u32[]{:S(2)}) collective-permute-start(bf16[640,640]{1,0:T(8,128)(2,1)} %get-tuple-element.41.refs_4_), channel_id=1, source_target_pairs={{1,2},{2,1},{5,6},{6,5},{9,10},{10,9},{13,14},{14,13},{17,18},{18,... | collective-permute-start | bytes 2457608 | tf_op jit(solution)/shard_map/ppermute | solution.py:38
  26.6 1.7 %collective-permute-start.4 = (bf16[640,640]{1,0:T(8,128)(2,1)}, bf16[640,640]{1,0:T(8,128)(2,1)}, u32[]{:S(2)}, u32[]{:S(2)}) collective-permute-start(bf16[640,640]{1,0:T(8,128)(2,1)} %get-tuple-element.41.refs_4_), channel_id=1, source_target_pairs={{0,8},{4,20},{8,0},{12,28},{16,24},{20,4},{24,16},{28,12},{1,9},{5... | collective-permute-start | bytes 2457608 | tf_op jit(solution)/shard_map/ppermute | solution.py:42
  28.2 1.5 %collective-permute-start.5 = (bf16[640,640]{1,0:T(8,128)(2,1)}, bf16[640,640]{1,0:T(8,128)(2,1)}, u32[]{:S(2)}, u32[]{:S(2)}) collective-permute-start(bf16[640,640]{1,0:T(8,128)(2,1)} %get-tuple-element.41.refs_4_), channel_id=1, source_target_pairs={{0,16},{4,12},{8,24},{12,4},{16,0},{20,28},{24,8},{28,20},{1,17},{... | collective-permute-start | bytes 2457608 | tf_op jit(solution)/shard_map/ppermute | solution.py:42
  29.7 17.7 %collective-permute-done.2.refs_1_ = bf16[640,640]{1,0:T(8,128)(2,1)} collective-permute-done((bf16[640,640]{1,0:T(8,128)(2,1)}, bf16[640,640]{1,0:T(8,128)(2,1)}, u32[]{:S(2)}, u32[]{:S(2)}) %collective-permute-start.2) | collective-permute-done | bytes 819232 | tf_op jit(solution)/shard_map/ppermute | solution.py:38
  48.7 2.2 %collective-permute-start.11 = (bf16[512,2560]{1,0:T(8,128)(2,1)}, bf16[512,2560]{1,0:T(8,128)(2,1)}, u32[]{:S(2)}, u32[]{:S(2)}) collective-permute-start(bf16[512,2560]{1,0:T(8,128)(2,1)} %get-tuple-element.53), channel_id=1, source_target_pairs={{1,2},{2,1},{5,6},{6,5},{9,10},{10,9},{13,14},{14,13},{17,18},{18,... | collective-permute-start | bytes 7864328 | tf_op jit(solution)/shard_map/ppermute | solution.py:38
  50.9 2.1 %broadcast_select_fusion.1.refs_1_ = bf16[640,640]{1,0:T(8,128)(2,1)} fusion(bf16[640,640]{1,0:T(8,128)(2,1)} %get-tuple-element.48, bf16[640,640]{1,0:T(8,128)(2,1)} %get-tuple-element.40, pred[]{:T(512)S(6)} %or.3), kind=kLoop, calls=%fused_computation.1 | loop fusion | flops 409600 | bytes 2457601 | tf_op jit(solution)/shard_map/jit(_where)/select_n | solution.py:283
  53.0 1.5 %collective-permute-start.7 = (bf16[640,640]{1,0:T(8,128)(2,1)}, bf16[640,640]{1,0:T(8,128)(2,1)}, u32[]{:S(2)}, u32[]{:S(2)}) collective-permute-start(bf16[640,640]{1,0:T(8,128)(2,1)} %broadcast_select_fusion.1.refs_1_), channel_id=1, source_target_pairs={{0,8},{4,20},{8,0},{12,28},{16,24},{20,4},{24,16},{28,12},{1,9},{5... | collective-permute-start | bytes 2457608 | tf_op jit(solution)/shard_map/ppermute | solution.py:42
  54.5 1.5 %collective-permute-start.8 = (bf16[640,640]{1,0:T(8,128)(2,1)}, bf16[640,640]{1,0:T(8,128)(2,1)}, u32[]{:S(2)}, u32[]{:S(2)}) collective-permute-start(bf16[640,640]{1,0:T(8,128)(2,1)} %broadcast_select_fusion.1.refs_1_), channel_id=1, source_target_pairs={{0,16},{4,12},{8,24},{12,4},{16,0},{20,28},{24,8},{28,20},{1,17},{... | collective-permute-start | bytes 2457608 | tf_op jit(solution)/shard_map/ppermute | solution.py:42
  56.5 13.5 %collective-permute-done.6.refs_1_ = bf16[640,640]{1,0:T(8,128)(2,1)} collective-permute-done((bf16[640,640]{1,0:T(8,128)(2,1)}, bf16[640,640]{1,0:T(8,128)(2,1)}, u32[]{:S(2)}, u32[]{:S(2)}) %collective-permute-start.6) | collective-permute-done | bytes 819232 | tf_op jit(solution)/shard_map/ppermute | solution.py:38
  70.0 2.1 %broadcast_select_fusion.refs_2_ = bf16[640,640]{1,0:T(8,128)(2,1)} fusion(bf16[640,640]{1,0:T(8,128)(2,1)} %get-tuple-element.56, bf16[640,640]{1,0:T(8,128)(2,1)} %get-tuple-element.46, pred[]{:T(512)S(6)} %or.3), kind=kLoop, calls=%fused_computation | loop fusion | flops 409600 | bytes 2457601 | tf_op jit(solution)/shard_map/jit(_where)/select_n | solution.py:289
  72.1 2.4 %collective-permute-done.7.refs_2_ = bf16[640,640]{1,0:T(8,128)(2,1)} collective-permute-done((bf16[640,640]{1,0:T(8,128)(2,1)}, bf16[640,640]{1,0:T(8,128)(2,1)}, u32[]{:S(2)}, u32[]{:S(2)}) %collective-permute-start.7) | collective-permute-done | bytes 819232 | tf_op jit(solution)/shard_map/ppermute | solution.py:42
  74.5 1.5 %collective-permute-start.13 = (bf16[640,640]{1,0:T(8,128)(2,1)}, bf16[640,640]{1,0:T(8,128)(2,1)}, u32[]{:S(2)}, u32[]{:S(2)}) collective-permute-start(bf16[640,640]{1,0:T(8,128)(2,1)} %broadcast_select_fusion.refs_2_), channel_id=1, source_target_pairs={{0,8},{4,20},{8,0},{12,28},{16,24},{20,4},{24,16},{28,12},{1,9},{5... | collective-permute-start | bytes 2457608 | tf_op jit(solution)/shard_map/ppermute | solution.py:42
  76.0 1.5 %collective-permute-start.14 = (bf16[640,640]{1,0:T(8,128)(2,1)}, bf16[640,640]{1,0:T(8,128)(2,1)}, u32[]{:S(2)}, u32[]{:S(2)}) collective-permute-start(bf16[640,640]{1,0:T(8,128)(2,1)} %broadcast_select_fusion.refs_2_), channel_id=1, source_target_pairs={{0,16},{4,12},{8,24},{12,4},{16,0},{20,28},{24,8},{28,20},{1,17},{... | collective-permute-start | bytes 2457608 | tf_op jit(solution)/shard_map/ppermute | solution.py:42
  77.5 11.1 %collective-permute-done.9.refs_7_ = bf16[640,640]{1,0:T(8,128)(2,1)} collective-permute-done((bf16[640,640]{1,0:T(8,128)(2,1)}, bf16[640,640]{1,0:T(8,128)(2,1)}, u32[]{:S(2)}, u32[]{:S(2)}) %collective-permute-start.9) | collective-permute-done | bytes 819232 | tf_op jit(solution)/shard_map/ppermute | solution.py:42
  88.6 1.5 %collective-permute-start.12 = (bf16[640,640]{1,0:T(8,128)(2,1)}, bf16[640,640]{1,0:T(8,128)(2,1)}, u32[]{:S(2)}, u32[]{:S(2)}) collective-permute-start(bf16[640,640]{1,0:T(8,128)(2,1)} %get-tuple-element.55.refs_16_), channel_id=1, source_target_pairs={{0,16},{4,12},{8,24},{12,4},{16,0},{20,28},{24,8},{28,20},{1,17},{... | collective-permute-start | bytes 2457608 | tf_op jit(solution)/shard_map/ppermute | solution.py:42
  90.2 5.8 %collective-permute-done.13.refs_5_.refs_3_ = bf16[640,640]{1,0:T(8,128)(2,1)} collective-permute-done((bf16[640,640]{1,0:T(8,128)(2,1)}, bf16[640,640]{1,0:T(8,128)(2,1)}, u32[]{:S(2)}, u32[]{:S(2)}) %collective-permute-start.13) | collective-permute-done | bytes 819232 | tf_op jit(solution)/shard_map/ppermute | solution.py:42
  96.0 2.1 %collective-permute-done.14.refs_6_.refs_4_ = bf16[640,640]{1,0:T(8,128)(2,1)} collective-permute-done((bf16[640,640]{1,0:T(8,128)(2,1)}, bf16[640,640]{1,0:T(8,128)(2,1)}, u32[]{:S(2)}, u32[]{:S(2)}) %collective-permute-start.14) | collective-permute-done | bytes 819232 | tf_op jit(solution)/shard_map/ppermute | solution.py:42
  98.1 1.4 collective-permute-start.16
  99.5 7.4 %collective-permute-done.12.refs_4_ = bf16[640,640]{1,0:T(8,128)(2,1)} collective-permute-done((bf16[640,640]{1,0:T(8,128)(2,1)}, bf16[640,640]{1,0:T(8,128)(2,1)}, u32[]{:S(2)}, u32[]{:S(2)}) %collective-permute-start.12) | collective-permute-done | bytes 819232 | tf_op jit(solution)/shard_map/ppermute | solution.py:42
  106.9 1.4 collective-permute-start.17
  108.3 4.2 %collective-permute-done.10.refs_1_ = bf16[512,1920]{1,0:T(8,128)(2,1)} collective-permute-done((bf16[512,1920]{1,0:T(8,128)(2,1)}, bf16[512,1920]{1,0:T(8,128)(2,1)}, u32[]{:S(2)}, u32[]{:S(2)}) %collective-permute-start.10) | collective-permute-done | bytes 1966112 | tf_op jit(solution)/shard_map/ppermute | solution.py:38
  113.6 1.6 %collective-permute-done.18.refs_14_ = bf16[640,640]{1,0:T(8,128)(2,1)} collective-permute-done((bf16[640,640]{1,0:T(8,128)(2,1)}, bf16[640,640]{1,0:T(8,128)(2,1)}, u32[]{:S(2)}, u32[]{:S(2)}) %collective-permute-start.18) | collective-permute-done | bytes 819232 | tf_op jit(solution)/shard_map/ppermute | solution.py:42
  115.1 1.5 %collective-permute-start.24 = (bf16[640,640]{1,0:T(8,128)(2,1)}, bf16[640,640]{1,0:T(8,128)(2,1)}, u32[]{:S(2)}, u32[]{:S(2)}) collective-permute-start(bf16[640,640]{1,0:T(8,128)(2,1)} %collective-permute-done.13.refs_5_.refs_3_), channel_id=1, source_target_pairs={{0,16},{4,12},{8,24},{12,4},{16,0},{20,28},{24,8},{28,20},{1,17},{... | collective-permute-start | bytes 2457608 | tf_op jit(solution)/shard_map/ppermute | solution.py:42
  116.7 1.7 %collective-permute-start.23 = (bf16[512,640]{1,0:T(8,128)(2,1)}, bf16[512,640]{1,0:T(8,128)(2,1)}, u32[]{:S(2)}, u32[]{:S(2)}) collective-permute-start(bf16[512,640]{1,0:T(8,128)(2,1)} %get-tuple-element.67), channel_id=1, source_target_pairs={{0,1},{1,0},{2,3},{3,2},{4,5},{5,4},{6,7},{7,6},{8,9},{9,8},{10,11... | collective-permute-start | bytes 1966088 | tf_op jit(solution)/shard_map/ppermute | solution.py:38
  120.0 16.3 %work_off_slots.2.refs_1_ = f32[256,5120]{1,0:T(8,128)} custom-call(s32[21]{0:T(128)} %concatenate.3.place, bf16[256,2560]{1,0:T(8,128)(2,1)} %query_ref.3, bf16[256,2560]{1,0:T(8,128)(2,1)} %key_ref.5, bf16[256,2560]{1,0:T(8,128)(2,1)} %value_ref.5, bf16[256,5120]{1,0:T(8,128)(2,1)} %base_ref.1, ...), custom_call_target="tpu_custom_call" | custom-call | flops 6543114240 | bytes 37027840 | tf_op jit(solution)/shard_map/work_off_slots/pallas_call | solution.py:206
  136.8 2.3 %collective-permute-done.28.refs_9_ = bf16[640,640]{1,0:T(8,128)(2,1)} collective-permute-done((bf16[640,640]{1,0:T(8,128)(2,1)}, bf16[640,640]{1,0:T(8,128)(2,1)}, u32[]{:S(2)}, u32[]{:S(2)}) %collective-permute-start.28) | collective-permute-done | bytes 819232 | tf_op jit(solution)/shard_map/ppermute | solution.py:42
  139.1 8.9 %work_off_slots.3 = bf16[256,5120]{1,0:T(8,128)(2,1)} custom-call(s32[21]{0:T(128)} %concatenate.3.place, bf16[256,2560]{1,0:T(8,128)(2,1)} %query_ref.3, bf16[256,2560]{1,0:T(8,128)(2,1)} %key_ref.5, bf16[256,2560]{1,0:T(8,128)(2,1)} %value_ref.5, f32[256,5120]{1,0:T(8,128)} %get-tuple-element.68.base_ref, bf16[512,640]{1,0:T(8,128)(2,1)} %get-tuple-element.69.refs_0_, ...), custom_call_target="tpu_custom_call" | custom-call | flops 2181038080 | bytes 19333120 | tf_op jit(solution)/shard_map/work_off_slots/pallas_call | solution.py:206
  (41 shorter events, 7.6 us)
Async XLA Ops:
  2.1 21.6 %collective-permute-start = (bf16[640,640]{1,0:T(8,128)(2,1)}, bf16[640,640]{1,0:T(8,128)(2,1)}, u32[]{:S(2)}, u32[]{:S(2)}) collective-permute-start(bf16[640,640]{1,0:T(8,128)(2,1)} %constant_dynamic-slice_fusion), channel_id=1, source_target_pairs={{0,1},{1,0},{2,3},{3,2},{4,5},{5,4},{6,7},{7,6},{8,9},{9,8},{10,11... | collective-permute-start | bytes 2457608 | tf_op jit(solution)/shard_map/ppermute | solution.py:38
  5.1 18.6 %collective-permute-start.1 = (bf16[640,640]{1,0:T(8,128)(2,1)}, bf16[640,640]{1,0:T(8,128)(2,1)}, u32[]{:S(2)}, u32[]{:S(2)}) collective-permute-start(bf16[640,640]{1,0:T(8,128)(2,1)} %constant_dynamic-slice_fusion), channel_id=1, source_target_pairs={{1,2},{2,1},{5,6},{6,5},{9,10},{10,9},{13,14},{14,13},{17,18},{18,... | collective-permute-start | bytes 2457608 | tf_op jit(solution)/shard_map/ppermute | solution.py:38
  23.7 23.7 %collective-permute-start.2 = (bf16[640,640]{1,0:T(8,128)(2,1)}, bf16[640,640]{1,0:T(8,128)(2,1)}, u32[]{:S(2)}, u32[]{:S(2)}) collective-permute-start(bf16[640,640]{1,0:T(8,128)(2,1)} %get-tuple-element.40), channel_id=1, source_target_pairs={{1,0},{2,3},{5,4},{6,7},{9,8},{10,11},{13,12},{14,15},{17,16},{18,... | collective-permute-start | bytes 2457608 | tf_op jit(solution)/shard_map/ppermute | solution.py:38
  25.0 22.4 %collective-permute-start.3 = (bf16[640,640]{1,0:T(8,128)(2,1)}, bf16[640,640]{1,0:T(8,128)(2,1)}, u32[]{:S(2)}, u32[]{:S(2)}) collective-permute-start(bf16[640,640]{1,0:T(8,128)(2,1)} %get-tuple-element.41.refs_4_), channel_id=1, source_target_pairs={{1,2},{2,1},{5,6},{6,5},{9,10},{10,9},{13,14},{14,13},{17,18},{18,... | collective-permute-start | bytes 2457608 | tf_op jit(solution)/shard_map/ppermute | solution.py:38
  26.6 28.0 %collective-permute-start.4 = (bf16[640,640]{1,0:T(8,128)(2,1)}, bf16[640,640]{1,0:T(8,128)(2,1)}, u32[]{:S(2)}, u32[]{:S(2)}) collective-permute-start(bf16[640,640]{1,0:T(8,128)(2,1)} %get-tuple-element.41.refs_4_), channel_id=1, source_target_pairs={{0,8},{4,20},{8,0},{12,28},{16,24},{20,4},{24,16},{28,12},{1,9},{5... | collective-permute-start | bytes 2457608 | tf_op jit(solution)/shard_map/ppermute | solution.py:42
  28.2 27.8 %collective-permute-start.5 = (bf16[640,640]{1,0:T(8,128)(2,1)}, bf16[640,640]{1,0:T(8,128)(2,1)}, u32[]{:S(2)}, u32[]{:S(2)}) collective-permute-start(bf16[640,640]{1,0:T(8,128)(2,1)} %get-tuple-element.41.refs_4_), channel_id=1, source_target_pairs={{0,16},{4,12},{8,24},{12,4},{16,0},{20,28},{24,8},{28,20},{1,17},{... | collective-permute-start | bytes 2457608 | tf_op jit(solution)/shard_map/ppermute | solution.py:42
  47.4 22.6 %collective-permute-start.6 = (bf16[640,640]{1,0:T(8,128)(2,1)}, bf16[640,640]{1,0:T(8,128)(2,1)}, u32[]{:S(2)}, u32[]{:S(2)}) collective-permute-start(bf16[640,640]{1,0:T(8,128)(2,1)} %get-tuple-element.46), channel_id=1, source_target_pairs={{1,0},{2,3},{5,4},{6,7},{9,8},{10,11},{13,12},{14,15},{17,16},{18,... | collective-permute-start | bytes 2457608 | tf_op jit(solution)/shard_map/ppermute | solution.py:38
  48.7 63.7 %collective-permute-start.11 = (bf16[512,2560]{1,0:T(8,128)(2,1)}, bf16[512,2560]{1,0:T(8,128)(2,1)}, u32[]{:S(2)}, u32[]{:S(2)}) collective-permute-start(bf16[512,2560]{1,0:T(8,128)(2,1)} %get-tuple-element.53), channel_id=1, source_target_pairs={{1,2},{2,1},{5,6},{6,5},{9,10},{10,9},{13,14},{14,13},{17,18},{18,... | collective-permute-start | bytes 7864328 | tf_op jit(solution)/shard_map/ppermute | solution.py:38
  53.0 21.5 %collective-permute-start.7 = (bf16[640,640]{1,0:T(8,128)(2,1)}, bf16[640,640]{1,0:T(8,128)(2,1)}, u32[]{:S(2)}, u32[]{:S(2)}) collective-permute-start(bf16[640,640]{1,0:T(8,128)(2,1)} %broadcast_select_fusion.1.refs_1_), channel_id=1, source_target_pairs={{0,8},{4,20},{8,0},{12,28},{16,24},{20,4},{24,16},{28,12},{1,9},{5... | collective-permute-start | bytes 2457608 | tf_op jit(solution)/shard_map/ppermute | solution.py:42
  54.5 21.5 %collective-permute-start.8 = (bf16[640,640]{1,0:T(8,128)(2,1)}, bf16[640,640]{1,0:T(8,128)(2,1)}, u32[]{:S(2)}, u32[]{:S(2)}) collective-permute-start(bf16[640,640]{1,0:T(8,128)(2,1)} %broadcast_select_fusion.1.refs_1_), channel_id=1, source_target_pairs={{0,16},{4,12},{8,24},{12,4},{16,0},{20,28},{24,8},{28,20},{1,17},{... | collective-permute-start | bytes 2457608 | tf_op jit(solution)/shard_map/ppermute | solution.py:42
  56.0 32.6 %collective-permute-start.9 = (bf16[640,640]{1,0:T(8,128)(2,1)}, bf16[640,640]{1,0:T(8,128)(2,1)}, u32[]{:S(2)}, u32[]{:S(2)}) collective-permute-start(bf16[640,640]{1,0:T(8,128)(2,1)} %get-tuple-element.49.refs_5_), channel_id=1, source_target_pairs={{0,16},{4,12},{8,24},{12,4},{16,0},{20,28},{24,8},{28,20},{1,17},{... | collective-permute-start | bytes 2457608 | tf_op jit(solution)/shard_map/ppermute | solution.py:42
  70.0 42.4 %collective-permute-start.10 = (bf16[512,1920]{1,0:T(8,128)(2,1)}, bf16[512,1920]{1,0:T(8,128)(2,1)}, u32[]{:S(2)}, u32[]{:S(2)}) collective-permute-start(bf16[512,1920]{1,0:T(8,128)(2,1)} %get-tuple-element.52), channel_id=1, source_target_pairs={{0,1},{1,0},{2,3},{3,2},{4,5},{5,4},{6,7},{7,6},{8,9},{9,8},{10,11... | collective-permute-start | bytes 5898248 | tf_op jit(solution)/shard_map/ppermute | solution.py:38
  74.5 21.5 %collective-permute-start.13 = (bf16[640,640]{1,0:T(8,128)(2,1)}, bf16[640,640]{1,0:T(8,128)(2,1)}, u32[]{:S(2)}, u32[]{:S(2)}) collective-permute-start(bf16[640,640]{1,0:T(8,128)(2,1)} %broadcast_select_fusion.refs_2_), channel_id=1, source_target_pairs={{0,8},{4,20},{8,0},{12,28},{16,24},{20,4},{24,16},{28,12},{1,9},{5... | collective-permute-start | bytes 2457608 | tf_op jit(solution)/shard_map/ppermute | solution.py:42
  76.0 22.1 %collective-permute-start.14 = (bf16[640,640]{1,0:T(8,128)(2,1)}, bf16[640,640]{1,0:T(8,128)(2,1)}, u32[]{:S(2)}, u32[]{:S(2)}) collective-permute-start(bf16[640,640]{1,0:T(8,128)(2,1)} %broadcast_select_fusion.refs_2_), channel_id=1, source_target_pairs={{0,16},{4,12},{8,24},{12,4},{16,0},{20,28},{24,8},{28,20},{1,17},{... | collective-permute-start | bytes 2457608 | tf_op jit(solution)/shard_map/ppermute | solution.py:42
  88.6 18.3 %collective-permute-start.12 = (bf16[640,640]{1,0:T(8,128)(2,1)}, bf16[640,640]{1,0:T(8,128)(2,1)}, u32[]{:S(2)}, u32[]{:S(2)}) collective-permute-start(bf16[640,640]{1,0:T(8,128)(2,1)} %get-tuple-element.55.refs_16_), channel_id=1, source_target_pairs={{0,16},{4,12},{8,24},{12,4},{16,0},{20,28},{24,8},{28,20},{1,17},{... | collective-permute-start | bytes 2457608 | tf_op jit(solution)/shard_map/ppermute | solution.py:42
  96.0 17.0 %collective-permute-start.15 = (bf16[640,640]{1,0:T(8,128)(2,1)}, bf16[640,640]{1,0:T(8,128)(2,1)}, u32[]{:S(2)}, u32[]{:S(2)}) collective-permute-start(bf16[640,640]{1,0:T(8,128)(2,1)} %get-tuple-element.60.refs_7_), channel_id=1, source_target_pairs={{0,4},{4,0},{8,12},{12,8},{16,20},{20,16},{24,28},{28,24},{1,5},{5... | collective-permute-start | bytes 2457608 | tf_op jit(solution)/shard_map/ppermute | solution.py:42
  98.1 14.9 %collective-permute-start.16 = (bf16[640,640]{1,0:T(8,128)(2,1)}, bf16[640,640]{1,0:T(8,128)(2,1)}, u32[]{:S(2)}, u32[]{:S(2)}) collective-permute-start(bf16[640,640]{1,0:T(8,128)(2,1)} %get-tuple-element.61.refs_8_), channel_id=1, source_target_pairs={{0,4},{4,0},{8,12},{12,8},{16,20},{20,16},{24,28},{28,24},{1,5},{5... | collective-permute-start | bytes 2457608 | tf_op jit(solution)/shard_map/ppermute | solution.py:42
  106.9 6.6 %collective-permute-start.17 = (bf16[640,640]{1,0:T(8,128)(2,1)}, bf16[640,640]{1,0:T(8,128)(2,1)}, u32[]{:S(2)}, u32[]{:S(2)}) collective-permute-start(bf16[640,640]{1,0:T(8,128)(2,1)} %get-tuple-element.62.refs_9_), channel_id=1, source_target_pairs={{0,4},{4,0},{8,12},{12,8},{16,20},{20,16},{24,28},{28,24},{1,5},{5... | collective-permute-start | bytes 2457608 | tf_op jit(solution)/shard_map/ppermute | solution.py:42
  112.5 2.7 %collective-permute-start.18 = (bf16[640,640]{1,0:T(8,128)(2,1)}, bf16[640,640]{1,0:T(8,128)(2,1)}, u32[]{:S(2)}, u32[]{:S(2)}) collective-permute-start(bf16[640,640]{1,0:T(8,128)(2,1)} %get-tuple-element.63.refs_10_), channel_id=1, source_target_pairs={{0,4},{4,0},{8,12},{12,8},{16,20},{20,16},{24,28},{28,24},{1,5},{5... | collective-permute-start | bytes 2457608 | tf_op jit(solution)/shard_map/ppermute | solution.py:42
  112.5 4.2 %collective-permute-start.19 = (bf16[640,640]{1,0:T(8,128)(2,1)}, bf16[640,640]{1,0:T(8,128)(2,1)}, u32[]{:S(2)}, u32[]{:S(2)}) collective-permute-start(bf16[640,640]{1,0:T(8,128)(2,1)} %get-tuple-element.64.refs_15_), channel_id=1, source_target_pairs={{0,4},{4,0},{8,12},{12,8},{16,20},{20,16},{24,28},{28,24},{1,5},{5... | collective-permute-start | bytes 2457608 | tf_op jit(solution)/shard_map/ppermute | solution.py:42
  113.0 5.4 %collective-permute-start.20 = (bf16[640,640]{1,0:T(8,128)(2,1)}, bf16[640,640]{1,0:T(8,128)(2,1)}, u32[]{:S(2)}, u32[]{:S(2)}) collective-permute-start(bf16[640,640]{1,0:T(8,128)(2,1)} %get-tuple-element.55.refs_16_), channel_id=1, source_target_pairs={{0,4},{4,0},{8,12},{12,8},{16,20},{20,16},{24,28},{28,24},{1,5},{5... | collective-permute-start | bytes 2457608 | tf_op jit(solution)/shard_map/ppermute | solution.py:42
  113.0 5.6 %collective-permute-start.21 = (bf16[640,640]{1,0:T(8,128)(2,1)}, bf16[640,640]{1,0:T(8,128)(2,1)}, u32[]{:S(2)}, u32[]{:S(2)}) collective-permute-start(bf16[640,640]{1,0:T(8,128)(2,1)} %get-tuple-element.65.refs_17_), channel_id=1, source_target_pairs={{0,4},{4,0},{8,12},{12,8},{16,20},{20,16},{24,28},{28,24},{1,5},{5... | collective-permute-start | bytes 2457608 | tf_op jit(solution)/shard_map/ppermute | solution.py:42
  113.5 6.3 %collective-permute-start.22 = (bf16[640,640]{1,0:T(8,128)(2,1)}, bf16[640,640]{1,0:T(8,128)(2,1)}, u32[]{:S(2)}, u32[]{:S(2)}) collective-permute-start(bf16[640,640]{1,0:T(8,128)(2,1)} %get-tuple-element.66.refs_18_), channel_id=1, source_target_pairs={{0,4},{4,0},{8,12},{12,8},{16,20},{20,16},{24,28},{28,24},{1,5},{5... | collective-permute-start | bytes 2457608 | tf_op jit(solution)/shard_map/ppermute | solution.py:42
  115.1 21.1 %collective-permute-start.24 = (bf16[640,640]{1,0:T(8,128)(2,1)}, bf16[640,640]{1,0:T(8,128)(2,1)}, u32[]{:S(2)}, u32[]{:S(2)}) collective-permute-start(bf16[640,640]{1,0:T(8,128)(2,1)} %collective-permute-done.13.refs_5_.refs_3_), channel_id=1, source_target_pairs={{0,16},{4,12},{8,24},{12,4},{16,0},{20,28},{24,8},{28,20},{1,17},{... | collective-permute-start | bytes 2457608 | tf_op jit(solution)/shard_map/ppermute | solution.py:42
  116.7 19.6 %collective-permute-start.23 = (bf16[512,640]{1,0:T(8,128)(2,1)}, bf16[512,640]{1,0:T(8,128)(2,1)}, u32[]{:S(2)}, u32[]{:S(2)}) collective-permute-start(bf16[512,640]{1,0:T(8,128)(2,1)} %get-tuple-element.67), channel_id=1, source_target_pairs={{0,1},{1,0},{2,3},{3,2},{4,5},{5,4},{6,7},{7,6},{8,9},{9,8},{10,11... | collective-permute-start | bytes 1966088 | tf_op jit(solution)/shard_map/ppermute | solution.py:38
  118.4 18.4 %collective-permute-start.25 = (bf16[640,640]{1,0:T(8,128)(2,1)}, bf16[640,640]{1,0:T(8,128)(2,1)}, u32[]{:S(2)}, u32[]{:S(2)}) collective-permute-start(bf16[640,640]{1,0:T(8,128)(2,1)} %broadcast_select_fusion.refs_2_), channel_id=1, source_target_pairs={{0,4},{4,0},{8,12},{12,8},{16,20},{20,16},{24,28},{28,24},{1,5},{5... | collective-permute-start | bytes 2457608 | tf_op jit(solution)/shard_map/ppermute | solution.py:42
  118.6 18.1 %collective-permute-start.26 = (bf16[640,640]{1,0:T(8,128)(2,1)}, bf16[640,640]{1,0:T(8,128)(2,1)}, u32[]{:S(2)}, u32[]{:S(2)}) collective-permute-start(bf16[640,640]{1,0:T(8,128)(2,1)} %collective-permute-done.13.refs_5_.refs_3_), channel_id=1, source_target_pairs={{0,4},{4,0},{8,12},{12,8},{16,20},{20,16},{24,28},{28,24},{1,5},{5... | collective-permute-start | bytes 2457608 | tf_op jit(solution)/shard_map/ppermute | solution.py:42
  119.8 17.0 %collective-permute-start.27 = (bf16[640,640]{1,0:T(8,128)(2,1)}, bf16[640,640]{1,0:T(8,128)(2,1)}, u32[]{:S(2)}, u32[]{:S(2)}) collective-permute-start(bf16[640,640]{1,0:T(8,128)(2,1)} %collective-permute-done.14.refs_6_.refs_4_), channel_id=1, source_target_pairs={{0,4},{4,0},{8,12},{12,8},{16,20},{20,16},{24,28},{28,24},{1,5},{5... | collective-permute-start | bytes 2457608 | tf_op jit(solution)/shard_map/ppermute | solution.py:42
  136.3 2.8 %collective-permute-start.28 = (bf16[640,640]{1,0:T(8,128)(2,1)}, bf16[640,640]{1,0:T(8,128)(2,1)}, u32[]{:S(2)}, u32[]{:S(2)}) collective-permute-start(bf16[640,640]{1,0:T(8,128)(2,1)} %get-tuple-element.70.refs_5_), channel_id=1, source_target_pairs={{0,4},{4,0},{8,12},{12,8},{16,20},{20,16},{24,28},{28,24},{1,5},{5... | collective-permute-start | bytes 2457608 | tf_op jit(solution)/shard_map/ppermute | solution.py:42

commit v7 on v6

--- a/solution.py
+++ b/solution.py
@@ -284,7 +284,7 @@
     second_near = to_neighbours(second)
 
     chain, outer_next = step(chain, [], [outer_next])
-    chain, second, *operands = step(chain, [], [second, *second_near, *first_all], 8 * MIB)
+    chain, second, *operands = step(chain, [], [second, *second_near, *first_all], 24 * MIB)
     second_near, first_all = operands[:2], operands[2:]
     third = jnp.where(edge, outer_next, across)
     third_near = to_neighbours(third)

time: 149 us -> 149 us (level)
  no operation moved by 1% of the time
where the time goes in v7:
time: 149 us; the launch traced here: 148 us
  waiting for transfers between devices  79.7 us (53%)
  Pallas kernels  30.3 us (20%)
  starting transfers between devices  30.2 us (20%)
  other arithmetic  4.91 us (3%)
  local copies, waits for them, and re-layouts  2.74 us (2%)
    ppermute x8, waiting for transfers between devices, along_line(): return lax.ppermute(value, ('dp', 'ctx'), pairs)  45.9 us
    ppermute x21, waiting for transfers between devices, in_plane(): lax.ppermute(value, 'dp', [(lane, lane ^ masks[lane % 2]) for lane in ran...  33.8 us
    pallas_call x2, Pallas kernels, worked_off(): pl.pallas_call(kernel, out_shape=jax.ShapeDtypeStruct(base.shape, dtype),...  25.2 us
    ppermute x21, starting transfers between devices, in_plane(): lax.ppermute(value, 'dp', [(lane, lane ^ masks[lane % 2]) for lane in ran...  17.6 us
    ppermute x8, starting transfers between devices, along_line(): return lax.ppermute(value, ('dp', 'ctx'), pairs)  12.6 us
    pallas_call x1, Pallas kernels, packed(): pl.pallas_call(pack_kernel, out_shape=shapes, grid_spec=pltpu.PrefetchSca...  5.13 us
  transfers between devices with their start and end apart: 29, of which 13 were waited for; matrix products, arithmetic and copies ran while one was open for 4% of the time, Pallas kernels for 14%

profile of v7, /device:TPU:0, one launch (start us, length us, event | category | flops | bytes accessed | tf_op | source)
XLA Modules:
  0.0 148.1 jit_solution(16318600354896829876)
XLA Ops:
  0.0 2.1 %constant_dynamic-slice_fusion = bf16[640,640]{1,0:T(8,128)(2,1)} fusion(bf16[640,5120]{1,0:T(8,128)(2,1)} %refs_6_.1, s32[]{:T(128)S(6)} %select_n.30), kind=kLoop, calls=%fused_computation.7 | loop fusion | bytes 1638404 | tf_op jit(solution)/shard_map/dynamic_slice | solution.py:253
  2.1 3.0 %collective-permute-start = (bf16[640,640]{1,0:T(8,128)(2,1)}, bf16[640,640]{1,0:T(8,128)(2,1)}, u32[]{:S(2)}, u32[]{:S(2)}) collective-permute-start(bf16[640,640]{1,0:T(8,128)(2,1)} %constant_dynamic-slice_fusion), channel_id=1, source_target_pairs={{0,1},{1,0},{2,3},{3,2},{4,5},{5,4},{6,7},{7,6},{8,9},{9,8},{10,11... | collective-permute-start | bytes 2457608 | tf_op jit(solution)/shard_map/ppermute | solution.py:38
  5.1 1.6 %collective-permute-start.1 = (bf16[640,640]{1,0:T(8,128)(2,1)}, bf16[640,640]{1,0:T(8,128)(2,1)}, u32[]{:S(2)}, u32[]{:S(2)}) collective-permute-start(bf16[640,640]{1,0:T(8,128)(2,1)} %constant_dynamic-slice_fusion), channel_id=1, source_target_pairs={{1,2},{2,1},{5,6},{6,5},{9,10},{10,9},{13,14},{14,13},{17,18},{18,... | collective-permute-start | bytes 2457608 | tf_op jit(solution)/shard_map/ppermute | solution.py:38
  8.0 5.1 %pack_window.1 = (f32[8,128]{1,0:T(8,128)}, bf16[512,1920]{1,0:T(8,128)(2,1)}, bf16[512,640]{1,0:T(8,128)(2,1)}, bf16[512,2560]{1,0:T(8,128)(2,1)}) custom-call(s32[21]{0:T(128)} %concatenate.3.place, bf16[256,2560]{1,0:T(8,128)(2,1)} %key_ref.5, bf16[256,2560]{1,0:T(8,128)(2,1)} %value_ref.5), custom_call_target="tpu_custom_call" | custom-call | tf_op jit(solution)/shard_map/pack_window/pallas_call | solution.py:106
  13.1 10.6 %collective-permute-done.refs_1_ = bf16[640,640]{1,0:T(8,128)(2,1)} collective-permute-done((bf16[640,640]{1,0:T(8,128)(2,1)}, bf16[640,640]{1,0:T(8,128)(2,1)}, u32[]{:S(2)}, u32[]{:S(2)}) %collective-permute-start) | collective-permute-done | bytes 819232 | tf_op jit(solution)/shard_map/ppermute | solution.py:38
  25.0 1.6 %collective-permute-start.3 = (bf16[640,640]{1,0:T(8,128)(2,1)}, bf16[640,640]{1,0:T(8,128)(2,1)}, u32[]{:S(2)}, u32[]{:S(2)}) collective-permute-start(bf16[640,640]{1,0:T(8,128)(2,1)} %get-tuple-element.41.refs_4_), channel_id=1, source_target_pairs={{1,2},{2,1},{5,6},{6,5},{9,10},{10,9},{13,14},{14,13},{17,18},{18,... | collective-permute-start | bytes 2457608 | tf_op jit(solution)/shard_map/ppermute | solution.py:38
  26.6 1.7 %collective-permute-start.4 = (bf16[640,640]{1,0:T(8,128)(2,1)}, bf16[640,640]{1,0:T(8,128)(2,1)}, u32[]{:S(2)}, u32[]{:S(2)}) collective-permute-start(bf16[640,640]{1,0:T(8,128)(2,1)} %get-tuple-element.41.refs_4_), channel_id=1, source_target_pairs={{0,8},{4,20},{8,0},{12,28},{16,24},{20,4},{24,16},{28,12},{1,9},{5... | collective-permute-start | bytes 2457608 | tf_op jit(solution)/shard_map/ppermute | solution.py:42
  28.2 1.5 %collective-permute-start.5 = (bf16[640,640]{1,0:T(8,128)(2,1)}, bf16[640,640]{1,0:T(8,128)(2,1)}, u32[]{:S(2)}, u32[]{:S(2)}) collective-permute-start(bf16[640,640]{1,0:T(8,128)(2,1)} %get-tuple-element.41.refs_4_), channel_id=1, source_target_pairs={{0,16},{4,12},{8,24},{12,4},{16,0},{20,28},{24,8},{28,20},{1,17},{... | collective-permute-start | bytes 2457608 | tf_op jit(solution)/shard_map/ppermute | solution.py:42
  29.7 17.7 %collective-permute-done.2.refs_1_ = bf16[640,640]{1,0:T(8,128)(2,1)} collective-permute-done((bf16[640,640]{1,0:T(8,128)(2,1)}, bf16[640,640]{1,0:T(8,128)(2,1)}, u32[]{:S(2)}, u32[]{:S(2)}) %collective-permute-start.2) | collective-permute-done | bytes 819232 | tf_op jit(solution)/shard_map/ppermute | solution.py:38
  48.7 2.2 %collective-permute-start.11 = (bf16[512,2560]{1,0:T(8,128)(2,1)}, bf16[512,2560]{1,0:T(8,128)(2,1)}, u32[]{:S(2)}, u32[]{:S(2)}) collective-permute-start(bf16[512,2560]{1,0:T(8,128)(2,1)} %get-tuple-element.53), channel_id=1, source_target_pairs={{1,2},{2,1},{5,6},{6,5},{9,10},{10,9},{13,14},{14,13},{17,18},{18,... | collective-permute-start | bytes 7864328 | tf_op jit(solution)/shard_map/ppermute | solution.py:38
  50.9 2.1 %broadcast_select_fusion.1.refs_1_ = bf16[640,640]{1,0:T(8,128)(2,1)} fusion(bf16[640,640]{1,0:T(8,128)(2,1)} %get-tuple-element.48, bf16[640,640]{1,0:T(8,128)(2,1)} %get-tuple-element.40, pred[]{:T(512)S(6)} %or.3), kind=kLoop, calls=%fused_computation.1 | loop fusion | flops 409600 | bytes 2457601 | tf_op jit(solution)/shard_map/jit(_where)/select_n | solution.py:283
  53.0 1.5 %collective-permute-start.7 = (bf16[640,640]{1,0:T(8,128)(2,1)}, bf16[640,640]{1,0:T(8,128)(2,1)}, u32[]{:S(2)}, u32[]{:S(2)}) collective-permute-start(bf16[640,640]{1,0:T(8,128)(2,1)} %broadcast_select_fusion.1.refs_1_), channel_id=1, source_target_pairs={{0,8},{4,20},{8,0},{12,28},{16,24},{20,4},{24,16},{28,12},{1,9},{5... | collective-permute-start | bytes 2457608 | tf_op jit(solution)/shard_map/ppermute | solution.py:42
  54.5 1.5 %collective-permute-start.8 = (bf16[640,640]{1,0:T(8,128)(2,1)}, bf16[640,640]{1,0:T(8,128)(2,1)}, u32[]{:S(2)}, u32[]{:S(2)}) collective-permute-start(bf16[640,640]{1,0:T(8,128)(2,1)} %broadcast_select_fusion.1.refs_1_), channel_id=1, source_target_pairs={{0,16},{4,12},{8,24},{12,4},{16,0},{20,28},{24,8},{28,20},{1,17},{... | collective-permute-start | bytes 2457608 | tf_op jit(solution)/shard_map/ppermute | solution.py:42
  56.5 13.5 %collective-permute-done.6.refs_1_ = bf16[640,640]{1,0:T(8,128)(2,1)} collective-permute-done((bf16[640,640]{1,0:T(8,128)(2,1)}, bf16[640,640]{1,0:T(8,128)(2,1)}, u32[]{:S(2)}, u32[]{:S(2)}) %collective-permute-start.6) | collective-permute-done | bytes 819232 | tf_op jit(solution)/shard_map/ppermute | solution.py:38
  70.0 2.1 %broadcast_select_fusion.refs_2_ = bf16[640,640]{1,0:T(8,128)(2,1)} fusion(bf16[640,640]{1,0:T(8,128)(2,1)} %get-tuple-element.56, bf16[640,640]{1,0:T(8,128)(2,1)} %get-tuple-element.46, pred[]{:T(512)S(6)} %or.3), kind=kLoop, calls=%fused_computation | loop fusion | flops 409600 | bytes 2457601 | tf_op jit(solution)/shard_map/jit(_where)/select_n | solution.py:289
  72.1 2.4 %collective-permute-done.7.refs_2_ = bf16[640,640]{1,0:T(8,128)(2,1)} collective-permute-done((bf16[640,640]{1,0:T(8,128)(2,1)}, bf16[640,640]{1,0:T(8,128)(2,1)}, u32[]{:S(2)}, u32[]{:S(2)}) %collective-permute-start.7) | collective-permute-done | bytes 819232 | tf_op jit(solution)/shard_map/ppermute | solution.py:42
  74.5 1.5 %collective-permute-start.13 = (bf16[640,640]{1,0:T(8,128)(2,1)}, bf16[640,640]{1,0:T(8,128)(2,1)}, u32[]{:S(2)}, u32[]{:S(2)}) collective-permute-start(bf16[640,640]{1,0:T(8,128)(2,1)} %broadcast_select_fusion.refs_2_), channel_id=1, source_target_pairs={{0,8},{4,20},{8,0},{12,28},{16,24},{20,4},{24,16},{28,12},{1,9},{5... | collective-permute-start | bytes 2457608 | tf_op jit(solution)/shard_map/ppermute | solution.py:42
  76.0 1.5 %collective-permute-start.14 = (bf16[640,640]{1,0:T(8,128)(2,1)}, bf16[640,640]{1,0:T(8,128)(2,1)}, u32[]{:S(2)}, u32[]{:S(2)}) collective-permute-start(bf16[640,640]{1,0:T(8,128)(2,1)} %broadcast_select_fusion.refs_2_), channel_id=1, source_target_pairs={{0,16},{4,12},{8,24},{12,4},{16,0},{20,28},{24,8},{28,20},{1,17},{... | collective-permute-start | bytes 2457608 | tf_op jit(solution)/shard_map/ppermute | solution.py:42
  77.5 11.1 %collective-permute-done.9.refs_7_ = bf16[640,640]{1,0:T(8,128)(2,1)} collective-permute-done((bf16[640,640]{1,0:T(8,128)(2,1)}, bf16[640,640]{1,0:T(8,128)(2,1)}, u32[]{:S(2)}, u32[]{:S(2)}) %collective-permute-start.9) | collective-permute-done | bytes 819232 | tf_op jit(solution)/shard_map/ppermute | solution.py:42
  88.6 1.5 %collective-permute-start.12 = (bf16[640,640]{1,0:T(8,128)(2,1)}, bf16[640,640]{1,0:T(8,128)(2,1)}, u32[]{:S(2)}, u32[]{:S(2)}) collective-permute-start(bf16[640,640]{1,0:T(8,128)(2,1)} %get-tuple-element.55.refs_16_), channel_id=1, source_target_pairs={{0,16},{4,12},{8,24},{12,4},{16,0},{20,28},{24,8},{28,20},{1,17},{... | collective-permute-start | bytes 2457608 | tf_op jit(solution)/shard_map/ppermute | solution.py:42
  90.2 5.8 %collective-permute-done.13.refs_5_.refs_3_ = bf16[640,640]{1,0:T(8,128)(2,1)} collective-permute-done((bf16[640,640]{1,0:T(8,128)(2,1)}, bf16[640,640]{1,0:T(8,128)(2,1)}, u32[]{:S(2)}, u32[]{:S(2)}) %collective-permute-start.13) | collective-permute-done | bytes 819232 | tf_op jit(solution)/shard_map/ppermute | solution.py:42
  96.0 2.1 %collective-permute-done.14.refs_6_.refs_4_ = bf16[640,640]{1,0:T(8,128)(2,1)} collective-permute-done((bf16[640,640]{1,0:T(8,128)(2,1)}, bf16[640,640]{1,0:T(8,128)(2,1)}, u32[]{:S(2)}, u32[]{:S(2)}) %collective-permute-start.14) | collective-permute-done | bytes 819232 | tf_op jit(solution)/shard_map/ppermute | solution.py:42
  98.1 1.4 collective-permute-start.16
  99.5 7.4 %collective-permute-done.12.refs_4_ = bf16[640,640]{1,0:T(8,128)(2,1)} collective-permute-done((bf16[640,640]{1,0:T(8,128)(2,1)}, bf16[640,640]{1,0:T(8,128)(2,1)}, u32[]{:S(2)}, u32[]{:S(2)}) %collective-permute-start.12) | collective-permute-done | bytes 819232 | tf_op jit(solution)/shard_map/ppermute | solution.py:42
  106.9 1.4 collective-permute-start.17
  108.3 4.2 %collective-permute-done.10.refs_1_ = bf16[512,1920]{1,0:T(8,128)(2,1)} collective-permute-done((bf16[512,1920]{1,0:T(8,128)(2,1)}, bf16[512,1920]{1,0:T(8,128)(2,1)}, u32[]{:S(2)}, u32[]{:S(2)}) %collective-permute-start.10) | collective-permute-done | bytes 1966112 | tf_op jit(solution)/shard_map/ppermute | solution.py:38
  113.6 1.6 %collective-permute-done.18.refs_14_ = bf16[640,640]{1,0:T(8,128)(2,1)} collective-permute-done((bf16[640,640]{1,0:T(8,128)(2,1)}, bf16[640,640]{1,0:T(8,128)(2,1)}, u32[]{:S(2)}, u32[]{:S(2)}) %collective-permute-start.18) | collective-permute-done | bytes 819232 | tf_op jit(solution)/shard_map/ppermute | solution.py:42
  115.1 1.5 %collective-permute-start.24 = (bf16[640,640]{1,0:T(8,128)(2,1)}, bf16[640,640]{1,0:T(8,128)(2,1)}, u32[]{:S(2)}, u32[]{:S(2)}) collective-permute-start(bf16[640,640]{1,0:T(8,128)(2,1)} %collective-permute-done.13.refs_5_.refs_3_), channel_id=1, source_target_pairs={{0,16},{4,12},{8,24},{12,4},{16,0},{20,28},{24,8},{28,20},{1,17},{... | collective-permute-start | bytes 2457608 | tf_op jit(solution)/shard_map/ppermute | solution.py:42
  116.7 1.7 %collective-permute-start.23 = (bf16[512,640]{1,0:T(8,128)(2,1)}, bf16[512,640]{1,0:T(8,128)(2,1)}, u32[]{:S(2)}, u32[]{:S(2)}) collective-permute-start(bf16[512,640]{1,0:T(8,128)(2,1)} %get-tuple-element.67), channel_id=1, source_target_pairs={{0,1},{1,0},{2,3},{3,2},{4,5},{5,4},{6,7},{7,6},{8,9},{9,8},{10,11... | collective-permute-start | bytes 1966088 | tf_op jit(solution)/shard_map/ppermute | solution.py:38
  120.0 16.3 %work_off_slots.2.refs_1_ = f32[256,5120]{1,0:T(8,128)} custom-call(s32[21]{0:T(128)} %concatenate.3.place, bf16[256,2560]{1,0:T(8,128)(2,1)} %query_ref.3, bf16[256,2560]{1,0:T(8,128)(2,1)} %key_ref.5, bf16[256,2560]{1,0:T(8,128)(2,1)} %value_ref.5, bf16[256,5120]{1,0:T(8,128)(2,1)} %base_ref.1, ...), custom_call_target="tpu_custom_call" | custom-call | flops 6543114240 | bytes 37027840 | tf_op jit(solution)/shard_map/work_off_slots/pallas_call | solution.py:206
  136.8 2.3 %collective-permute-done.28.refs_9_ = bf16[640,640]{1,0:T(8,128)(2,1)} collective-permute-done((bf16[640,640]{1,0:T(8,128)(2,1)}, bf16[640,640]{1,0:T(8,128)(2,1)}, u32[]{:S(2)}, u32[]{:S(2)}) %collective-permute-start.28) | collective-permute-done | bytes 819232 | tf_op jit(solution)/shard_map/ppermute | solution.py:42
  139.1 8.9 %work_off_slots.3 = bf16[256,5120]{1,0:T(8,128)(2,1)} custom-call(s32[21]{0:T(128)} %concatenate.3.place, bf16[256,2560]{1,0:T(8,128)(2,1)} %query_ref.3, bf16[256,2560]{1,0:T(8,128)(2,1)} %key_ref.5, bf16[256,2560]{1,0:T(8,128)(2,1)} %value_ref.5, f32[256,5120]{1,0:T(8,128)} %get-tuple-element.68.base_ref, bf16[512,640]{1,0:T(8,128)(2,1)} %get-tuple-element.69.refs_0_, ...), custom_call_target="tpu_custom_call" | custom-call | flops 2181038080 | bytes 19333120 | tf_op jit(solution)/shard_map/work_off_slots/pallas_call | solution.py:206
  (41 shorter events, 7.6 us)
Async XLA Ops:
  2.1 21.6 %collective-permute-start = (bf16[640,640]{1,0:T(8,128)(2,1)}, bf16[640,640]{1,0:T(8,128)(2,1)}, u32[]{:S(2)}, u32[]{:S(2)}) collective-permute-start(bf16[640,640]{1,0:T(8,128)(2,1)} %constant_dynamic-slice_fusion), channel_id=1, source_target_pairs={{0,1},{1,0},{2,3},{3,2},{4,5},{5,4},{6,7},{7,6},{8,9},{9,8},{10,11... | collective-permute-start | bytes 2457608 | tf_op jit(solution)/shard_map/ppermute | solution.py:38
  5.1 18.6 %collective-permute-start.1 = (bf16[640,640]{1,0:T(8,128)(2,1)}, bf16[640,640]{1,0:T(8,128)(2,1)}, u32[]{:S(2)}, u32[]{:S(2)}) collective-permute-start(bf16[640,640]{1,0:T(8,128)(2,1)} %constant_dynamic-slice_fusion), channel_id=1, source_target_pairs={{1,2},{2,1},{5,6},{6,5},{9,10},{10,9},{13,14},{14,13},{17,18},{18,... | collective-permute-start | bytes 2457608 | tf_op jit(solution)/shard_map/ppermute | solution.py:38
  23.7 23.7 %collective-permute-start.2 = (bf16[640,640]{1,0:T(8,128)(2,1)}, bf16[640,640]{1,0:T(8,128)(2,1)}, u32[]{:S(2)}, u32[]{:S(2)}) collective-permute-start(bf16[640,640]{1,0:T(8,128)(2,1)} %get-tuple-element.40), channel_id=1, source_target_pairs={{1,0},{2,3},{5,4},{6,7},{9,8},{10,11},{13,12},{14,15},{17,16},{18,... | collective-permute-start | bytes 2457608 | tf_op jit(solution)/shard_map/ppermute | solution.py:38
  25.0 22.4 %collective-permute-start.3 = (bf16[640,640]{1,0:T(8,128)(2,1)}, bf16[640,640]{1,0:T(8,128)(2,1)}, u32[]{:S(2)}, u32[]{:S(2)}) collective-permute-start(bf16[640,640]{1,0:T(8,128)(2,1)} %get-tuple-element.41.refs_4_), channel_id=1, source_target_pairs={{1,2},{2,1},{5,6},{6,5},{9,10},{10,9},{13,14},{14,13},{17,18},{18,... | collective-permute-start | bytes 2457608 | tf_op jit(solution)/shard_map/ppermute | solution.py:38
  26.6 28.0 %collective-permute-start.4 = (bf16[640,640]{1,0:T(8,128)(2,1)}, bf16[640,640]{1,0:T(8,128)(2,1)}, u32[]{:S(2)}, u32[]{:S(2)}) collective-permute-start(bf16[640,640]{1,0:T(8,128)(2,1)} %get-tuple-element.41.refs_4_), channel_id=1, source_target_pairs={{0,8},{4,20},{8,0},{12,28},{16,24},{20,4},{24,16},{28,12},{1,9},{5... | collective-permute-start | bytes 2457608 | tf_op jit(solution)/shard_map/ppermute | solution.py:42
  28.2 27.8 %collective-permute-start.5 = (bf16[640,640]{1,0:T(8,128)(2,1)}, bf16[640,640]{1,0:T(8,128)(2,1)}, u32[]{:S(2)}, u32[]{:S(2)}) collective-permute-start(bf16[640,640]{1,0:T(8,128)(2,1)} %get-tuple-element.41.refs_4_), channel_id=1, source_target_pairs={{0,16},{4,12},{8,24},{12,4},{16,0},{20,28},{24,8},{28,20},{1,17},{... | collective-permute-start | bytes 2457608 | tf_op jit(solution)/shard_map/ppermute | solution.py:42
  47.4 22.6 %collective-permute-start.6 = (bf16[640,640]{1,0:T(8,128)(2,1)}, bf16[640,640]{1,0:T(8,128)(2,1)}, u32[]{:S(2)}, u32[]{:S(2)}) collective-permute-start(bf16[640,640]{1,0:T(8,128)(2,1)} %get-tuple-element.46), channel_id=1, source_target_pairs={{1,0},{2,3},{5,4},{6,7},{9,8},{10,11},{13,12},{14,15},{17,16},{18,... | collective-permute-start | bytes 2457608 | tf_op jit(solution)/shard_map/ppermute | solution.py:38
  48.7 63.7 %collective-permute-start.11 = (bf16[512,2560]{1,0:T(8,128)(2,1)}, bf16[512,2560]{1,0:T(8,128)(2,1)}, u32[]{:S(2)}, u32[]{:S(2)}) collective-permute-start(bf16[512,2560]{1,0:T(8,128)(2,1)} %get-tuple-element.53), channel_id=1, source_target_pairs={{1,2},{2,1},{5,6},{6,5},{9,10},{10,9},{13,14},{14,13},{17,18},{18,... | collective-permute-start | bytes 7864328 | tf_op jit(solution)/shard_map/ppermute | solution.py:38
  53.0 21.5 %collective-permute-start.7 = (bf16[640,640]{1,0:T(8,128)(2,1)}, bf16[640,640]{1,0:T(8,128)(2,1)}, u32[]{:S(2)}, u32[]{:S(2)}) collective-permute-start(bf16[640,640]{1,0:T(8,128)(2,1)} %broadcast_select_fusion.1.refs_1_), channel_id=1, source_target_pairs={{0,8},{4,20},{8,0},{12,28},{16,24},{20,4},{24,16},{28,12},{1,9},{5... | collective-permute-start | bytes 2457608 | tf_op jit(solution)/shard_map/ppermute | solution.py:42
  54.5 21.5 %collective-permute-start.8 = (bf16[640,640]{1,0:T(8,128)(2,1)}, bf16[640,640]{1,0:T(8,128)(2,1)}, u32[]{:S(2)}, u32[]{:S(2)}) collective-permute-start(bf16[640,640]{1,0:T(8,128)(2,1)} %broadcast_select_fusion.1.refs_1_), channel_id=1, source_target_pairs={{0,16},{4,12},{8,24},{12,4},{16,0},{20,28},{24,8},{28,20},{1,17},{... | collective-permute-start | bytes 2457608 | tf_op jit(solution)/shard_map/ppermute | solution.py:42
  56.0 32.6 %collective-permute-start.9 = (bf16[640,640]{1,0:T(8,128)(2,1)}, bf16[640,640]{1,0:T(8,128)(2,1)}, u32[]{:S(2)}, u32[]{:S(2)}) collective-permute-start(bf16[640,640]{1,0:T(8,128)(2,1)} %get-tuple-element.49.refs_5_), channel_id=1, source_target_pairs={{0,16},{4,12},{8,24},{12,4},{16,0},{20,28},{24,8},{28,20},{1,17},{... | collective-permute-start | bytes 2457608 | tf_op jit(solution)/shard_map/ppermute | solution.py:42
  70.0 42.4 %collective-permute-start.10 = (bf16[512,1920]{1,0:T(8,128)(2,1)}, bf16[512,1920]{1,0:T(8,128)(2,1)}, u32[]{:S(2)}, u32[]{:S(2)}) collective-permute-start(bf16[512,1920]{1,0:T(8,128)(2,1)} %get-tuple-element.52), channel_id=1, source_target_pairs={{0,1},{1,0},{2,3},{3,2},{4,5},{5,4},{6,7},{7,6},{8,9},{9,8},{10,11... | collective-permute-start | bytes 5898248 | tf_op jit(solution)/shard_map/ppermute | solution.py:38
  74.5 21.5 %collective-permute-start.13 = (bf16[640,640]{1,0:T(8,128)(2,1)}, bf16[640,640]{1,0:T(8,128)(2,1)}, u32[]{:S(2)}, u32[]{:S(2)}) collective-permute-start(bf16[640,640]{1,0:T(8,128)(2,1)} %broadcast_select_fusion.refs_2_), channel_id=1, source_target_pairs={{0,8},{4,20},{8,0},{12,28},{16,24},{20,4},{24,16},{28,12},{1,9},{5... | collective-permute-start | bytes 2457608 | tf_op jit(solution)/shard_map/ppermute | solution.py:42
  76.0 22.1 %collective-permute-start.14 = (bf16[640,640]{1,0:T(8,128)(2,1)}, bf16[640,640]{1,0:T(8,128)(2,1)}, u32[]{:S(2)}, u32[]{:S(2)}) collective-permute-start(bf16[640,640]{1,0:T(8,128)(2,1)} %broadcast_select_fusion.refs_2_), channel_id=1, source_target_pairs={{0,16},{4,12},{8,24},{12,4},{16,0},{20,28},{24,8},{28,20},{1,17},{... | collective-permute-start | bytes 2457608 | tf_op jit(solution)/shard_map/ppermute | solution.py:42
  88.6 18.3 %collective-permute-start.12 = (bf16[640,640]{1,0:T(8,128)(2,1)}, bf16[640,640]{1,0:T(8,128)(2,1)}, u32[]{:S(2)}, u32[]{:S(2)}) collective-permute-start(bf16[640,640]{1,0:T(8,128)(2,1)} %get-tuple-element.55.refs_16_), channel_id=1, source_target_pairs={{0,16},{4,12},{8,24},{12,4},{16,0},{20,28},{24,8},{28,20},{1,17},{... | collective-permute-start | bytes 2457608 | tf_op jit(solution)/shard_map/ppermute | solution.py:42
  96.0 17.0 %collective-permute-start.15 = (bf16[640,640]{1,0:T(8,128)(2,1)}, bf16[640,640]{1,0:T(8,128)(2,1)}, u32[]{:S(2)}, u32[]{:S(2)}) collective-permute-start(bf16[640,640]{1,0:T(8,128)(2,1)} %get-tuple-element.60.refs_7_), channel_id=1, source_target_pairs={{0,4},{4,0},{8,12},{12,8},{16,20},{20,16},{24,28},{28,24},{1,5},{5... | collective-permute-start | bytes 2457608 | tf_op jit(solution)/shard_map/ppermute | solution.py:42
  98.1 14.9 %collective-permute-start.16 = (bf16[640,640]{1,0:T(8,128)(2,1)}, bf16[640,640]{1,0:T(8,128)(2,1)}, u32[]{:S(2)}, u32[]{:S(2)}) collective-permute-start(bf16[640,640]{1,0:T(8,128)(2,1)} %get-tuple-element.61.refs_8_), channel_id=1, source_target_pairs={{0,4},{4,0},{8,12},{12,8},{16,20},{20,16},{24,28},{28,24},{1,5},{5... | collective-permute-start | bytes 2457608 | tf_op jit(solution)/shard_map/ppermute | solution.py:42
  106.9 6.6 %collective-permute-start.17 = (bf16[640,640]{1,0:T(8,128)(2,1)}, bf16[640,640]{1,0:T(8,128)(2,1)}, u32[]{:S(2)}, u32[]{:S(2)}) collective-permute-start(bf16[640,640]{1,0:T(8,128)(2,1)} %get-tuple-element.62.refs_9_), channel_id=1, source_target_pairs={{0,4},{4,0},{8,12},{12,8},{16,20},{20,16},{24,28},{28,24},{1,5},{5... | collective-permute-start | bytes 2457608 | tf_op jit(solution)/shard_map/ppermute | solution.py:42
  112.5 2.7 %collective-permute-start.18 = (bf16[640,640]{1,0:T(8,128)(2,1)}, bf16[640,640]{1,0:T(8,128)(2,1)}, u32[]{:S(2)}, u32[]{:S(2)}) collective-permute-start(bf16[640,640]{1,0:T(8,128)(2,1)} %get-tuple-element.63.refs_10_), channel_id=1, source_target_pairs={{0,4},{4,0},{8,12},{12,8},{16,20},{20,16},{24,28},{28,24},{1,5},{5... | collective-permute-start | bytes 2457608 | tf_op jit(solution)/shard_map/ppermute | solution.py:42
  112.5 4.2 %collective-permute-start.19 = (bf16[640,640]{1,0:T(8,128)(2,1)}, bf16[640,640]{1,0:T(8,128)(2,1)}, u32[]{:S(2)}, u32[]{:S(2)}) collective-permute-start(bf16[640,640]{1,0:T(8,128)(2,1)} %get-tuple-element.64.refs_15_), channel_id=1, source_target_pairs={{0,4},{4,0},{8,12},{12,8},{16,20},{20,16},{24,28},{28,24},{1,5},{5... | collective-permute-start | bytes 2457608 | tf_op jit(solution)/shard_map/ppermute | solution.py:42
  113.0 5.4 %collective-permute-start.20 = (bf16[640,640]{1,0:T(8,128)(2,1)}, bf16[640,640]{1,0:T(8,128)(2,1)}, u32[]{:S(2)}, u32[]{:S(2)}) collective-permute-start(bf16[640,640]{1,0:T(8,128)(2,1)} %get-tuple-element.55.refs_16_), channel_id=1, source_target_pairs={{0,4},{4,0},{8,12},{12,8},{16,20},{20,16},{24,28},{28,24},{1,5},{5... | collective-permute-start | bytes 2457608 | tf_op jit(solution)/shard_map/ppermute | solution.py:42
  113.0 5.6 %collective-permute-start.21 = (bf16[640,640]{1,0:T(8,128)(2,1)}, bf16[640,640]{1,0:T(8,128)(2,1)}, u32[]{:S(2)}, u32[]{:S(2)}) collective-permute-start(bf16[640,640]{1,0:T(8,128)(2,1)} %get-tuple-element.65.refs_17_), channel_id=1, source_target_pairs={{0,4},{4,0},{8,12},{12,8},{16,20},{20,16},{24,28},{28,24},{1,5},{5... | collective-permute-start | bytes 2457608 | tf_op jit(solution)/shard_map/ppermute | solution.py:42
  113.5 6.3 %collective-permute-start.22 = (bf16[640,640]{1,0:T(8,128)(2,1)}, bf16[640,640]{1,0:T(8,128)(2,1)}, u32[]{:S(2)}, u32[]{:S(2)}) collective-permute-start(bf16[640,640]{1,0:T(8,128)(2,1)} %get-tuple-element.66.refs_18_), channel_id=1, source_target_pairs={{0,4},{4,0},{8,12},{12,8},{16,20},{20,16},{24,28},{28,24},{1,5},{5... | collective-permute-start | bytes 2457608 | tf_op jit(solution)/shard_map/ppermute | solution.py:42
  115.1 21.1 %collective-permute-start.24 = (bf16[640,640]{1,0:T(8,128)(2,1)}, bf16[640,640]{1,0:T(8,128)(2,1)}, u32[]{:S(2)}, u32[]{:S(2)}) collective-permute-start(bf16[640,640]{1,0:T(8,128)(2,1)} %collective-permute-done.13.refs_5_.refs_3_), channel_id=1, source_target_pairs={{0,16},{4,12},{8,24},{12,4},{16,0},{20,28},{24,8},{28,20},{1,17},{... | collective-permute-start | bytes 2457608 | tf_op jit(solution)/shard_map/ppermute | solution.py:42
  116.7 19.6 %collective-permute-start.23 = (bf16[512,640]{1,0:T(8,128)(2,1)}, bf16[512,640]{1,0:T(8,128)(2,1)}, u32[]{:S(2)}, u32[]{:S(2)}) collective-permute-start(bf16[512,640]{1,0:T(8,128)(2,1)} %get-tuple-element.67), channel_id=1, source_target_pairs={{0,1},{1,0},{2,3},{3,2},{4,5},{5,4},{6,7},{7,6},{8,9},{9,8},{10,11... | collective-permute-start | bytes 1966088 | tf_op jit(solution)/shard_map/ppermute | solution.py:38
  118.4 18.4 %collective-permute-start.25 = (bf16[640,640]{1,0:T(8,128)(2,1)}, bf16[640,640]{1,0:T(8,128)(2,1)}, u32[]{:S(2)}, u32[]{:S(2)}) collective-permute-start(bf16[640,640]{1,0:T(8,128)(2,1)} %broadcast_select_fusion.refs_2_), channel_id=1, source_target_pairs={{0,4},{4,0},{8,12},{12,8},{16,20},{20,16},{24,28},{28,24},{1,5},{5... | collective-permute-start | bytes 2457608 | tf_op jit(solution)/shard_map/ppermute | solution.py:42
  118.6 18.1 %collective-permute-start.26 = (bf16[640,640]{1,0:T(8,128)(2,1)}, bf16[640,640]{1,0:T(8,128)(2,1)}, u32[]{:S(2)}, u32[]{:S(2)}) collective-permute-start(bf16[640,640]{1,0:T(8,128)(2,1)} %collective-permute-done.13.refs_5_.refs_3_), channel_id=1, source_target_pairs={{0,4},{4,0},{8,12},{12,8},{16,20},{20,16},{24,28},{28,24},{1,5},{5... | collective-permute-start | bytes 2457608 | tf_op jit(solution)/shard_map/ppermute | solution.py:42
  119.8 17.0 %collective-permute-start.27 = (bf16[640,640]{1,0:T(8,128)(2,1)}, bf16[640,640]{1,0:T(8,128)(2,1)}, u32[]{:S(2)}, u32[]{:S(2)}) collective-permute-start(bf16[640,640]{1,0:T(8,128)(2,1)} %collective-permute-done.14.refs_6_.refs_4_), channel_id=1, source_target_pairs={{0,4},{4,0},{8,12},{12,8},{16,20},{20,16},{24,28},{28,24},{1,5},{5... | collective-permute-start | bytes 2457608 | tf_op jit(solution)/shard_map/ppermute | solution.py:42
  136.3 2.8 %collective-permute-start.28 = (bf16[640,640]{1,0:T(8,128)(2,1)}, bf16[640,640]{1,0:T(8,128)(2,1)}, u32[]{:S(2)}, u32[]{:S(2)}) collective-permute-start(bf16[640,640]{1,0:T(8,128)(2,1)} %get-tuple-element.70.refs_5_), channel_id=1, source_target_pairs={{0,4},{4,0},{8,12},{12,8},{16,20},{20,16},{24,28},{28,24},{1,5},{5... | collective-permute-start | bytes 2457608 | tf_op jit(solution)/shard_map/ppermute | solution.py:42
